TPU v7x, 256 devices: a whole 4x4x8 slice. The times are simulated.
256 devices in a mesh: video: 8 (over x, core), tm: 32 (over z, y).
Axes of the slice: x: 4, y: 4, z: 8, core: 2. Of those that a mesh axis runs over, the one named last changes fastest.
Arguments:
- queries: bfloat16 [8, 32, 4096, 256], P('video', 'tm'), may hold values from -720 to 720
- memory: bfloat16 [8, 32, 64, 4096], P('video', 'tm'), may hold values from -6 to 6
- tpos: float32 [7, 64], replicated, may hold values from -4 to 4
- w_k: bfloat16 [64, 256], replicated, may hold values from -0.75 to 0.75
- w_v: bfloat16 [64, 256], replicated, may hold values from -0.75 to 0.75
- w_o: bfloat16 [256, 256], replicated, may hold values from -0.375 to 0.375
- keyframes: int32 [8, 32, 64], P('video', 'tm'), may hold values from 0 to 2047, as said below
- cot: bfloat16 [8, 32, 4096, 256], P('video', 'tm'), may hold values from -6 to 6
Outputs:
- branch: bfloat16 [8, 32, 4096, 256], P('video', 'tm')
- grad_wo: float32 [256, 256], P('tm')
Inputs may be any that keep to these rules, and one draw needn't show every extreme that they name: `keyframes`: each frame's list is made of runs of 4 consecutive entries that lie in one frame; the runs of one list lie in different frames.
All inputs are finite; a program needn't handle non-finite values.
Results may differ from a plain program's by a relative error of at most 0.012.
The roundings to bfloat16 on the way count: a program that leaves them out, or rounds other values in their place, can miss the bound.
Values may be sent and summed in bfloat16 or wider, within the bound.
No kernel may reach another device: no remote copies, remote signals or barrier semaphores. Data moves between devices by JAX's collectives and lax.ppermute only.
A program may use at most 128 MiB of HBM per device.

v0:
```python
import math

import jax
import jax.numpy as jnp
from jax import lax
from jax.sharding import PartitionSpec as P

D = 256
MD = 64
TT = 64
TILES = 64
KF = 64
KSEL = 8
CLASSES = 8


tile_block = 8


def shifted(shard, axis, by):
    size = lax.axis_size(axis)
    pairs = [(i, i + by) for i in range(size) if 0 <= i + by < size]
    return lax.ppermute(shard, axis, pairs)


def project_pairs(tiles, position, w_pair):
    leading = tiles.shape[:-1]
    mixed = tiles.reshape(leading + (TT, MD)).astype(jnp.float32) + position
    mixed = mixed.astype(jnp.bfloat16)
    kv_pairs = jnp.dot(mixed.reshape(-1, MD), w_pair, preferred_element_type=jnp.float32)
    return kv_pairs.astype(jnp.bfloat16).reshape(leading + (TT, 2 * D))


def attend(query_tiles, recent_pairs, keyed_pairs, valid_back):
    tile_num = query_tiles.shape[0]
    recent = jnp.transpose(recent_pairs, (1, 0, 2, 3))
    kv_pairs = jnp.concatenate([recent, keyed_pairs], axis=1).reshape(
        tile_num, (6 + KSEL) * TT, 2 * D
    )
    key_part = kv_pairs[..., :D]
    value_part = kv_pairs[..., D:]
    scores = jnp.einsum("tqd,tkd->tqk", query_tiles, key_part, preferred_element_type=jnp.float32)
    scores = scores * (1.0 / math.sqrt(D))
    live_keys = jnp.concatenate([jnp.repeat(valid_back, TT), jnp.ones((KSEL * TT,), dtype=bool)])
    scores = jnp.where(live_keys[None, None, :], scores, -jnp.inf)
    row_max = jnp.max(scores, axis=-1, keepdims=True)
    weights = jnp.exp(scores - row_max)
    weights = (weights / jnp.sum(weights, axis=-1, keepdims=True)).astype(jnp.bfloat16)
    attended = jnp.einsum("tqk,tkd->tqd", weights, value_part, preferred_element_type=jnp.float32)
    return attended.astype(jnp.bfloat16)


def per_device(queries, memory, tpos, w_k, w_v, w_o, keyframes, cot):
    tile_count = memory.shape[2]
    row_width = memory.shape[3]
    own_tiles = memory[0, 0]
    device_index = lax.axis_index("tm")
    devices = lax.axis_size("tm")
    w_pair = jnp.concatenate([w_k, w_v], axis=1)
    recent = jnp.stack([shifted(own_tiles, "tm", offset) for offset in range(1, 7)])
    valid_back = device_index - jnp.arange(1, 7, dtype=jnp.int32) >= 0
    listed = keyframes[0, 0]
    owners = listed // TILES
    entries = jnp.arange(KF, dtype=jnp.int32)
    earlier = (owners[:, None] == owners[None, :]) & (entries[None, :] < entries[:, None])
    slot_rank = jnp.sum(earlier.astype(jnp.int32), axis=1)
    capacity = max(4, 2 * KF // devices)
    slot_ids = jnp.arange(capacity, dtype=jnp.int32)
    all_lists = lax.all_gather(listed[None], "tm", axis=0, tiled=True)
    all_owners = all_lists // TILES
    all_local = all_lists % TILES
    all_earlier = (all_owners[:, :, None] == all_owners[:, None, :]) & (
        entries[None, None, :] < entries[None, :, None]
    )
    all_rank = jnp.sum(all_earlier.astype(jnp.int32), axis=2)
    matches = (all_owners[:, :, None] == device_index) & (
        all_rank[:, :, None] == slot_ids[None, None, :]
    )
    chosen = jnp.sum(jnp.where(matches, all_local[:, :, None], 0), axis=1)
    filled = jnp.any(matches, axis=1)
    outgoing = jnp.where(filled[:, :, None], own_tiles[chosen], jnp.zeros((), jnp.bfloat16))
    incoming = lax.all_to_all(outgoing, "tm", split_axis=0, concat_axis=0, tiled=True)
    keyed_raw = incoming.reshape(-1, row_width)[owners * capacity + slot_rank]
    keyed_all = project_pairs(keyed_raw, tpos[6], w_pair)
    query_all = queries[0, 0].reshape(tile_count, TT, D)
    block_size = min(tile_block, tile_count)

    def one_block(block_index):
        first_tile = block_index * block_size
        query_tiles = lax.dynamic_slice_in_dim(query_all, first_tile, block_size, 0)
        recent_raw = lax.dynamic_slice_in_dim(recent, first_tile, block_size, 1)
        recent_pairs = project_pairs(recent_raw, tpos[:6][:, None, None, :], w_pair)
        tile_ids = first_tile + jnp.arange(block_size, dtype=jnp.int32)
        entry_ids = (tile_ids % CLASSES)[:, None] + CLASSES * jnp.arange(KSEL, dtype=jnp.int32)[
            None, :
        ]
        keyed_pairs = keyed_all[entry_ids]
        return attend(query_tiles, recent_pairs, keyed_pairs, valid_back)

    attended = lax.map(one_block, jnp.arange(tile_count // block_size, dtype=jnp.int32))
    attended = attended.reshape(tile_count * TT, D)
    branch = jnp.dot(attended, w_o, preferred_element_type=jnp.float32).astype(jnp.bfloat16)
    cot_rows = cot[0, 0]
    grad_local = lax.psum_scatter(
        lax.dot_general(
            attended, cot_rows, (((0,), (0,)), ((), ())), preferred_element_type=jnp.float32
        ),
        "tm",
        scatter_dimension=0,
        tiled=True,
    )
    summed = lax.psum(grad_local, "video")
    norm_scale = 1.0 / math.sqrt(lax.axis_size("video") * devices * tile_count * TT)
    return (branch.reshape(queries.shape), summed * norm_scale)


def solution(mesh):
    in_specs = (
        P("video", "tm", None, None),
        P("video", "tm", None, None),
        P(),
        P(),
        P(),
        P(),
        P("video", "tm", None),
        P("video", "tm", None, None),
    )
    out_specs = (P("video", "tm", None, None), P("tm", None))
    return jax.shard_map(
        per_device, mesh=mesh, in_specs=in_specs, out_specs=out_specs, check_vma=False
    )
```

profile of v0, /device:TPU:6, one launch (start us, length us, event | category | flops | bytes accessed | tf_op | source)
XLA Modules:
  0.0 677.2 jit_solution(11544194702233342380)
XLA Ops:
  7.2 4.4 collective-permute-start
  11.6 4.8 collective-permute-start.1
  16.4 4.6 collective-permute-start.2
  21.0 3.9 collective-permute-start.3
  24.9 4.0 collective-permute-start.4
  28.9 95.6 %all-gather = s32[32,1,64]{2,1,0:T(1,128)S(1)} all-gather(s32[1,1,64]{2,1,0:T(1,128)} %param.16), channel_id=2, replica_groups=mesh['video'=8,'tm'=32] {'tm'}, dimensions={0}, use_global_device_ids=true | all-gather | bytes 8448 | tf_op jit(solution)/shard_map/all_gather | solution.py:69
  125.9 3.3 gather_fusion.1
  133.4 7.3 %all-to-all-start = ((bf16[32,4,4096]{2,1,0:T(4,128)(2,1)}), bf16[32,4,4096]{2,1,0:T(4,128)(2,1)}, u32[]{:S(2)}, u32[]{:S(2)}) async-start(bf16[32,4,4096]{2,1,0:T(4,128)(2,1)} %broadcast_select_fusion), calls=%async_computation | async-start | bytes 2097152 | tf_op jit(solution)/shard_map/all_to_all | solution.py:82
  141.2 6.2 collective-permute-start.5
  156.8 8.9 %collective-permute-done.5 = bf16[64,4096]{1,0:T(8,128)(2,1)S(1)} collective-permute-done((bf16[64,4096]{1,0:T(8,128)(2,1)S(1)}, bf16[64,4096]{1,0:T(8,128)(2,1)S(1)}, u32[]{:S(2)}, u32[]{:S(2)}) %collective-permute-start.5) | collective-permute-done | bytes 524320 | tf_op jit(solution)/shard_map/ppermute | solution.py:23
  172.5 4.9 convolution_convert_fusion.1
  177.5 252.6 %while.13 = (s32[]{:T(128)}, bf16[8,8,64,256]{3,2,1,0:T(8,128)(2,1)}, s32[8]{0:T(128)S(1)}, bf16[64,64,256]{2,1,0:T(8,128)(2,1)}, bf16[6,64,4096]{2,1,0:T(8,128)...) while((s32[]{:T(128)}, ...), condition=%wide.region_7.8_spmd.clone, body=%wide.region_4.7_spmd.clone.sunk | while | flops 692194944 | bytes 43990744 | solution.py:100
  185.8 5.0 gather_fusion
  190.9 7.1 %pad_maximum_fusion.2 = bf16[8,14,64,512]{3,2,1,0:T(8,128)(2,1)} fusion(bf16[8,8,64,512]{3,2,1,0:T(8,128)(2,1)} %bitcast.93, bf16[8,6,64,512]{3,2,0,1:T(8,128)(2,1)} %bitcast.96), kind=kLoop, calls=%fused_computation.5.clone.1 | loop fusion | flops 14680064 | bytes 14680064 | tf_op jit(solution)/shard_map/while/body/eval_jaxpr/concatenate | solution.py:37
  198.0 4.6 fusion.65
  204.7 4.3 fusion.67
  217.4 5.0 gather_fusion
  222.4 7.1 %pad_maximum_fusion.2 = bf16[8,14,64,512]{3,2,1,0:T(8,128)(2,1)} fusion(bf16[8,8,64,512]{3,2,1,0:T(8,128)(2,1)} %bitcast.93, bf16[8,6,64,512]{3,2,0,1:T(8,128)(2,1)} %bitcast.96), kind=kLoop, calls=%fused_computation.5.clone.1 | loop fusion | flops 14680064 | bytes 14680064 | tf_op jit(solution)/shard_map/while/body/eval_jaxpr/concatenate | solution.py:37
  229.5 4.6 fusion.65
  236.3 4.3 fusion.67
  249.0 5.0 gather_fusion
  254.0 7.1 %pad_maximum_fusion.2 = bf16[8,14,64,512]{3,2,1,0:T(8,128)(2,1)} fusion(bf16[8,8,64,512]{3,2,1,0:T(8,128)(2,1)} %bitcast.93, bf16[8,6,64,512]{3,2,0,1:T(8,128)(2,1)} %bitcast.96), kind=kLoop, calls=%fused_computation.5.clone.1 | loop fusion | flops 14680064 | bytes 14680064 | tf_op jit(solution)/shard_map/while/body/eval_jaxpr/concatenate | solution.py:37
  261.1 4.6 fusion.65
  267.9 4.3 fusion.67
  280.6 5.0 gather_fusion
  285.6 7.1 %pad_maximum_fusion.2 = bf16[8,14,64,512]{3,2,1,0:T(8,128)(2,1)} fusion(bf16[8,8,64,512]{3,2,1,0:T(8,128)(2,1)} %bitcast.93, bf16[8,6,64,512]{3,2,0,1:T(8,128)(2,1)} %bitcast.96), kind=kLoop, calls=%fused_computation.5.clone.1 | loop fusion | flops 14680064 | bytes 14680064 | tf_op jit(solution)/shard_map/while/body/eval_jaxpr/concatenate | solution.py:37
  292.7 4.6 fusion.65
  299.5 4.3 fusion.67
  312.1 5.0 gather_fusion
  317.2 7.1 %pad_maximum_fusion.2 = bf16[8,14,64,512]{3,2,1,0:T(8,128)(2,1)} fusion(bf16[8,8,64,512]{3,2,1,0:T(8,128)(2,1)} %bitcast.93, bf16[8,6,64,512]{3,2,0,1:T(8,128)(2,1)} %bitcast.96), kind=kLoop, calls=%fused_computation.5.clone.1 | loop fusion | flops 14680064 | bytes 14680064 | tf_op jit(solution)/shard_map/while/body/eval_jaxpr/concatenate | solution.py:37
  324.3 4.6 fusion.65
  331.0 4.3 fusion.67
  343.7 5.0 gather_fusion
  348.7 7.1 %pad_maximum_fusion.2 = bf16[8,14,64,512]{3,2,1,0:T(8,128)(2,1)} fusion(bf16[8,8,64,512]{3,2,1,0:T(8,128)(2,1)} %bitcast.93, bf16[8,6,64,512]{3,2,0,1:T(8,128)(2,1)} %bitcast.96), kind=kLoop, calls=%fused_computation.5.clone.1 | loop fusion | flops 14680064 | bytes 14680064 | tf_op jit(solution)/shard_map/while/body/eval_jaxpr/concatenate | solution.py:37
  355.8 4.6 fusion.65
  362.6 4.3 fusion.67
  375.3 5.0 gather_fusion
  380.3 7.1 %pad_maximum_fusion.2 = bf16[8,14,64,512]{3,2,1,0:T(8,128)(2,1)} fusion(bf16[8,8,64,512]{3,2,1,0:T(8,128)(2,1)} %bitcast.93, bf16[8,6,64,512]{3,2,0,1:T(8,128)(2,1)} %bitcast.96), kind=kLoop, calls=%fused_computation.5.clone.1 | loop fusion | flops 14680064 | bytes 14680064 | tf_op jit(solution)/shard_map/while/body/eval_jaxpr/concatenate | solution.py:37
  387.4 4.6 fusion.65
  394.2 4.3 fusion.67
  406.8 5.0 gather_fusion
  411.9 7.1 %pad_maximum_fusion.2 = bf16[8,14,64,512]{3,2,1,0:T(8,128)(2,1)} fusion(bf16[8,8,64,512]{3,2,1,0:T(8,128)(2,1)} %bitcast.93, bf16[8,6,64,512]{3,2,0,1:T(8,128)(2,1)} %bitcast.96), kind=kLoop, calls=%fused_computation.5.clone.1 | loop fusion | flops 14680064 | bytes 14680064 | tf_op jit(solution)/shard_map/while/body/eval_jaxpr/concatenate | solution.py:37
  419.0 4.6 fusion.65
  425.7 4.3 fusion.67
  430.1 3.1 fusion.32
  433.2 3.6 fusion.31
  436.8 222.6 %reduce-scatter.2.cloned.1.call-done = f32[8,256]{1,0:T(8,128)} async-done(((f32[256,256]{1,0:T(8,128)}), f32[8,256]{1,0:T(8,128)}) %reduce-scatter.2.cloned.1.call-update) | async-done | bytes 8208 | tf_op jit(solution)/shard_map/reduce_scatter | solution.py:104
  659.4 10.4 %psum.7 = f32[8,256]{1,0:T(8,128)S(1)} all-reduce(f32[8,256]{1,0:T(8,128)} %reduce-scatter.2.cloned.1.call-done), channel_id=1, replica_groups=mesh['video'=8,'tm'=32] {'video'}, use_global_device_ids=true, to_apply=%region_9.10 | all-reduce | flops 2048 | bytes 16384 | tf_op jit(solution)/shard_map/psum | solution.py:112
  (166 shorter events, 101.8 us)
Async XLA Ops:
  7.2 422.9 %copy-start = (bf16[1,1,4096,256]{3,2,1,0:T(8,128)(2,1)S(1)}, bf16[1,1,4096,256]{3,2,1,0:T(8,128)(2,1)}, u32[]{:S(2)}) copy-start(bf16[1,1,4096,256]{3,2,1,0:T(8,128)(2,1)} %param.17) | copy-start | bytes 6291460
  7.2 134.0 %collective-permute-start = (bf16[64,4096]{1,0:T(8,128)(2,1)}, bf16[64,4096]{1,0:T(8,128)(2,1)}, u32[]{:S(2)}, u32[]{:S(2)}) collective-permute-start(bf16[64,4096]{1,0:T(8,128)(2,1)} %bitcast.98), channel_id=1, source_target_pairs={{0,1},{1,2},{2,3},{3,4},{4,5},{5,6},{6,7},{7,8},{8,9},{9,10},{10,1... | collective-permute-start | bytes 1572872 | tf_op jit(solution)/shard_map/ppermute | solution.py:23
  11.6 137.7 %collective-permute-start.1 = (bf16[64,4096]{1,0:T(8,128)(2,1)}, bf16[64,4096]{1,0:T(8,128)(2,1)}, u32[]{:S(2)}, u32[]{:S(2)}) collective-permute-start(bf16[64,4096]{1,0:T(8,128)(2,1)} %bitcast.99), channel_id=1, source_target_pairs={{0,2},{1,3},{2,4},{3,5},{4,6},{5,7},{6,8},{7,9},{8,10},{9,11},{10,... | collective-permute-start | bytes 1572872 | tf_op jit(solution)/shard_map/ppermute | solution.py:23
  16.4 134.7 %collective-permute-start.2 = (bf16[64,4096]{1,0:T(8,128)(2,1)}, bf16[64,4096]{1,0:T(8,128)(2,1)}, u32[]{:S(2)}, u32[]{:S(2)}) collective-permute-start(bf16[64,4096]{1,0:T(8,128)(2,1)} %bitcast.100), channel_id=1, source_target_pairs={{0,3},{1,4},{2,5},{3,6},{4,7},{5,8},{6,9},{7,10},{8,11},{9,12},{10... | collective-permute-start | bytes 1572872 | tf_op jit(solution)/shard_map/ppermute | solution.py:23
  21.0 132.0 %collective-permute-start.3 = (bf16[64,4096]{1,0:T(8,128)(2,1)}, bf16[64,4096]{1,0:T(8,128)(2,1)}, u32[]{:S(2)}, u32[]{:S(2)}) collective-permute-start(bf16[64,4096]{1,0:T(8,128)(2,1)} %bitcast.101), channel_id=1, source_target_pairs={{0,4},{1,5},{2,6},{3,7},{4,8},{5,9},{6,10},{7,11},{8,12},{9,13},{1... | collective-permute-start | bytes 1572872 | tf_op jit(solution)/shard_map/ppermute | solution.py:23
  24.9 130.0 %collective-permute-start.4 = (bf16[64,4096]{1,0:T(8,128)(2,1)}, bf16[64,4096]{1,0:T(8,128)(2,1)}, u32[]{:S(2)}, u32[]{:S(2)}) collective-permute-start(bf16[64,4096]{1,0:T(8,128)(2,1)} %bitcast.102), channel_id=1, source_target_pairs={{0,5},{1,6},{2,7},{3,8},{4,9},{5,10},{6,11},{7,12},{8,13},{9,14},{... | collective-permute-start | bytes 1572872 | tf_op jit(solution)/shard_map/ppermute | solution.py:23
  130.6 10.2 %copy-start.6 = (s32[1,1,64]{2,1,0:T(1,128)S(1)}, s32[1,1,64]{2,1,0:T(1,128)}, u32[]{:S(2)}) copy-start(s32[1,1,64]{2,1,0:T(1,128)} %param.16) | copy-start | bytes 772
  130.6 10.5 %copy-start.4 = (bf16[64,256]{1,0:T(8,128)(2,1)S(1)}, bf16[64,256]{1,0:T(8,128)(2,1)}, u32[]{:S(2)}) copy-start(bf16[64,256]{1,0:T(8,128)(2,1)} %param.13) | copy-start | bytes 98308
  130.6 10.5 %copy-start.5 = (bf16[64,256]{1,0:T(8,128)(2,1)S(1)}, bf16[64,256]{1,0:T(8,128)(2,1)}, u32[]{:S(2)}) copy-start(bf16[64,256]{1,0:T(8,128)(2,1)} %param.14) | copy-start | bytes 98308
  130.6 10.5 %copy-start.3 = (f32[7,64]{1,0:T(8,128)S(1)}, f32[7,64]{1,0:T(8,128)}, u32[]{:S(2)}) copy-start(f32[7,64]{1,0:T(8,128)} %param.12) | copy-start | bytes 5380
  130.6 10.5 %copy-start.1 = (bf16[1,1,64,4096]{3,2,1,0:T(8,128)(2,1)S(1)}, bf16[1,1,64,4096]{3,2,1,0:T(8,128)(2,1)}, u32[]{:S(2)}) copy-start(bf16[1,1,64,4096]{3,2,1,0:T(8,128)(2,1)} %param.11) | copy-start | bytes 1572868
  133.4 33.1 %all-to-all-start = ((bf16[32,4,4096]{2,1,0:T(4,128)(2,1)}), bf16[32,4,4096]{2,1,0:T(4,128)(2,1)}, u32[]{:S(2)}, u32[]{:S(2)}) async-start(bf16[32,4,4096]{2,1,0:T(4,128)(2,1)} %broadcast_select_fusion), calls=%async_computation | async-start | bytes 2097152 | tf_op jit(solution)/shard_map/all_to_all | solution.py:82
  140.8 518.6 %reduce-scatter.2.cloned.1.call-start = ((), (), s32[]{:S(2)}) async-start(), calls=%async_computation.2 | async-start | bytes 270336 | tf_op jit(solution)/shard_map/reduce_scatter | solution.py:104
  141.2 24.5 %collective-permute-start.5 = (bf16[64,4096]{1,0:T(8,128)(2,1)S(1)}, bf16[64,4096]{1,0:T(8,128)(2,1)S(1)}, u32[]{:S(2)}, u32[]{:S(2)}) collective-permute-start(bf16[64,4096]{1,0:T(8,128)(2,1)S(1)} %bitcast.104), channel_id=1, source_target_pairs={{0,6},{1,7},{2,8},{3,9},{4,10},{5,11},{6,12},{7,13},{8,14},{9,15},... | collective-permute-start | bytes 1572872 | tf_op jit(solution)/shard_map/ppermute | solution.py:23
  430.1 3.1 copy-start.2
Sparse Core Ops, SparseCore 0:
  433.3 226.0 reduce-scatter.1
where the time goes:
time: 683 us; the launch traced here: 677 us
  waiting for transfers between devices  231 us (34%)
  blocking collectives  106 us (16%)
  matrix products  104 us (15%)
  other arithmetic  98.9 us (14%)
  local copies, waits for them, and re-layouts  82.3 us (12%)
  starting transfers between devices  35.3 us (5%)
  between operations  14.3 us (2%)
    reduce_scatter x1, waiting for transfers between devices, per_device(): lax.psum_scatter(lax.dot_general(attended, cot_rows, (((0,), (0,)), ((),...  223 us
    all_gather x1, blocking collectives, per_device(): all_lists = lax.all_gather(listed[None], 'tm', axis=0, tiled=True)  95.6 us
    concatenate x8, other arithmetic, attend(): jnp.concatenate([recent, keyed_pairs], axis=1)  56.8 us
    gather x8, local copies, waits for them, and re-layouts, one_block(): keyed_pairs = keyed_all[entry_ids]  40.3 us
    dot_general x8, matrix products, attend(): jnp.einsum('tqd,tkd->tqk', query_tiles, key_part, preferred_element_type=...  36.5 us
    dot_general x8, matrix products, attend(): jnp.einsum('tqk,tkd->tqd', weights, value_part, preferred_element_type=jn...  34.5 us
    ppermute x6, starting transfers between devices, shifted(): return lax.ppermute(shard, axis, pairs)  27.9 us
    dot_general x9, matrix products, project_pairs(): jnp.dot(mixed.reshape(-1, MD), w_pair, preferred_element_type=jnp.float32)  25.9 us
  transfers between devices with their start and end apart: 8, of which 2 were waited for; matrix products, arithmetic and copies ran while one was open for 3% of the time, Pallas kernels for 0%

commit v1 on v0

v1 whole, which is shorter than its diff:
```python
import math

import jax
import jax.numpy as jnp
from jax import lax
from jax.experimental import pallas as pl
from jax.experimental.pallas import tpu as pltpu
from jax.sharding import PartitionSpec as P

D = 256
MD = 64
TT = 64
TILES = 64
KF = 64
KSEL = 8
CLASSES = 8
RUN = 4
RING = 4
PAIRS = TT // 2
LANES = 2 * MD
BLOCK = 8
LOW = -1e30
EXP2_SCALE = math.log2(math.e) / math.sqrt(D)
MIB = 1024 * 1024


def routed(shard, rows, target):
    pairs = []
    for row in range(rows):
        for place in range(RING):
            to = target(row, place)
            if to is not None and to[0] < rows:
                pairs.append((row * RING + place, to[0] * RING + to[1]))
    return lax.ppermute(shard, "tm", pairs)


def project(tiles, position, w_pair):
    mixed = (tiles.astype(jnp.float32) + position).astype(jnp.bfloat16)
    pairs = jnp.dot(mixed.reshape(-1, LANES), w_pair, preferred_element_type=jnp.float32)
    return pairs.astype(jnp.bfloat16)


def pick_kernel(asked, own, outgoing):
    def one(dest, carry):
        for slot in range(RUN):
            outgoing[dest * RUN + slot] = own[asked[dest, slot]]
        return carry

    lax.fori_loop(0, asked.shape[0], one, 0)


def recent_kernel(place, q, b1, c1, b2, c3, b3, c2, a, d2, d1, z2, tpos, w_pair, acc, stat, keys, values):
    frame = place[0]
    y = frame % RING
    f32 = lambda ref: ref[...].astype(jnp.float32)
    picked = (
        lambda: jnp.where(y == 0, f32(c1), f32(b1)),
        lambda: jnp.where(y < 2, f32(c3), f32(b2)),
        lambda: jnp.where(y == 3, f32(b3), f32(c2)),
        lambda: f32(a),
        lambda: jnp.where(y == 0, f32(d2), f32(c1)),
        lambda: jnp.where(y < 2, f32(d1), f32(z2)),
    )
    for j in range(6):
        pairs = project(picked[j](), tpos[j : j + 1, :], w_pair[...])
        for part, ref in enumerate((keys, values)):
            for odd in range(2):
                first = (2 * part + odd) * D
                ref[:, odd * 6 + j] = pairs[:, first : first + D].reshape(BLOCK, PAIRS, D)
    column = lax.broadcasted_iota(jnp.int32, (1, 6 * TT), 1)
    offset = (column % (6 * PAIRS)) // PAIRS + 1
    bias = jnp.where(offset <= frame, 0.0, LOW).astype(jnp.float32)
    for t in range(BLOCK):
        scores = lax.dot_general(
            q[t], keys[t].reshape(6 * TT, D), (((1,), (1,)), ((), ())), preferred_element_type=jnp.float32
        )
        scores = scores * EXP2_SCALE + bias
        top = jnp.max(scores, axis=-1, keepdims=True)
        weights = jnp.exp2(scores - top)
        stat[t, :, 0:1] = top
        stat[t, :, 1:2] = jnp.sum(weights, axis=-1, keepdims=True)
        acc[t] = jnp.dot(
            weights.astype(jnp.bfloat16), values[t].reshape(6 * TT, D), preferred_element_type=jnp.float32
        )


def keyed_kernel(owners, q, incoming, tpos, w_pair, acc, stat, w_o, cot, branch, grad, tiles):
    c = pl.program_id(0)
    for s in range(KSEL):
        tiles[s] = incoming[owners[2 * s + c // RUN] * RUN + c % RUN]
    pairs = project(tiles[...], tpos[6:7, :], w_pair[...])
    keys = jnp.concatenate([pairs[:, :D], pairs[:, D : 2 * D]], axis=0)
    values = jnp.concatenate([pairs[:, 2 * D : 3 * D], pairs[:, 3 * D :]], axis=0)
    rows = q.shape[0] * TT
    scores = lax.dot_general(
        q[...].reshape(rows, D), keys, (((1,), (1,)), ((), ())), preferred_element_type=jnp.float32
    )
    scores = scores * EXP2_SCALE
    top_near = stat[...].reshape(rows, 2)[:, 0:1]
    sum_near = stat[...].reshape(rows, 2)[:, 1:2]
    top = jnp.maximum(jnp.max(scores, axis=-1, keepdims=True), top_near)
    weights = jnp.exp2(scores - top)
    near = jnp.exp2(top_near - top)
    total = jnp.sum(weights, axis=-1, keepdims=True) + sum_near * near
    summed = jnp.dot(weights.astype(jnp.bfloat16), values, preferred_element_type=jnp.float32)
    summed = (summed + acc[...].reshape(rows, D) * near) / total
    attended = summed.astype(jnp.bfloat16)
    out = jnp.dot(attended, w_o[...], preferred_element_type=jnp.float32).astype(jnp.bfloat16)
    branch[...] = out.reshape(branch.shape)
    term = lax.dot_general(
        attended, cot[...].reshape(rows, D), (((0,), (0,)), ((), ())), preferred_element_type=jnp.float32
    )

    @pl.when(c == 0)
    def _():
        grad[...] = term

    @pl.when(c > 0)
    def _():
        grad[...] += term


def per_device(queries, memory, tpos, w_k, w_v, w_o, keyframes, cot):
    device_index = lax.axis_index("tm")
    devices = lax.axis_size("tm")
    rows = devices // RING
    groups = TILES // CLASSES
    own = memory[0, 0].reshape(TILES, PAIRS, LANES)

    run_ids = keyframes[0, 0].reshape(KF // RUN, RUN)
    owners = run_ids[:, 0] // TILES
    hits = owners[None, :, None] == jnp.arange(devices, dtype=jnp.int32)[:, None, None]
    asks = jnp.sum(jnp.where(hits, run_ids[None] % TILES, 0), axis=1)
    asked = lax.all_to_all(asks, "tm", split_axis=0, concat_axis=0, tiled=True)

    a = routed(own, rows, lambda z, y: (z + 1, y))
    b1 = routed(own, rows, lambda z, y: (z, y + 1) if y < 3 else None)
    b2 = routed(own, rows, lambda z, y: (z, y + 2) if y < 2 else None)
    b3 = routed(own, rows, lambda z, y: (z, 3) if y == 0 else None)
    c1 = routed(a, rows, lambda z, y: (z, (y + 1) % RING))
    c2 = routed(a, rows, lambda z, y: (z, y - 1) if y > 0 else None)
    c3 = routed(a, rows, lambda z, y: (z, y - 2) if y > 1 else None)
    z2 = routed(b2, rows, lambda z, y: (z + 1, y) if y > 1 else None)
    d1 = routed(c3, rows, lambda z, y: (z + 1, y) if y < 2 else None)
    d2 = routed(c1, rows, lambda z, y: (z + 1, y) if y == 0 else None)

    outgoing = pl.pallas_call(
        pick_kernel,
        out_shape=jax.ShapeDtypeStruct((devices * RUN, PAIRS, LANES), jnp.bfloat16),
        in_specs=[pl.BlockSpec(memory_space=pltpu.SMEM), pl.BlockSpec(memory_space=pltpu.VMEM)],
        out_specs=pl.BlockSpec(memory_space=pltpu.VMEM),
        compiler_params=pltpu.CompilerParams(vmem_limit_bytes=8 * MIB),
        name="pick",
    )(asked, own)
    incoming = lax.all_to_all(outgoing, "tm", split_axis=0, concat_axis=0, tiled=True)

    zero = jnp.zeros_like(w_k)
    w_pair = jnp.concatenate(
        [
            jnp.concatenate([w_k, zero, w_v, zero], axis=1),
            jnp.concatenate([zero, w_k, zero, w_v], axis=1),
        ],
        axis=0,
    )
    tpos_pair = jnp.concatenate([tpos, tpos], axis=1)
    q_tiles = queries[0, 0].reshape(TILES, TT, D)
    whole = lambda *shape: pl.BlockSpec(shape, lambda i, *_: (0,) * len(shape))
    tile_block = pl.BlockSpec((BLOCK, PAIRS, LANES), lambda i, *_: (i, 0, 0))
    row_block = pl.BlockSpec((BLOCK, TT, D), lambda i, *_: (i, 0, 0))
    acc, stat = pl.pallas_call(
        recent_kernel,
        grid_spec=pltpu.PrefetchScalarGridSpec(
            num_scalar_prefetch=1,
            grid=(TILES // BLOCK,),
            in_specs=[row_block] + [tile_block] * 10 + [whole(7, LANES), whole(LANES, 4 * D)],
            out_specs=[row_block, pl.BlockSpec((BLOCK, TT, 2), lambda i, *_: (i, 0, 0))],
            scratch_shapes=[pltpu.VMEM((BLOCK, 12, PAIRS, D), jnp.bfloat16)] * 2,
        ),
        out_shape=[
            jax.ShapeDtypeStruct((TILES, TT, D), jnp.float32),
            jax.ShapeDtypeStruct((TILES, TT, 2), jnp.float32),
        ],
        compiler_params=pltpu.CompilerParams(vmem_limit_bytes=40 * MIB),
        name="recent",
    )(device_index[None], q_tiles, b1, c1, b2, c3, b3, c2, a, d2, d1, z2, tpos_pair, w_pair)

    by_class = lambda x: x.reshape((groups, CLASSES) + x.shape[1:])
    class_block = lambda width: pl.BlockSpec((groups, 1, TT, width), lambda i, *_: (0, i, 0, 0))
    branch, grad = pl.pallas_call(
        keyed_kernel,
        grid_spec=pltpu.PrefetchScalarGridSpec(
            num_scalar_prefetch=1,
            grid=(CLASSES,),
            in_specs=[
                class_block(D),
                whole(devices * RUN, PAIRS, LANES),
                whole(7, LANES),
                whole(LANES, 4 * D),
                class_block(D),
                class_block(2),
                whole(D, D),
                class_block(D),
            ],
            out_specs=[class_block(D), whole(D, D)],
            scratch_shapes=[pltpu.VMEM((KSEL, PAIRS, LANES), jnp.bfloat16)],
        ),
        out_shape=[
            jax.ShapeDtypeStruct((groups, CLASSES, TT, D), jnp.bfloat16),
            jax.ShapeDtypeStruct((D, D), jnp.float32),
        ],
        compiler_params=pltpu.CompilerParams(vmem_limit_bytes=40 * MIB),
        name="keyed",
    )(
        owners,
        by_class(q_tiles),
        incoming,
        tpos_pair,
        w_pair,
        by_class(acc),
        by_class(stat),
        w_o,
        by_class(cot[0, 0].reshape(TILES, TT, D)),
    )

    parts = lax.all_to_all(
        grad.reshape(devices, D // devices, D), "tm", split_axis=0, concat_axis=0, tiled=True
    )
    videos = lax.axis_size("video")
    summed = jnp.sum(parts, axis=0) * (1.0 / math.sqrt(videos * devices * TILES * TT))
    step = 1
    while step < videos:
        summed = summed + lax.ppermute(summed, "video", [(i, i ^ step) for i in range(videos)])
        step *= 2
    return branch.reshape(queries.shape), summed


def solution(mesh):
    in_specs = (
        P("video", "tm", None, None),
        P("video", "tm", None, None),
        P(),
        P(),
        P(),
        P(),
        P("video", "tm", None),
        P("video", "tm", None, None),
    )
    out_specs = (P("video", "tm", None, None), P("tm", None))
    return jax.shard_map(
        per_device, mesh=mesh, in_specs=in_specs, out_specs=out_specs, check_vma=False
    )
```

time: 683 us -> 198 us (0.29)
  waiting for transfers between devices: 231 us -> 50.7 us
  matrix products: 104 us -> 0 us
  other arithmetic: 98.9 us -> 2.25 us
  blocking collectives: 106 us -> 21.7 us
  local copies, waits for them, and re-layouts: 82.3 us -> 13.1 us
  Pallas kernels: 0 us -> 53.9 us
  starting transfers between devices: 35.3 us -> 54.5 us
  between operations: 14.3 us -> 0.85 us
    reduce_scatter x1 -> x0, waiting for transfers between devices: 223 us -> none  [per_device(): lax.psum_scatter(lax.dot_general(attended, cot_rows, (((0,), (0,)), ((),...]
    dot_general x27 -> x0, matrix products: 104 us -> none  [the longest x8 36.5 us: attend(): jnp.einsum('tqd,tkd->tqk', query_tiles, key_part, preferred_element_type=...]
    all_gather x1 -> x0, blocking collectives: 95.6 us -> none  [per_device(): all_lists = lax.all_gather(listed[None], 'tm', axis=0, tiled=True)]
    concatenate x8 -> x2, other arithmetic: 56.8 us -> 0.09 us  [the longest x1 0.07 us: per_device(): tpos_pair = jnp.concatenate([tpos, tpos], axis=1)]
    pallas_call x0 -> x3, Pallas kernels: none -> 53.9 us  [the longest x1 26.2 us: per_device(): pl.pallas_call(keyed_kernel, grid_spec=pltpu.PrefetchScalarGridSpec(num_s...]
    gather x11 -> x0, local copies, waits for them, and re-layouts: 46.5 us -> none  [the longest x8 40.3 us: one_block(): keyed_pairs = keyed_all[entry_ids]]
    ppermute x6 -> x13, waiting for transfers between devices: 8.9 us -> 42.1 us  [the longest x10 34.4 us: routed(): return lax.ppermute(shard, 'tm', pairs)]
    all_to_all x0 -> x1, blocking collectives: none -> 21.7 us  [per_device(): lax.all_to_all(grad.reshape(devices, D // devices, D), 'tm', split_axis=0...]
  transfers between devices with their start and end apart: 8 -> 15, of which waited for: 2 -> 8; matrix products, arithmetic and copies ran while one was open for 3% -> 1% of each run, Pallas kernels for 0% -> 13%
where the time goes in v1:
time: 198 us; the launch traced here: 197 us
  starting transfers between devices  54.5 us (28%)
  Pallas kernels  53.9 us (27%)
  waiting for transfers between devices  50.7 us (26%)
  blocking collectives  21.7 us (11%)
  local copies, waits for them, and re-layouts  13.1 us (7%)
  other arithmetic  2.25 us (1%)
    ppermute x10, starting transfers between devices, routed(): return lax.ppermute(shard, 'tm', pairs)  36.8 us
    ppermute x10, waiting for transfers between devices, routed(): return lax.ppermute(shard, 'tm', pairs)  34.4 us
    pallas_call x1, Pallas kernels, per_device(): pl.pallas_call(keyed_kernel, grid_spec=pltpu.PrefetchScalarGridSpec(num_s...  26.2 us
    pallas_call x1, Pallas kernels, per_device(): pl.pallas_call(recent_kernel, grid_spec=pltpu.PrefetchScalarGridSpec(num_...  25.6 us
    all_to_all x1, blocking collectives, per_device(): lax.all_to_all(grad.reshape(devices, D // devices, D), 'tm', split_axis=0...  21.7 us
    unnamed x28, local copies, waits for them, and re-layouts  12.2 us
    all_to_all x1, starting transfers between devices, per_device(): asked = lax.all_to_all(asks, 'tm', split_axis=0, concat_axis=0, tiled=True)  11.5 us
    all_to_all x1, waiting for transfers between devices, per_device(): asked = lax.all_to_all(asks, 'tm', split_axis=0, concat_axis=0, tiled=True)  8.54 us
  transfers between devices with their start and end apart: 15, of which 8 were waited for; matrix products, arithmetic and copies ran while one was open for 1% of the time, Pallas kernels for 13%

profile of v1, /device:TPU:6, one launch (start us, length us, event | category | flops | bytes accessed | tf_op | source)
XLA Modules:
  0.0 197.1 jit_solution(7568398325385098460)
XLA Ops:
  0.6 0.5 broadcast.87
  1.1 1.3 reduce.5
  2.5 0.1 reshape_squeeze.9
  2.5 0.1 slice_reduce_fusion
  2.7 0.1 iota_compare_fusion
  2.8 0.1 copy.15
  2.8 0.1 select_reduce_fusion
  2.9 0.7 copy.16
  3.6 11.5 %all-to-all-start = ((s32[32,1,4]{2,1,0:T(1,128)}), s32[32,1,4]{2,1,0:T(1,128)S(1)}, u32[]{:S(2)}, u32[]{:S(2)}) async-start(s32[32,1,4]{2,1,0:T(1,128)} %copy.16), calls=%async_computation | async-start | bytes 32768 | tf_op jit(solution)/shard_map/all_to_all | solution.py:134
  15.1 1.1 copy.20
  16.3 0.0 copy-start.3
  16.3 0.0 copy-start.12
  16.3 0.0 copy-start.10
  16.3 8.5 %all-to-all-done = s32[32,1,4]{2,1,0:T(1,128)S(1)} async-done(((s32[32,1,4]{2,1,0:T(1,128)}), s32[32,1,4]{2,1,0:T(1,128)S(1)}, u32[]{:S(2)}, u32[]{:S(2)}) %all-to-all-start) | async-done | bytes 544 | tf_op jit(solution)/shard_map/all_to_all | solution.py:134
  24.9 2.1 %pick.1 = bf16[128,32,128]{2,1,0:T(8,128)(2,1)} custom-call(s32[32,4]{1,0:T(8,128)S(1)} %bitcast.25, bf16[64,32,128]{2,1,0:T(8,128)(2,1)S(1)} %bitcast.17), custom_call_target="tpu_custom_call" | custom-call | tf_op jit(solution)/shard_map/pick/pallas_call | solution.py:147
  27.0 3.9 %all-to-all-start.1 = ((bf16[128,32,128]{2,1,0:T(8,128)(2,1)}), bf16[128,32,128]{2,1,0:T(8,128)(2,1)S(1)}, u32[]{:S(2)}, u32[]{:S(2)}) async-start(bf16[128,32,128]{2,1,0:T(8,128)(2,1)} %pick.1), calls=%async_computation.1 | async-start | bytes 2097152 | tf_op jit(solution)/shard_map/all_to_all | solution.py:155
  30.9 4.4 %collective-permute-start.1 = (bf16[64,32,128]{2,1,0:T(8,128)(2,1)}, bf16[64,32,128]{2,1,0:T(8,128)(2,1)}, u32[]{:S(2)}, u32[]{:S(2)}) collective-permute-start(bf16[64,32,128]{2,1,0:T(8,128)(2,1)} %bitcast.18), channel_id=1, source_target_pairs={{0,4},{1,5},{2,6},{3,7},{4,8},{5,9},{6,10},{7,11},{8,12},{9,13},{1... | collective-permute-start | bytes 1572872 | tf_op jit(solution)/shard_map/ppermute | solution.py:34
  35.3 5.7 %collective-permute-start.3 = (bf16[64,32,128]{2,1,0:T(8,128)(2,1)}, bf16[64,32,128]{2,1,0:T(8,128)(2,1)}, u32[]{:S(2)}, u32[]{:S(2)}) collective-permute-start(bf16[64,32,128]{2,1,0:T(8,128)(2,1)} %bitcast.19), channel_id=1, source_target_pairs={{0,2},{1,3},{4,6},{5,7},{8,10},{9,11},{12,14},{13,15},{16,18},{17,... | collective-permute-start | bytes 1572872 | tf_op jit(solution)/shard_map/ppermute | solution.py:34
  41.0 2.5 %collective-permute-start = (bf16[64,32,128]{2,1,0:T(8,128)(2,1)}, bf16[64,32,128]{2,1,0:T(8,128)(2,1)S(1)}, u32[]{:S(2)}, u32[]{:S(2)}) collective-permute-start(bf16[64,32,128]{2,1,0:T(8,128)(2,1)} %bitcast.20), channel_id=1, source_target_pairs={{0,1},{1,2},{2,3},{4,5},{5,6},{6,7},{8,9},{9,10},{10,11},{12,13},{... | collective-permute-start | bytes 1572872 | tf_op jit(solution)/shard_map/ppermute | solution.py:34
  43.5 19.8 %collective-permute-done.1.a = bf16[64,32,128]{2,1,0:T(8,128)(2,1)} collective-permute-done((bf16[64,32,128]{2,1,0:T(8,128)(2,1)}, bf16[64,32,128]{2,1,0:T(8,128)(2,1)}, u32[]{:S(2)}, u32[]{:S(2)}) %collective-permute-start.1) | collective-permute-done | bytes 524320 | tf_op jit(solution)/shard_map/ppermute | solution.py:34
  63.3 1.5 collective-permute-start.2
  64.9 1.3 collective-permute-start.4
  66.1 8.3 %collective-permute-start.5 = (bf16[64,32,128]{2,1,0:T(8,128)(2,1)}, bf16[64,32,128]{2,1,0:T(8,128)(2,1)}, u32[]{:S(2)}, u32[]{:S(2)}) collective-permute-start(bf16[64,32,128]{2,1,0:T(8,128)(2,1)} %bitcast.21), channel_id=1, source_target_pairs={{0,3},{4,7},{8,11},{12,15},{16,19},{20,23},{24,27},{28,31},{32,35}... | collective-permute-start | bytes 1572872 | tf_op jit(solution)/shard_map/ppermute | solution.py:34
  74.4 1.3 collective-permute-start.6
  75.7 0.8 copy-done.7
  76.5 1.5 collective-permute-start.9
  78.0 1.0 collective-permute-done.2.c1
  79.0 4.5 %collective-permute-start.7 = (bf16[64,32,128]{2,1,0:T(8,128)(2,1)}, bf16[64,32,128]{2,1,0:T(8,128)(2,1)}, u32[]{:S(2)}, u32[]{:S(2)}) collective-permute-start(bf16[64,32,128]{2,1,0:T(8,128)(2,1)} %collective-permute-done.2.c1), channel_id=1, source_target_pairs={{0,4},{4,8},{8,12},{12,16},{16,20},{20,24},{24,28},{32,36},{36,40}... | collective-permute-start | bytes 1572872 | tf_op jit(solution)/shard_map/ppermute | solution.py:34
  83.5 5.0 %collective-permute-done.4.c3 = bf16[64,32,128]{2,1,0:T(8,128)(2,1)} collective-permute-done((bf16[64,32,128]{2,1,0:T(8,128)(2,1)}, bf16[64,32,128]{2,1,0:T(8,128)(2,1)}, u32[]{:S(2)}, u32[]{:S(2)}) %collective-permute-start.4) | collective-permute-done | bytes 524320 | tf_op jit(solution)/shard_map/ppermute | solution.py:34
  88.5 5.8 %collective-permute-start.8 = (bf16[64,32,128]{2,1,0:T(8,128)(2,1)}, bf16[64,32,128]{2,1,0:T(8,128)(2,1)}, u32[]{:S(2)}, u32[]{:S(2)}) collective-permute-start(bf16[64,32,128]{2,1,0:T(8,128)(2,1)} %collective-permute-done.4.c3), channel_id=1, source_target_pairs={{0,4},{1,5},{4,8},{5,9},{8,12},{9,13},{12,16},{13,17},{16,20},{17,... | collective-permute-start | bytes 1572872 | tf_op jit(solution)/shard_map/ppermute | solution.py:34
  94.4 0.1 pad_maximum_fusion.tpos
  94.5 8.5 %collective-permute-done.8.d1 = bf16[64,32,128]{2,1,0:T(8,128)(2,1)} collective-permute-done((bf16[64,32,128]{2,1,0:T(8,128)(2,1)}, bf16[64,32,128]{2,1,0:T(8,128)(2,1)}, u32[]{:S(2)}, u32[]{:S(2)}) %collective-permute-start.8) | collective-permute-done | bytes 524320 | tf_op jit(solution)/shard_map/ppermute | solution.py:34
  103.1 1.0 copy-done.8
  104.1 25.6 %recent.1 = (f32[64,64,256]{2,1,0:T(8,128)S(1)}, f32[64,64,2]{2,1,0:T(8,128)S(1)}) custom-call(s32[1]{0:T(128)} %bitcast.3.place, bf16[64,64,256]{2,1,0:T(8,128)(2,1)S(1)} %bitcast.14, bf16[64,32,128]{2,1,0:T(8,128)(2,1)S(1)} %copy-done.8, bf16[64,32,128]{2,1,0:T(8,128)(2,1)} %collective-permute-done.2.c1, bf16[64,32,128]{2,1,0:T(8,128)(2,1)} %collective-permute-done.3.b2, ...), custom_call_target="tpu_custom_call" | custom-call | tf_op jit(solution)/shard_map/recent/pallas_call | solution.py:170
  129.8 1.9 copy-done.1
  131.7 1.3 copy-done.5
  133.0 2.2 %copy-done.2 = f32[64,64,256]{2,1,0:T(8,128)S(1)} copy-done((f32[64,64,256]{2,1,0:T(8,128)S(1)}, f32[64,64,256]{2,1,0:T(8,128)}, u32[]{:S(2)}) %copy-start.2) | copy-done | bytes 4194328
  135.2 1.6 copy-done.4
  136.8 1.6 copy-done.6
  138.4 26.2 %keyed.1 = (bf16[8,8,64,256]{3,2,1,0:T(8,128)(2,1)}, f32[256,256]{1,0:T(8,128)S(1)}) custom-call(s32[16]{0:T(128)S(1)} %and_select_fusion.owners, bf16[8,8,64,256]{3,2,1,0:T(8,128)(2,1)S(1)} %bitcast.15, bf16[128,32,128]{2,1,0:T(8,128)(2,1)S(1)} %all-to-all-done.1.incoming, f32[7,128]{1,0:T(8,128)S(1)} %pad_maximum_fusion.tpos, ...), custom_call_target="tpu_custom_call" | custom-call | tf_op jit(solution)/shard_map/keyed/pallas_call | solution.py:189
  164.6 21.7 %all_to_all.21 = f32[32,8,256]{2,1,0:T(8,128)S(1)} all-to-all(f32[32,8,256]{2,1,0:T(8,128)S(1)} %bitcast.24), channel_id=1, replica_groups=mesh['video'=8,'tm'=32] {'tm'}, dimensions={0} | all-to-all | bytes 524288 | tf_op jit(solution)/shard_map/all_to_all | solution.py:225
  186.4 0.1 collective-permute-start.10
  186.5 1.2 collective-permute-done.10
  187.6 0.8 collective-permute-start.11
  188.5 2.8 %collective-permute-done.11 = f32[8,256]{1,0:T(8,128)S(1)} collective-permute-done((f32[8,256]{1,0:T(8,128)S(1)}, f32[8,256]{1,0:T(8,128)S(1)}, u32[]{:S(2)}, u32[]{:S(2)}) %collective-permute-start.11) | collective-permute-done | bytes 8224 | tf_op jit(solution)/shard_map/ppermute | solution.py:232
  191.3 1.4 collective-permute-start.12
  192.7 3.7 %collective-permute-done.12 = f32[8,256]{1,0:T(8,128)S(1)} collective-permute-done((f32[8,256]{1,0:T(8,128)S(1)}, f32[8,256]{1,0:T(8,128)S(1)}, u32[]{:S(2)}, u32[]{:S(2)}) %collective-permute-start.12) | collective-permute-done | bytes 8224 | tf_op jit(solution)/shard_map/ppermute | solution.py:232
  196.5 0.6 add.28
  (31 shorter events, 0.1 us)
Async XLA Ops:
  3.6 21.2 %all-to-all-start = ((s32[32,1,4]{2,1,0:T(1,128)}), s32[32,1,4]{2,1,0:T(1,128)S(1)}, u32[]{:S(2)}, u32[]{:S(2)}) async-start(s32[32,1,4]{2,1,0:T(1,128)} %copy.16), calls=%async_computation | async-start | bytes 32768 | tf_op jit(solution)/shard_map/all_to_all | solution.py:134
  16.3 10.7 %copy-start.3 = (bf16[8,8,32,128]{3,2,1,0:T(8,128)(2,1)}, bf16[8,8,32,128]{3,2,1,0:T(8,128)(2,1)S(1)}, u32[]{:S(2)}) copy-start(bf16[8,8,32,128]{3,2,1,0:T(8,128)(2,1)S(1)} %copy.20) | copy-start | bytes 1572868
  16.3 78.1 %copy-start.12 = (f32[7,64]{1,0:T(8,128)S(1)}, f32[7,64]{1,0:T(8,128)}, u32[]{:S(2)}) copy-start(f32[7,64]{1,0:T(8,128)} %param.10) | copy-start | bytes 5380
  16.3 78.2 %copy-start.10 = (bf16[64,256]{1,0:T(8,128)(2,1)S(1)}, bf16[64,256]{1,0:T(8,128)(2,1)}, u32[]{:S(2)}) copy-start(bf16[64,256]{1,0:T(8,128)(2,1)} %param.12) | copy-start | bytes 98308
  16.3 78.2 %copy-start.11 = (bf16[64,256]{1,0:T(8,128)(2,1)S(1)}, bf16[64,256]{1,0:T(8,128)(2,1)}, u32[]{:S(2)}) copy-start(bf16[64,256]{1,0:T(8,128)(2,1)} %param.11) | copy-start | bytes 98308
  16.3 86.8 %copy-start = (bf16[1,1,4096,256]{3,2,1,0:T(8,128)(2,1)S(1)}, bf16[1,1,4096,256]{3,2,1,0:T(8,128)(2,1)}, u32[]{:S(2)}) copy-start(bf16[1,1,4096,256]{3,2,1,0:T(8,128)(2,1)} %param.8) | copy-start | bytes 6291460
  27.0 106.0 %all-to-all-start.1 = ((bf16[128,32,128]{2,1,0:T(8,128)(2,1)}), bf16[128,32,128]{2,1,0:T(8,128)(2,1)S(1)}, u32[]{:S(2)}, u32[]{:S(2)}) async-start(bf16[128,32,128]{2,1,0:T(8,128)(2,1)} %pick.1), calls=%async_computation.1 | async-start | bytes 2097152 | tf_op jit(solution)/shard_map/all_to_all | solution.py:155
  30.9 32.4 %collective-permute-start.1 = (bf16[64,32,128]{2,1,0:T(8,128)(2,1)}, bf16[64,32,128]{2,1,0:T(8,128)(2,1)}, u32[]{:S(2)}, u32[]{:S(2)}) collective-permute-start(bf16[64,32,128]{2,1,0:T(8,128)(2,1)} %bitcast.18), channel_id=1, source_target_pairs={{0,4},{1,5},{2,6},{3,7},{4,8},{5,9},{6,10},{7,11},{8,12},{9,13},{1... | collective-permute-start | bytes 1572872 | tf_op jit(solution)/shard_map/ppermute | solution.py:34
  35.3 39.1 %collective-permute-start.3 = (bf16[64,32,128]{2,1,0:T(8,128)(2,1)}, bf16[64,32,128]{2,1,0:T(8,128)(2,1)}, u32[]{:S(2)}, u32[]{:S(2)}) collective-permute-start(bf16[64,32,128]{2,1,0:T(8,128)(2,1)} %bitcast.19), channel_id=1, source_target_pairs={{0,2},{1,3},{4,6},{5,7},{8,10},{9,11},{12,14},{13,15},{16,18},{17,... | collective-permute-start | bytes 1572872 | tf_op jit(solution)/shard_map/ppermute | solution.py:34
  41.0 34.7 %collective-permute-start = (bf16[64,32,128]{2,1,0:T(8,128)(2,1)}, bf16[64,32,128]{2,1,0:T(8,128)(2,1)S(1)}, u32[]{:S(2)}, u32[]{:S(2)}) collective-permute-start(bf16[64,32,128]{2,1,0:T(8,128)(2,1)} %bitcast.20), channel_id=1, source_target_pairs={{0,1},{1,2},{2,3},{4,5},{5,6},{6,7},{8,9},{9,10},{10,11},{12,13},{... | collective-permute-start | bytes 1572872 | tf_op jit(solution)/shard_map/ppermute | solution.py:34
  63.3 15.6 %collective-permute-start.2 = (bf16[64,32,128]{2,1,0:T(8,128)(2,1)}, bf16[64,32,128]{2,1,0:T(8,128)(2,1)}, u32[]{:S(2)}, u32[]{:S(2)}) collective-permute-start(bf16[64,32,128]{2,1,0:T(8,128)(2,1)} %collective-permute-done.1.a), channel_id=1, source_target_pairs={{0,1},{1,2},{2,3},{3,0},{4,5},{5,6},{6,7},{7,4},{8,9},{9,10},{10,1... | collective-permute-start | bytes 1572872 | tf_op jit(solution)/shard_map/ppermute | solution.py:34
  64.9 23.7 %collective-permute-start.4 = (bf16[64,32,128]{2,1,0:T(8,128)(2,1)}, bf16[64,32,128]{2,1,0:T(8,128)(2,1)}, u32[]{:S(2)}, u32[]{:S(2)}) collective-permute-start(bf16[64,32,128]{2,1,0:T(8,128)(2,1)} %collective-permute-done.1.a), channel_id=1, source_target_pairs={{2,0},{3,1},{6,4},{7,5},{10,8},{11,9},{14,12},{15,13},{18,16},{19,... | collective-permute-start | bytes 1572872 | tf_op jit(solution)/shard_map/ppermute | solution.py:34
  66.1 28.4 %collective-permute-start.5 = (bf16[64,32,128]{2,1,0:T(8,128)(2,1)}, bf16[64,32,128]{2,1,0:T(8,128)(2,1)}, u32[]{:S(2)}, u32[]{:S(2)}) collective-permute-start(bf16[64,32,128]{2,1,0:T(8,128)(2,1)} %bitcast.21), channel_id=1, source_target_pairs={{0,3},{4,7},{8,11},{12,15},{16,19},{20,23},{24,27},{28,31},{32,35}... | collective-permute-start | bytes 1572872 | tf_op jit(solution)/shard_map/ppermute | solution.py:34
  74.4 20.1 %collective-permute-start.6 = (bf16[64,32,128]{2,1,0:T(8,128)(2,1)}, bf16[64,32,128]{2,1,0:T(8,128)(2,1)}, u32[]{:S(2)}, u32[]{:S(2)}) collective-permute-start(bf16[64,32,128]{2,1,0:T(8,128)(2,1)} %collective-permute-done.1.a), channel_id=1, source_target_pairs={{1,0},{2,1},{3,2},{5,4},{6,5},{7,6},{9,8},{10,9},{11,10},{13,12},{... | collective-permute-start | bytes 1572872 | tf_op jit(solution)/shard_map/ppermute | solution.py:34
  75.7 0.8 copy-start.7
  76.5 18.0 %collective-permute-start.9 = (bf16[64,32,128]{2,1,0:T(8,128)(2,1)}, bf16[64,32,128]{2,1,0:T(8,128)(2,1)}, u32[]{:S(2)}, u32[]{:S(2)}) collective-permute-start(bf16[64,32,128]{2,1,0:T(8,128)(2,1)} %collective-permute-done.3.b2), channel_id=1, source_target_pairs={{2,6},{3,7},{6,10},{7,11},{10,14},{11,15},{14,18},{15,19},{18,22},... | collective-permute-start | bytes 1572872 | tf_op jit(solution)/shard_map/ppermute | solution.py:34
  79.0 15.6 %collective-permute-start.7 = (bf16[64,32,128]{2,1,0:T(8,128)(2,1)}, bf16[64,32,128]{2,1,0:T(8,128)(2,1)}, u32[]{:S(2)}, u32[]{:S(2)}) collective-permute-start(bf16[64,32,128]{2,1,0:T(8,128)(2,1)} %collective-permute-done.2.c1), channel_id=1, source_target_pairs={{0,4},{4,8},{8,12},{12,16},{16,20},{20,24},{24,28},{32,36},{36,40}... | collective-permute-start | bytes 1572872 | tf_op jit(solution)/shard_map/ppermute | solution.py:34
  88.5 14.6 %collective-permute-start.8 = (bf16[64,32,128]{2,1,0:T(8,128)(2,1)}, bf16[64,32,128]{2,1,0:T(8,128)(2,1)}, u32[]{:S(2)}, u32[]{:S(2)}) collective-permute-start(bf16[64,32,128]{2,1,0:T(8,128)(2,1)} %collective-permute-done.4.c3), channel_id=1, source_target_pairs={{0,4},{1,5},{4,8},{5,9},{8,12},{9,13},{12,16},{13,17},{16,20},{17,... | collective-permute-start | bytes 1572872 | tf_op jit(solution)/shard_map/ppermute | solution.py:34
  103.1 1.0 copy-start.8
  104.1 28.9 %copy-start.9 = (bf16[256,256]{1,0:T(8,128)(2,1)S(1)}, bf16[256,256]{1,0:T(8,128)(2,1)}, u32[]{:S(2)}) copy-start(bf16[256,256]{1,0:T(8,128)(2,1)} %w_o.1) | copy-start | bytes 393220
  129.7 1.9 copy-start.1
  131.7 1.3 copy-start.5
  133.0 2.2 %copy-start.2 = (f32[64,64,256]{2,1,0:T(8,128)S(1)}, f32[64,64,256]{2,1,0:T(8,128)}, u32[]{:S(2)}) copy-start(f32[64,64,256]{2,1,0:T(8,128)} %copy-done.1) | copy-start | bytes 12582916
  135.2 1.6 copy-start.4
  136.8 1.6 copy-start.6
  186.4 1.3 collective-permute-start.10
  187.6 3.7 %collective-permute-start.11 = (f32[8,256]{1,0:T(8,128)S(1)}, f32[8,256]{1,0:T(8,128)S(1)}, u32[]{:S(2)}, u32[]{:S(2)}) collective-permute-start(f32[8,256]{1,0:T(8,128)S(1)} %fusion.1), channel_id=1, source_target_pairs={{0,64},{32,96},{64,0},{96,32},{128,192},{160,224},{192,128},{224,1... | collective-permute-start | bytes 24584 | tf_op jit(solution)/shard_map/ppermute | solution.py:232
  191.3 5.2 %collective-permute-start.12 = (f32[8,256]{1,0:T(8,128)S(1)}, f32[8,256]{1,0:T(8,128)S(1)}, u32[]{:S(2)}, u32[]{:S(2)}) collective-permute-start(f32[8,256]{1,0:T(8,128)S(1)} %add.27), channel_id=1, source_target_pairs={{0,128},{32,160},{64,192},{96,224},{128,0},{160,32},{192,64},{224,... | collective-permute-start | bytes 24584 | tf_op jit(solution)/shard_map/ppermute | solution.py:232

commit v2 on v1

v2 whole, which is shorter than its diff:
```python
import math

import jax
import jax.numpy as jnp
from jax import lax
from jax.experimental import pallas as pl
from jax.experimental.pallas import tpu as pltpu
from jax.sharding import PartitionSpec as P

D = 256
MD = 64
TT = 64
TILES = 64
KF = 64
KSEL = 8
CLASSES = 8
RUN = 4
RING = 4
PAIRS = TT // 2
LANES = 2 * MD
BLOCK = 16
NEAR = 4
LOW = -1e30
EXP2_SCALE = math.log2(math.e) / math.sqrt(D)
MIB = 1024 * 1024


def routed(shard, rows, target):
    pairs = []
    for row in range(rows):
        for place in range(RING):
            to = target(row, place)
            if to is not None and to[0] < rows:
                pairs.append((row * RING + place, to[0] * RING + to[1]))
    return lax.ppermute(shard, "tm", pairs)


def mix(tiles, position):
    return (tiles.astype(jnp.float32) + position).astype(jnp.bfloat16)


def times(left, right):
    return jnp.dot(left, right, preferred_element_type=jnp.float32)


def against(queries, pairs):
    keys = jnp.concatenate([pairs[:, :D], pairs[:, D:]], axis=0)
    return lax.dot_general(queries, keys, (((1,), (1,)), ((), ())), preferred_element_type=jnp.float32)


def gathered(weights, mixed):
    rows, pairs = weights.shape[0], mixed.shape[0]
    both = times(jnp.concatenate([weights[:, :pairs], weights[:, pairs:]], axis=0), mixed)
    lane = lax.broadcasted_iota(jnp.int32, (rows, LANES), 1)
    return jnp.where(lane < MD, both[:rows], both[rows:])


def absent(frame, first, count):
    column = lax.broadcasted_iota(jnp.int32, (1, 2 * count * PAIRS), 1)
    offset = (column // PAIRS) % count + first
    return jnp.where(offset <= frame, 0.0, LOW).astype(jnp.float32)


def ask_kernel(listed, asks):
    shape = asks.shape
    dest = lax.broadcasted_iota(jnp.int32, shape, 0)
    lane = lax.broadcasted_iota(jnp.int32, shape, 1)
    total = jnp.zeros(shape, jnp.int32)
    for run in range(KF // RUN):
        owner = listed[run * RUN] // TILES
        for slot in range(RUN):
            hit = (dest == owner) & (lane == slot)
            total = jnp.where(hit, listed[run * RUN + slot] % TILES, total)
    asks[...] = total


def pick_kernel(asked, own, *rest):
    outgoing = rest[-1]

    def one(dest, carry):
        for slot in range(RUN):
            outgoing[dest * RUN + slot] = own[asked[dest, slot]]
        return carry

    lax.fori_loop(0, asked.shape[0], one, 0)


def near_kernel(place, q, b1, c1, b2, c3, b3, c2, a, tpos, w_key, near, mixed):
    frame = place[0]
    y = frame % RING
    mixed[:, 0] = mix(jnp.where(y == 0, c1[...], b1[...]), tpos[0:1, :])
    mixed[:, 1] = mix(jnp.where(y < 2, c3[...], b2[...]), tpos[1:2, :])
    mixed[:, 2] = mix(jnp.where(y == 3, b3[...], c2[...]), tpos[2:3, :])
    mixed[:, 3] = mix(a[...], tpos[3:4, :])
    rows = NEAR * PAIRS
    flat = mixed[...].reshape(BLOCK * rows, LANES)
    pairs = times(flat, w_key[...]).astype(jnp.bfloat16)
    tiles = range(BLOCK)
    scores = jnp.concatenate([against(q[t], pairs[t * rows : (t + 1) * rows]) for t in tiles], axis=0)
    scores = scores * EXP2_SCALE + absent(frame, 1, NEAR)
    top = jnp.max(scores, axis=-1, keepdims=True)
    weights = jnp.exp2(scores - top)
    total = jnp.sum(weights, axis=-1, keepdims=True)
    weights = weights.astype(jnp.bfloat16)
    summed = jnp.concatenate(
        [gathered(weights[t * TT : (t + 1) * TT], flat[t * rows : (t + 1) * rows]) for t in tiles], axis=0
    )
    summed = summed + pltpu.roll(summed, MD, 1)
    lane = lax.broadcasted_iota(jnp.int32, summed.shape, 1)
    packed = jnp.where(lane < MD, summed, jnp.where(lane < MD + PAIRS, top, total))
    near[...] = packed.reshape(near.shape)


def final_kernel(
    place, listed, q, incoming, c1, d2, d1, z2, near, tpos, w_key, w_value, w_o, cot, branch, grad, tiles, mixed
):
    frame = place[0]
    y = frame % RING
    c = pl.program_id(0)
    for s in range(KSEL):
        run = 2 * s + c // RUN
        tiles[s] = incoming[(listed[run * RUN] // TILES) * RUN + c % RUN]
    keyed = mix(tiles[...], tpos[6:7, :]).reshape(KSEL * PAIRS, LANES)
    keyed_pairs = times(keyed, w_key[...]).astype(jnp.bfloat16)
    mixed[:, 0] = mix(jnp.where(y == 0, d2[:, 0], c1[:, 0]), tpos[4:5, :])
    mixed[:, 1] = mix(jnp.where(y < 2, d1[:, 0], z2[:, 0]), tpos[5:6, :])
    far_rows = 2 * PAIRS
    count = q.shape[0]
    rows = count * TT
    far = mixed[...].reshape(count * far_rows, LANES)
    far_pairs = times(far, w_key[...]).astype(jnp.bfloat16)
    queries = q[...].reshape(rows, D)
    scores = against(queries, keyed_pairs) * EXP2_SCALE
    far_scores = jnp.concatenate(
        [against(q[t, 0], far_pairs[t * far_rows : (t + 1) * far_rows]) for t in range(count)], axis=0
    )
    far_scores = far_scores * EXP2_SCALE + absent(frame, NEAR + 1, 2)
    packed = near[...].reshape(rows, LANES)
    near_top = packed[:, MD : MD + 1]
    near_sum = packed[:, MD + PAIRS : MD + PAIRS + 1]
    top = jnp.maximum(jnp.max(scores, axis=-1, keepdims=True), jnp.max(far_scores, axis=-1, keepdims=True))
    top = jnp.maximum(top, near_top)
    weights = jnp.exp2(scores - top)
    far_weights = jnp.exp2(far_scores - top)
    near_scale = jnp.exp2(near_top - top)
    total = jnp.sum(weights, axis=-1, keepdims=True) + jnp.sum(far_weights, axis=-1, keepdims=True)
    total = total + near_sum * near_scale
    weights = weights.astype(jnp.bfloat16)
    far_weights = far_weights.astype(jnp.bfloat16)
    summed = gathered(weights, keyed) + jnp.concatenate(
        [
            gathered(far_weights[t * TT : (t + 1) * TT], far[t * far_rows : (t + 1) * far_rows])
            for t in range(count)
        ],
        axis=0,
    )
    lane = lax.broadcasted_iota(jnp.int32, (rows, LANES), 1)
    summed = (summed + jnp.where(lane < MD, packed, 0.0) * near_scale) / total
    high = summed.astype(jnp.bfloat16)
    low = (summed - high.astype(jnp.float32)).astype(jnp.bfloat16)
    attended = times(jnp.concatenate([high, low], axis=1), w_value[...]).astype(jnp.bfloat16)
    branch[...] = times(attended, w_o[...]).astype(jnp.bfloat16).reshape(branch.shape)
    term = lax.dot_general(
        attended, cot[...].reshape(rows, D), (((0,), (0,)), ((), ())), preferred_element_type=jnp.float32
    )

    @pl.when(c == 0)
    def _():
        grad[...] = term

    @pl.when(c > 0)
    def _():
        grad[...] += term


def per_device(queries, memory, tpos, w_k, w_v, w_o, keyframes, cot):
    place = lax.axis_index("tm")[None]
    devices = lax.axis_size("tm")
    rows = devices // RING
    groups = TILES // CLASSES
    own = memory[0, 0].reshape(TILES, PAIRS, LANES)
    listed = keyframes.reshape(KF)
    in_smem = pl.BlockSpec(memory_space=pltpu.SMEM)
    in_vmem = pl.BlockSpec(memory_space=pltpu.VMEM)

    asks = pl.pallas_call(
        ask_kernel,
        out_shape=jax.ShapeDtypeStruct((devices, LANES), jnp.int32),
        in_specs=[in_smem],
        out_specs=in_vmem,
        name="ask",
    )(listed)
    a = routed(own, rows, lambda z, y: (z + 1, y))
    b1 = routed(own, rows, lambda z, y: (z, y + 1) if y < 3 else None)
    b2 = routed(own, rows, lambda z, y: (z, y + 2) if y < 2 else None)
    b3 = routed(own, rows, lambda z, y: (z, 3) if y == 0 else None)
    asked = lax.all_to_all(asks, "tm", split_axis=0, concat_axis=0, tiled=True)
    outgoing = pl.pallas_call(
        pick_kernel,
        out_shape=jax.ShapeDtypeStruct((devices * RUN, PAIRS, LANES), jnp.bfloat16),
        in_specs=[in_smem, in_vmem] + [pl.BlockSpec(memory_space=pl.ANY)] * 3,
        out_specs=in_vmem,
        compiler_params=pltpu.CompilerParams(vmem_limit_bytes=56 * MIB),
        name="pick",
    )(asked, own, a, b1, b3)
    incoming = lax.all_to_all(outgoing, "tm", split_axis=0, concat_axis=0, tiled=True)
    c1 = routed(a, rows, lambda z, y: (z, (y + 1) % RING))
    c2 = routed(a, rows, lambda z, y: (z, y - 1) if y > 0 else None)
    c3 = routed(a, rows, lambda z, y: (z, y - 2) if y > 1 else None)
    z2 = routed(b2, rows, lambda z, y: (z + 1, y) if y > 1 else None)
    d1 = routed(c3, rows, lambda z, y: (z + 1, y) if y < 2 else None)
    d2 = routed(c1, rows, lambda z, y: (z + 1, y) if y == 0 else None)

    zero = jnp.zeros_like(w_k)
    w_key = jnp.concatenate(
        [jnp.concatenate([w_k, zero], axis=1), jnp.concatenate([zero, w_k], axis=1)], axis=0
    )
    w_value = jnp.concatenate([w_v] * 4, axis=0)
    tpos_pair = jnp.concatenate([tpos, tpos], axis=1)
    q_tiles = queries[0, 0].reshape(TILES, TT, D)
    whole = lambda *shape: pl.BlockSpec(shape, lambda i, *_: (0,) * len(shape))
    tile_block = pl.BlockSpec((BLOCK, PAIRS, LANES), lambda i, *_: (i, 0, 0))
    row_block = lambda width: pl.BlockSpec((BLOCK, TT, width), lambda i, *_: (i, 0, 0))
    near = pl.pallas_call(
        near_kernel,
        grid_spec=pltpu.PrefetchScalarGridSpec(
            num_scalar_prefetch=1,
            grid=(TILES // BLOCK,),
            in_specs=[row_block(D)] + [tile_block] * 7 + [whole(7, LANES), whole(LANES, 2 * D)],
            out_specs=row_block(LANES),
            scratch_shapes=[pltpu.VMEM((BLOCK, NEAR, PAIRS, LANES), jnp.bfloat16)],
        ),
        out_shape=jax.ShapeDtypeStruct((TILES, TT, LANES), jnp.float32),
        compiler_params=pltpu.CompilerParams(vmem_limit_bytes=56 * MIB),
        name="near",
    )(place, q_tiles, b1, c1, b2, c3, b3, c2, a, tpos_pair, w_key)

    by_class = lambda x: x.reshape((groups, CLASSES) + x.shape[1:])
    class_block = lambda *tile: pl.BlockSpec((groups, 1) + tile, lambda i, *_: (0, i) + (0,) * len(tile))
    branch, grad = pl.pallas_call(
        final_kernel,
        grid_spec=pltpu.PrefetchScalarGridSpec(
            num_scalar_prefetch=2,
            grid=(CLASSES,),
            in_specs=[class_block(TT, D), whole(devices * RUN, PAIRS, LANES)]
            + [class_block(PAIRS, LANES)] * 4
            + [
                class_block(TT, LANES),
                whole(7, LANES),
                whole(LANES, 2 * D),
                whole(2 * LANES, D),
                whole(D, D),
                class_block(TT, D),
            ],
            out_specs=[class_block(TT, D), whole(D, D)],
            scratch_shapes=[
                pltpu.VMEM((KSEL, PAIRS, LANES), jnp.bfloat16),
                pltpu.VMEM((groups, 2, PAIRS, LANES), jnp.bfloat16),
            ],
        ),
        out_shape=[
            jax.ShapeDtypeStruct((groups, CLASSES, TT, D), jnp.bfloat16),
            jax.ShapeDtypeStruct((D, D), jnp.float32),
        ],
        compiler_params=pltpu.CompilerParams(vmem_limit_bytes=56 * MIB),
        name="final",
    )(
        place,
        listed,
        by_class(q_tiles),
        incoming,
        by_class(c1),
        by_class(d2),
        by_class(d1),
        by_class(z2),
        by_class(near),
        tpos_pair,
        w_key,
        w_value,
        w_o,
        by_class(cot[0, 0].reshape(TILES, TT, D)),
    )

    parts = lax.all_to_all(
        grad.reshape(devices, D // devices, D), "tm", split_axis=0, concat_axis=0, tiled=True
    )
    videos = lax.axis_size("video")
    summed = jnp.sum(parts, axis=0) * (1.0 / math.sqrt(videos * devices * TILES * TT))
    step = 1
    while step < videos:
        summed = summed + lax.ppermute(summed, "video", [(i, i ^ step) for i in range(videos)])
        step *= 2
    return branch.reshape(queries.shape), summed


def solution(mesh):
    in_specs = (
        P("video", "tm", None, None),
        P("video", "tm", None, None),
        P(),
        P(),
        P(),
        P(),
        P("video", "tm", None),
        P("video", "tm", None, None),
    )
    out_specs = (P("video", "tm", None, None), P("tm", None))
    return jax.shard_map(
        per_device, mesh=mesh, in_specs=in_specs, out_specs=out_specs, check_vma=False
    )
```

time: 198 us -> 152 us (0.77)
  starting transfers between devices: 54.5 us -> 32.3 us
  Pallas kernels: 53.9 us -> 35.2 us
  blocking collectives: 21.7 us -> 37.2 us
  waiting for transfers between devices: 50.7 us -> 39.7 us
  local copies, waits for them, and re-layouts: 13.1 us -> 3.28 us
    pallas_call x2 -> x3, Pallas kernels: 51.8 us -> 32.9 us  [the longest x1 22.1 us: per_device(): pl.pallas_call(final_kernel, grid_spec=pltpu.PrefetchScalarGridSpec(num_s...]
    all_to_all x0 -> x1, blocking collectives: none -> 18 us  [per_device(): asked = lax.all_to_all(asks, 'tm', split_axis=0, concat_axis=0, tiled=True)]
    all_to_all x1 -> x0, starting transfers between devices: 11.5 us -> none  [per_device(): asked = lax.all_to_all(asks, 'tm', split_axis=0, concat_axis=0, tiled=True)]
    ppermute x10, starting transfers between devices: 36.8 us -> 26.1 us  [routed(): return lax.ppermute(shard, 'tm', pairs)]
    unnamed x28 -> x25, local copies, waits for them, and re-layouts: 12.2 us -> 3.28 us
    all_to_all x1 -> x0, waiting for transfers between devices: 8.54 us -> none  [per_device(): asked = lax.all_to_all(asks, 'tm', split_axis=0, concat_axis=0, tiled=True)]
    all_to_all x1, blocking collectives: 21.7 us -> 19.3 us  [per_device(): lax.all_to_all(grad.reshape(devices, D // devices, D), 'tm', split_axis=0...]
    ppermute x10, waiting for transfers between devices: 34.4 us -> 32 us  [routed(): return lax.ppermute(shard, 'tm', pairs)]
  transfers between devices with their start and end apart: 15 -> 14, of which waited for: 8 -> 6; matrix products, arithmetic and copies ran while one was open for 1% -> 1% of each run, Pallas kernels for 13% -> 7%
where the time goes in v2:
time: 152 us; the launch traced here: 151 us
  waiting for transfers between devices  39.7 us (26%)
  blocking collectives  37.2 us (24%)
  Pallas kernels  35.2 us (23%)
  starting transfers between devices  32.3 us (21%)
  local copies, waits for them, and re-layouts  3.28 us (2%)
  other arithmetic  2.64 us (2%)
    ppermute x10, waiting for transfers between devices, routed(): return lax.ppermute(shard, 'tm', pairs)  32 us
    ppermute x10, starting transfers between devices, routed(): return lax.ppermute(shard, 'tm', pairs)  26.1 us
    pallas_call x1, Pallas kernels, per_device(): pl.pallas_call(final_kernel, grid_spec=pltpu.PrefetchScalarGridSpec(num_s...  22.1 us
    all_to_all x1, blocking collectives, per_device(): lax.all_to_all(grad.reshape(devices, D // devices, D), 'tm', split_axis=0...  19.3 us
    all_to_all x1, blocking collectives, per_device(): asked = lax.all_to_all(asks, 'tm', split_axis=0, concat_axis=0, tiled=True)  18 us
    pallas_call x1, Pallas kernels, per_device(): pl.pallas_call(near_kernel, grid_spec=pltpu.PrefetchScalarGridSpec(num_sc...  9.25 us
    ppermute x3, waiting for transfers between devices, per_device(): lax.ppermute(summed, 'video', [(i, i ^ step) for i in range(videos)])  7.73 us
    all_to_all x1, starting transfers between devices, per_device(): lax.all_to_all(outgoing, 'tm', split_axis=0, concat_axis=0, tiled=True)  3.93 us
  transfers between devices with their start and end apart: 14, of which 6 were waited for; matrix products, arithmetic and copies ran while one was open for 1% of the time, Pallas kernels for 7%

profile of v2, /device:TPU:6, one launch (start us, length us, event | category | flops | bytes accessed | tf_op | source)
XLA Modules:
  0.0 151.2 jit_solution(4654665661046658590)
XLA Ops:
  0.6 1.1 copy.11
  1.8 3.9 %collective-permute-start = (bf16[64,32,128]{2,1,0:T(8,128)(2,1)S(1)}, bf16[64,32,128]{2,1,0:T(8,128)(2,1)S(1)}, u32[]{:S(2)}, u32[]{:S(2)}) collective-permute-start(bf16[64,32,128]{2,1,0:T(8,128)(2,1)S(1)} %bitcast.24), channel_id=1, source_target_pairs={{0,4},{1,5},{2,6},{3,7},{4,8},{5,9},{6,10},{7,11},{8,12},{9,13},{1... | collective-permute-start | bytes 1572872 | tf_op jit(solution)/shard_map/ppermute | solution.py:35
  5.6 3.5 %collective-permute-start.1 = (bf16[64,32,128]{2,1,0:T(8,128)(2,1)S(1)}, bf16[64,32,128]{2,1,0:T(8,128)(2,1)S(1)}, u32[]{:S(2)}, u32[]{:S(2)}) collective-permute-start(bf16[64,32,128]{2,1,0:T(8,128)(2,1)S(1)} %bitcast.25), channel_id=1, source_target_pairs={{0,1},{1,2},{2,3},{4,5},{5,6},{6,7},{8,9},{9,10},{10,11},{12,13},{... | collective-permute-start | bytes 1572872 | tf_op jit(solution)/shard_map/ppermute | solution.py:35
  9.2 2.7 %collective-permute-start.2 = (bf16[64,32,128]{2,1,0:T(8,128)(2,1)S(1)}, bf16[64,32,128]{2,1,0:T(8,128)(2,1)S(1)}, u32[]{:S(2)}, u32[]{:S(2)}) collective-permute-start(bf16[64,32,128]{2,1,0:T(8,128)(2,1)S(1)} %bitcast.26), channel_id=1, source_target_pairs={{0,3},{4,7},{8,11},{12,15},{16,19},{20,23},{24,27},{28,31},{32,35}... | collective-permute-start | bytes 1572872 | tf_op jit(solution)/shard_map/ppermute | solution.py:35
  11.9 1.5 ask.1
  13.4 18.0 %all_to_all.21 = s32[32,1,128]{2,1,0:T(1,128)} all-to-all(s32[32,1,128]{2,1,0:T(1,128)} %bitcast.34), channel_id=1, replica_groups=mesh['video'=8,'tm'=32] {'tm'}, dimensions={0} | all-to-all | bytes 32768 | tf_op jit(solution)/shard_map/all_to_all | solution.py:197
  31.4 0.0 collective-permute-done.rest_0_.a
  31.4 0.0 collective-permute-done.1.rest_1_.b1
  31.4 0.0 collective-permute-done.2.rest_2_.b3
  31.4 0.0 copy-start.4
  31.4 0.0 copy-done.5
  31.4 0.7 copy-done.2
  32.2 0.2 copy-done.3
  32.3 0.2 copy-done.4
  32.5 2.4 %pick.1 = bf16[128,32,128]{2,1,0:T(8,128)(2,1)} custom-call(s32[32,128]{1,0:T(8,128)} %bitcast.33, bf16[64,32,128]{2,1,0:T(8,128)(2,1)} %bitcast.27, bf16[64,32,128]{2,1,0:T(8,128)(2,1)} %copy-done.2, bf16[64,32,128]{2,1,0:T(8,128)(2,1)} %copy-done.3, bf16[64,32,128]{2,1,0:T(8,128)(2,1)} %copy-done.4), custom_call_target="tpu_custom_call" | custom-call | tf_op jit(solution)/shard_map/pick/pallas_call | solution.py:198
  34.9 3.9 %all-to-all-start.1 = ((bf16[128,32,128]{2,1,0:T(8,128)(2,1)}), bf16[128,32,128]{2,1,0:T(8,128)(2,1)S(1)}, u32[]{:S(2)}, u32[]{:S(2)}) async-start(bf16[128,32,128]{2,1,0:T(8,128)(2,1)} %pick.1), calls=%async_computation.1 | async-start | bytes 2097152 | tf_op jit(solution)/shard_map/all_to_all | solution.py:206
  38.8 5.1 %collective-permute-start.7 = (bf16[64,32,128]{2,1,0:T(8,128)(2,1)}, bf16[64,32,128]{2,1,0:T(8,128)(2,1)S(1)}, u32[]{:S(2)}, u32[]{:S(2)}) collective-permute-start(bf16[64,32,128]{2,1,0:T(8,128)(2,1)} %bitcast.28), channel_id=1, source_target_pairs={{0,2},{1,3},{4,6},{5,7},{8,10},{9,11},{12,14},{13,15},{16,18},{17,... | collective-permute-start | bytes 1572872 | tf_op jit(solution)/shard_map/ppermute | solution.py:35
  44.0 0.6 collective-permute-start.3
  44.6 1.3 collective-permute-start.5
  45.9 1.3 collective-permute-start.9
  47.2 16.3 %collective-permute-done.7.b2 = bf16[64,32,128]{2,1,0:T(8,128)(2,1)S(1)} collective-permute-done((bf16[64,32,128]{2,1,0:T(8,128)(2,1)}, bf16[64,32,128]{2,1,0:T(8,128)(2,1)S(1)}, u32[]{:S(2)}, u32[]{:S(2)}) %collective-permute-start.7) | collective-permute-done | bytes 524320 | tf_op jit(solution)/shard_map/ppermute | solution.py:35
  63.6 0.7 collective-permute-start.8
  64.2 12.4 %collective-permute-done.3.c1 = bf16[64,32,128]{2,1,0:T(8,128)(2,1)S(1)} collective-permute-done((bf16[64,32,128]{2,1,0:T(8,128)(2,1)}, bf16[64,32,128]{2,1,0:T(8,128)(2,1)S(1)}, u32[]{:S(2)}, u32[]{:S(2)}) %collective-permute-start.3) | collective-permute-done | bytes 524320 | tf_op jit(solution)/shard_map/ppermute | solution.py:35
  76.6 4.1 %collective-permute-start.4 = (bf16[64,32,128]{2,1,0:T(8,128)(2,1)S(1)}, bf16[64,32,128]{2,1,0:T(8,128)(2,1)}, u32[]{:S(2)}, u32[]{:S(2)}) collective-permute-start(bf16[64,32,128]{2,1,0:T(8,128)(2,1)S(1)} %collective-permute-done.3.c1), channel_id=1, source_target_pairs={{0,4},{4,8},{8,12},{12,16},{16,20},{20,24},{24,28},{32,36},{36,40}... | collective-permute-start | bytes 1572872 | tf_op jit(solution)/shard_map/ppermute | solution.py:35
  80.7 0.0 collective-permute-done.5.c3
  80.7 2.8 %collective-permute-start.6 = (bf16[64,32,128]{2,1,0:T(8,128)(2,1)S(1)}, bf16[64,32,128]{2,1,0:T(8,128)(2,1)}, u32[]{:S(2)}, u32[]{:S(2)}) collective-permute-start(bf16[64,32,128]{2,1,0:T(8,128)(2,1)S(1)} %collective-permute-done.5.c3), channel_id=1, source_target_pairs={{0,4},{1,5},{4,8},{5,9},{8,12},{9,13},{12,16},{13,17},{16,20},{17,... | collective-permute-start | bytes 1572872 | tf_op jit(solution)/shard_map/ppermute | solution.py:35
  83.6 0.7 pad_maximum_fusion.1.tpos
  84.2 0.7 fusion.2.w_key
  84.9 0.7 pad_maximum_fusion.w_value
  85.6 0.0 collective-permute-done.9.c2
  85.6 0.0 copy-done.1
  85.6 9.2 %near.1 = f32[64,64,128]{2,1,0:T(8,128)} custom-call(s32[1]{0:T(128)} %bitcast.place, bf16[64,64,256]{2,1,0:T(8,128)(2,1)} %bitcast.20, bf16[64,32,128]{2,1,0:T(8,128)(2,1)} %copy-done.3, bf16[64,32,128]{2,1,0:T(8,128)(2,1)} %copy-done.1, bf16[64,32,128]{2,1,0:T(8,128)(2,1)} %copy-done.7, bf16[64,32,128]{2,1,0:T(8,128)(2,1)} %copy-done.8, ...), custom_call_target="tpu_custom_call" | custom-call | tf_op jit(solution)/shard_map/near/pallas_call | solution.py:224
  94.8 0.0 collective-permute-done.8
  94.8 0.0 copy-start.6
  94.9 0.0 collective-permute-done.4
  94.9 3.2 %collective-permute-done.6 = bf16[64,32,128]{2,1,0:T(8,128)(2,1)} collective-permute-done((bf16[64,32,128]{2,1,0:T(8,128)(2,1)S(1)}, bf16[64,32,128]{2,1,0:T(8,128)(2,1)}, u32[]{:S(2)}, u32[]{:S(2)}) %collective-permute-start.6) | collective-permute-done | bytes 524320 | tf_op jit(solution)/shard_map/ppermute | solution.py:35
  98.1 0.0 all-to-all-done.1.incoming
  98.1 0.0 copy-done.6
  98.1 1.0 copy-done
  99.1 22.1 %final.1 = (bf16[8,8,64,256]{3,2,1,0:T(8,128)(2,1)}, f32[256,256]{1,0:T(8,128)}) custom-call(s32[1]{0:T(128)} %bitcast.place, s32[64]{0:T(128)} %bitcast.36, bf16[8,8,64,256]{3,2,1,0:T(8,128)(2,1)} %bitcast.21, bf16[128,32,128]{2,1,0:T(8,128)(2,1)} %copy-done, bf16[8,8,32,128]{3,2,1,0:T(8,128)(2,1)} %bitcast.23, bf16[8,8,32,128]{3,2,1,0:T(8,128)(2,1)} %bitcast.7.d2, ...), custom_call_target="tpu_custom_call" | custom-call | tf_op jit(solution)/shard_map/final/pallas_call | solution.py:240
  121.2 19.3 %all_to_all.22 = f32[32,8,256]{2,1,0:T(8,128)S(1)} all-to-all(f32[32,8,256]{2,1,0:T(8,128)} %bitcast.32), channel_id=1, replica_groups=mesh['video'=8,'tm'=32] {'tm'}, dimensions={0} | all-to-all | bytes 524288 | tf_op jit(solution)/shard_map/all_to_all | solution.py:284
  140.5 0.1 collective-permute-start.10
  140.6 1.2 collective-permute-done.10
  141.8 0.8 collective-permute-start.11
  142.6 2.8 %collective-permute-done.11 = f32[8,256]{1,0:T(8,128)S(1)} collective-permute-done((f32[8,256]{1,0:T(8,128)S(1)}, f32[8,256]{1,0:T(8,128)S(1)}, u32[]{:S(2)}, u32[]{:S(2)}) %collective-permute-start.11) | collective-permute-done | bytes 8224 | tf_op jit(solution)/shard_map/ppermute | solution.py:291
  145.4 1.4 collective-permute-start.12
  146.8 3.8 %collective-permute-done.12 = f32[8,256]{1,0:T(8,128)S(1)} collective-permute-done((f32[8,256]{1,0:T(8,128)S(1)}, f32[8,256]{1,0:T(8,128)S(1)}, u32[]{:S(2)}, u32[]{:S(2)}) %collective-permute-start.12) | collective-permute-done | bytes 8224 | tf_op jit(solution)/shard_map/ppermute | solution.py:291
  150.6 0.6 add.15
  (19 shorter events, 0.1 us)
Async XLA Ops:
  1.8 29.6 %copy-start.5 = (bf16[8,8,32,128]{3,2,1,0:T(8,128)(2,1)}, bf16[8,8,32,128]{3,2,1,0:T(8,128)(2,1)S(1)}, u32[]{:S(2)}) copy-start(bf16[8,8,32,128]{3,2,1,0:T(8,128)(2,1)S(1)} %copy.11) | copy-start | bytes 1572868
  1.8 29.6 %collective-permute-start = (bf16[64,32,128]{2,1,0:T(8,128)(2,1)S(1)}, bf16[64,32,128]{2,1,0:T(8,128)(2,1)S(1)}, u32[]{:S(2)}, u32[]{:S(2)}) collective-permute-start(bf16[64,32,128]{2,1,0:T(8,128)(2,1)S(1)} %bitcast.24), channel_id=1, source_target_pairs={{0,4},{1,5},{2,6},{3,7},{4,8},{5,9},{6,10},{7,11},{8,12},{9,13},{1... | collective-permute-start | bytes 1572872 | tf_op jit(solution)/shard_map/ppermute | solution.py:35
  5.6 25.7 %collective-permute-start.1 = (bf16[64,32,128]{2,1,0:T(8,128)(2,1)S(1)}, bf16[64,32,128]{2,1,0:T(8,128)(2,1)S(1)}, u32[]{:S(2)}, u32[]{:S(2)}) collective-permute-start(bf16[64,32,128]{2,1,0:T(8,128)(2,1)S(1)} %bitcast.25), channel_id=1, source_target_pairs={{0,1},{1,2},{2,3},{4,5},{5,6},{6,7},{8,9},{9,10},{10,11},{12,13},{... | collective-permute-start | bytes 1572872 | tf_op jit(solution)/shard_map/ppermute | solution.py:35
  9.2 22.2 %collective-permute-start.2 = (bf16[64,32,128]{2,1,0:T(8,128)(2,1)S(1)}, bf16[64,32,128]{2,1,0:T(8,128)(2,1)S(1)}, u32[]{:S(2)}, u32[]{:S(2)}) collective-permute-start(bf16[64,32,128]{2,1,0:T(8,128)(2,1)S(1)} %bitcast.26), channel_id=1, source_target_pairs={{0,3},{4,7},{8,11},{12,15},{16,19},{20,23},{24,27},{28,31},{32,35}... | collective-permute-start | bytes 1572872 | tf_op jit(solution)/shard_map/ppermute | solution.py:35
  31.4 0.8 copy-start.2
  31.4 1.0 copy-start.3
  31.4 1.1 copy-start.4
  32.5 51.0 %copy-start.11 = (f32[7,64]{1,0:T(8,128)S(1)}, f32[7,64]{1,0:T(8,128)}, u32[]{:S(2)}) copy-start(f32[7,64]{1,0:T(8,128)} %param.10) | copy-start | bytes 5380
  32.5 51.7 %copy-start.9 = (bf16[64,256]{1,0:T(8,128)(2,1)S(1)}, bf16[64,256]{1,0:T(8,128)(2,1)}, u32[]{:S(2)}) copy-start(bf16[64,256]{1,0:T(8,128)(2,1)} %param.11) | copy-start | bytes 98308
  32.5 52.4 %copy-start.10 = (bf16[64,256]{1,0:T(8,128)(2,1)S(1)}, bf16[64,256]{1,0:T(8,128)(2,1)}, u32[]{:S(2)}) copy-start(bf16[64,256]{1,0:T(8,128)(2,1)} %param.12) | copy-start | bytes 98308
  34.9 63.2 %all-to-all-start.1 = ((bf16[128,32,128]{2,1,0:T(8,128)(2,1)}), bf16[128,32,128]{2,1,0:T(8,128)(2,1)S(1)}, u32[]{:S(2)}, u32[]{:S(2)}) async-start(bf16[128,32,128]{2,1,0:T(8,128)(2,1)} %pick.1), calls=%async_computation.1 | async-start | bytes 2097152 | tf_op jit(solution)/shard_map/all_to_all | solution.py:206
  38.8 24.7 %collective-permute-start.7 = (bf16[64,32,128]{2,1,0:T(8,128)(2,1)}, bf16[64,32,128]{2,1,0:T(8,128)(2,1)S(1)}, u32[]{:S(2)}, u32[]{:S(2)}) collective-permute-start(bf16[64,32,128]{2,1,0:T(8,128)(2,1)} %bitcast.28), channel_id=1, source_target_pairs={{0,2},{1,3},{4,6},{5,7},{8,10},{9,11},{12,14},{13,15},{16,18},{17,... | collective-permute-start | bytes 1572872 | tf_op jit(solution)/shard_map/ppermute | solution.py:35
  44.0 32.7 %collective-permute-start.3 = (bf16[64,32,128]{2,1,0:T(8,128)(2,1)}, bf16[64,32,128]{2,1,0:T(8,128)(2,1)S(1)}, u32[]{:S(2)}, u32[]{:S(2)}) collective-permute-start(bf16[64,32,128]{2,1,0:T(8,128)(2,1)} %copy-done.2), channel_id=1, source_target_pairs={{0,1},{1,2},{2,3},{3,0},{4,5},{5,6},{6,7},{7,4},{8,9},{9,10},{10,1... | collective-permute-start | bytes 1572872 | tf_op jit(solution)/shard_map/ppermute | solution.py:35
  44.6 36.1 %collective-permute-start.5 = (bf16[64,32,128]{2,1,0:T(8,128)(2,1)}, bf16[64,32,128]{2,1,0:T(8,128)(2,1)S(1)}, u32[]{:S(2)}, u32[]{:S(2)}) collective-permute-start(bf16[64,32,128]{2,1,0:T(8,128)(2,1)} %copy-done.2), channel_id=1, source_target_pairs={{2,0},{3,1},{6,4},{7,5},{10,8},{11,9},{14,12},{15,13},{18,16},{19,... | collective-permute-start | bytes 1572872 | tf_op jit(solution)/shard_map/ppermute | solution.py:35
  45.9 39.7 %collective-permute-start.9 = (bf16[64,32,128]{2,1,0:T(8,128)(2,1)}, bf16[64,32,128]{2,1,0:T(8,128)(2,1)}, u32[]{:S(2)}, u32[]{:S(2)}) collective-permute-start(bf16[64,32,128]{2,1,0:T(8,128)(2,1)} %copy-done.2), channel_id=1, source_target_pairs={{1,0},{2,1},{3,2},{5,4},{6,5},{7,6},{9,8},{10,9},{11,10},{13,12},{... | collective-permute-start | bytes 1572872 | tf_op jit(solution)/shard_map/ppermute | solution.py:35
  63.6 22.0 %copy-start.7 = (bf16[64,32,128]{2,1,0:T(8,128)(2,1)}, bf16[64,32,128]{2,1,0:T(8,128)(2,1)S(1)}, u32[]{:S(2)}) copy-start(bf16[64,32,128]{2,1,0:T(8,128)(2,1)S(1)} %collective-permute-done.7.b2) | copy-start | bytes 1572868
  63.6 31.3 %collective-permute-start.8 = (bf16[64,32,128]{2,1,0:T(8,128)(2,1)S(1)}, bf16[64,32,128]{2,1,0:T(8,128)(2,1)S(1)}, u32[]{:S(2)}, u32[]{:S(2)}) collective-permute-start(bf16[64,32,128]{2,1,0:T(8,128)(2,1)S(1)} %collective-permute-done.7.b2), channel_id=1, source_target_pairs={{2,6},{3,7},{6,10},{7,11},{10,14},{11,15},{14,18},{15,19},{18,22},... | collective-permute-start | bytes 1572872 | tf_op jit(solution)/shard_map/ppermute | solution.py:35
  76.6 9.0 %copy-start.1 = (bf16[64,32,128]{2,1,0:T(8,128)(2,1)}, bf16[64,32,128]{2,1,0:T(8,128)(2,1)S(1)}, u32[]{:S(2)}) copy-start(bf16[64,32,128]{2,1,0:T(8,128)(2,1)S(1)} %collective-permute-done.3.c1) | copy-start | bytes 1572868
  76.6 18.2 %collective-permute-start.4 = (bf16[64,32,128]{2,1,0:T(8,128)(2,1)S(1)}, bf16[64,32,128]{2,1,0:T(8,128)(2,1)}, u32[]{:S(2)}, u32[]{:S(2)}) collective-permute-start(bf16[64,32,128]{2,1,0:T(8,128)(2,1)S(1)} %collective-permute-done.3.c1), channel_id=1, source_target_pairs={{0,4},{4,8},{8,12},{12,16},{16,20},{20,24},{24,28},{32,36},{36,40}... | collective-permute-start | bytes 1572872 | tf_op jit(solution)/shard_map/ppermute | solution.py:35
  80.7 4.9 %copy-start.8 = (bf16[64,32,128]{2,1,0:T(8,128)(2,1)}, bf16[64,32,128]{2,1,0:T(8,128)(2,1)S(1)}, u32[]{:S(2)}) copy-start(bf16[64,32,128]{2,1,0:T(8,128)(2,1)S(1)} %collective-permute-done.5.c3) | copy-start | bytes 1572868
  80.7 17.3 %collective-permute-start.6 = (bf16[64,32,128]{2,1,0:T(8,128)(2,1)S(1)}, bf16[64,32,128]{2,1,0:T(8,128)(2,1)}, u32[]{:S(2)}, u32[]{:S(2)}) collective-permute-start(bf16[64,32,128]{2,1,0:T(8,128)(2,1)S(1)} %collective-permute-done.5.c3), channel_id=1, source_target_pairs={{0,4},{1,5},{4,8},{5,9},{8,12},{9,13},{12,16},{13,17},{16,20},{17,... | collective-permute-start | bytes 1572872 | tf_op jit(solution)/shard_map/ppermute | solution.py:35
  94.8 3.2 %copy-start.6 = (bf16[64,32,128]{2,1,0:T(8,128)(2,1)}, bf16[64,32,128]{2,1,0:T(8,128)(2,1)S(1)}, u32[]{:S(2)}) copy-start(bf16[64,32,128]{2,1,0:T(8,128)(2,1)S(1)} %collective-permute-done.8) | copy-start | bytes 1572868
  98.1 1.0 copy-start
  140.5 1.3 collective-permute-start.10
  141.8 3.7 %collective-permute-start.11 = (f32[8,256]{1,0:T(8,128)S(1)}, f32[8,256]{1,0:T(8,128)S(1)}, u32[]{:S(2)}, u32[]{:S(2)}) collective-permute-start(f32[8,256]{1,0:T(8,128)S(1)} %fusion.3), channel_id=1, source_target_pairs={{0,64},{32,96},{64,0},{96,32},{128,192},{160,224},{192,128},{224,1... | collective-permute-start | bytes 24584 | tf_op jit(solution)/shard_map/ppermute | solution.py:291
  145.4 5.2 %collective-permute-start.12 = (f32[8,256]{1,0:T(8,128)S(1)}, f32[8,256]{1,0:T(8,128)S(1)}, u32[]{:S(2)}, u32[]{:S(2)}) collective-permute-start(f32[8,256]{1,0:T(8,128)S(1)} %add.14), channel_id=1, source_target_pairs={{0,128},{32,160},{64,192},{96,224},{128,0},{160,32},{192,64},{224,... | collective-permute-start | bytes 24584 | tf_op jit(solution)/shard_map/ppermute | solution.py:291

commit v3 on v2

v3 whole, which is shorter than its diff:
```python
import math

import jax
import jax.numpy as jnp
from jax import lax
from jax.experimental import pallas as pl
from jax.experimental.pallas import tpu as pltpu
from jax.sharding import PartitionSpec as P

D = 256
MD = 64
TT = 64
TILES = 64
KF = 64
KSEL = 8
CLASSES = 8
RUN = 4
RING = 4
PAIRS = TT // 2
LANES = 2 * MD
BLOCK = 16
EARLY = (1, 4)
LATE = (2, 3, 5, 6)
SHARED = 4
LOW = -1e30
EXP2_SCALE = math.log2(math.e) / math.sqrt(D)
MIB = 1024 * 1024


def routed(shard, rows, target):
    pairs = []
    for row in range(rows):
        for place in range(RING):
            to = target(row, place)
            if to is not None and to[0] < rows:
                pairs.append((row * RING + place, to[0] * RING + to[1]))
    return lax.ppermute(shard, "tm", pairs)


def mix(tiles, position):
    return (tiles.astype(jnp.float32) + position).astype(jnp.bfloat16)


def times(left, right):
    return jnp.dot(left, right, preferred_element_type=jnp.float32)


def against(queries, pairs):
    keys = jnp.concatenate([pairs[:, :D], pairs[:, D:]], axis=0)
    return lax.dot_general(queries, keys, (((1,), (1,)), ((), ())), preferred_element_type=jnp.float32)


def spread(mixed):
    lane = lax.broadcasted_iota(jnp.int32, mixed.shape, 1)
    zero = jnp.zeros_like(mixed)
    rows = jnp.concatenate([jnp.where(lane < MD, mixed, zero), jnp.where(lane < MD, zero, mixed)], axis=0)
    return jnp.concatenate([rows, jnp.ones_like(rows)], axis=1)


def absent(frame, offsets):
    column = lax.broadcasted_iota(jnp.int32, (1, 2 * len(offsets) * PAIRS), 1)
    part = (column // PAIRS) % len(offsets)
    bias = jnp.zeros(column.shape, jnp.float32)
    for at, offset in enumerate(offsets):
        bias = jnp.where((part == at) & (frame < offset), LOW, bias)
    return bias


def packed_with(both, top):
    values = both[:, :LANES]
    values = values + pltpu.roll(values, MD, 1)
    lane = lax.broadcasted_iota(jnp.int32, values.shape, 1)
    return jnp.where(lane < MD, values, jnp.where(lane < MD + PAIRS, top, both[:, LANES:]))


def ask_kernel(listed, asks):
    shape = asks.shape
    dest = lax.broadcasted_iota(jnp.int32, shape, 0)
    lane = lax.broadcasted_iota(jnp.int32, shape, 1)
    total = jnp.zeros(shape, jnp.int32)
    for run in range(KF // RUN):
        owner = listed[run * RUN] // TILES
        for slot in range(RUN):
            hit = (dest == owner) & (lane == slot)
            total = jnp.where(hit, listed[run * RUN + slot] % TILES, total)
    asks[...] = total


def weights_kernel(w_k, w_v, tpos, *rest):
    w_key, w_value, tpos_pair = rest[-3:]
    zero = jnp.zeros((MD, D), jnp.bfloat16)
    w_key[:MD, :] = jnp.concatenate([w_k[...], zero], axis=1)
    w_key[MD:, :] = jnp.concatenate([zero, w_k[...]], axis=1)
    for part in range(4):
        w_value[part * MD : (part + 1) * MD, :] = w_v[...]
    tpos_pair[...] = jnp.concatenate([tpos[...], tpos[...]], axis=1)


def pick_kernel(asked, own, *rest):
    outgoing = rest[-1]

    def one(dest, carry):
        for slot in range(RUN):
            outgoing[dest * RUN + slot] = own[asked[dest, slot]]
        return carry

    lax.fori_loop(0, asked.shape[0], one, 0)


def keyed_kernel(place, listed, q, incoming, b1, c1, a, tpos, w_key, packed, tiles, mixed):
    frame = place[0]
    y = frame % RING
    step = pl.program_id(0)
    count = q.shape[0]
    rows = count * TT
    part_rows = 2 * PAIRS
    bias = absent(frame, EARLY)
    several = range(SHARED)
    for k in several:
        c = step * SHARED + k
        for s in range(KSEL):
            run = 2 * s + c // RUN
            tiles[k, s] = incoming[(listed[run * RUN] // TILES) * RUN + c % RUN]
        mixed[k, :, 0] = mix(jnp.where(y == 0, c1[:, k], b1[:, k]), tpos[0:1, :])
        mixed[k, :, 1] = mix(a[:, k], tpos[3:4, :])
    keyed = mix(tiles[...], tpos[6:7, :]).reshape(SHARED, KSEL * PAIRS, LANES)
    near = mixed[...].reshape(SHARED, count * part_rows, LANES)
    keyed_pairs = [times(keyed[k], w_key[...]).astype(jnp.bfloat16) for k in several]
    near_pairs = [times(near[k], w_key[...]).astype(jnp.bfloat16) for k in several]
    part = lambda x, t: x[t * part_rows : (t + 1) * part_rows]
    scores = [against(q[:, k].reshape(rows, D), keyed_pairs[k]) for k in several]
    near_scores = [
        jnp.concatenate([against(q[t, k], part(near_pairs[k], t)) for t in range(count)], axis=0) + bias
        for k in several
    ]
    tops = [
        jnp.maximum(
            jnp.max(scores[k], axis=-1, keepdims=True), jnp.max(near_scores[k], axis=-1, keepdims=True)
        )
        for k in several
    ]
    weights = [jnp.exp2((scores[k] - tops[k]) * EXP2_SCALE).astype(jnp.bfloat16) for k in several]
    near_weights = [jnp.exp2((near_scores[k] - tops[k]) * EXP2_SCALE).astype(jnp.bfloat16) for k in several]
    both = [times(weights[k], spread(keyed[k])) for k in several]
    both = [
        both[k]
        + jnp.concatenate(
            [times(near_weights[k][t * TT : (t + 1) * TT], spread(part(near[k], t))) for t in range(count)],
            axis=0,
        )
        for k in several
    ]
    for k in several:
        packed[:, k] = packed_with(both[k], tops[k]).reshape(count, TT, LANES)


def final_kernel(
    place, q, r2, r3, c1, d2, r6, packed, tpos, w_key, w_value, w_o, cot, branch, grad, mixed
):
    frame = place[0]
    y = frame % RING
    step = pl.program_id(0)
    mixed[:, 0] = mix(r2[...], tpos[1:2, :])
    mixed[:, 1] = mix(r3[...], tpos[2:3, :])
    mixed[:, 2] = mix(jnp.where(y == 0, d2[...], c1[...]), tpos[4:5, :])
    mixed[:, 3] = mix(r6[...], tpos[5:6, :])
    part_rows = 4 * PAIRS
    flat = mixed[...].reshape(BLOCK * part_rows, LANES)
    pairs = times(flat, w_key[...]).astype(jnp.bfloat16)
    tiles = range(BLOCK)
    part = lambda x, t: x[t * part_rows : (t + 1) * part_rows]
    scores = jnp.concatenate([against(q[t], part(pairs, t)) for t in tiles], axis=0)
    scores = scores + absent(frame, LATE)
    earlier = packed[...].reshape(BLOCK * TT, LANES)
    earlier_top = earlier[:, MD : MD + 1]
    top = jnp.maximum(jnp.max(scores, axis=-1, keepdims=True), earlier_top)
    weights = jnp.exp2((scores - top) * EXP2_SCALE).astype(jnp.bfloat16)
    both = jnp.concatenate(
        [times(weights[t * TT : (t + 1) * TT], spread(part(flat, t))) for t in tiles], axis=0
    )
    scaled = earlier * jnp.exp2((earlier_top - top) * EXP2_SCALE)
    lane = lax.broadcasted_iota(jnp.int32, earlier.shape, 1)
    summed = both[:, :LANES] + jnp.where(lane < MD, scaled, 0.0)
    summed = summed / (both[:, LANES:] + scaled[:, MD + PAIRS : MD + PAIRS + 1])
    high = summed.astype(jnp.bfloat16)
    low = (summed - high.astype(jnp.float32)).astype(jnp.bfloat16)
    attended = times(jnp.concatenate([high, low], axis=1), w_value[...]).astype(jnp.bfloat16)
    branch[...] = times(attended, w_o[...]).astype(jnp.bfloat16).reshape(branch.shape)
    term = lax.dot_general(
        attended, cot[...].reshape(BLOCK * TT, D), (((0,), (0,)), ((), ())), preferred_element_type=jnp.float32
    )

    @pl.when(step == 0)
    def _():
        grad[...] = term

    @pl.when(step > 0)
    def _():
        grad[...] += term


def per_device(queries, memory, tpos, w_k, w_v, w_o, keyframes, cot):
    place = lax.axis_index("tm")[None]
    devices = lax.axis_size("tm")
    rows = devices // RING
    groups = TILES // CLASSES
    own = memory[0, 0].reshape(TILES, PAIRS, LANES)
    listed = keyframes.reshape(KF)
    in_smem = pl.BlockSpec(memory_space=pltpu.SMEM)
    in_vmem = pl.BlockSpec(memory_space=pltpu.VMEM)

    asks = pl.pallas_call(
        ask_kernel,
        out_shape=jax.ShapeDtypeStruct((devices, LANES), jnp.int32),
        in_specs=[in_smem],
        out_specs=in_vmem,
        name="ask",
    )(listed)
    own, asks = lax.optimization_barrier((own, asks))
    a = routed(own, rows, lambda z, y: (z + 1, y))
    b1 = routed(own, rows, lambda z, y: (z, y + 1) if y < 3 else None)
    y = place[0] % RING
    c1 = routed(a, rows, lambda z, y: (z, (y + 1) % RING))
    r2 = routed(jnp.where(y > 1, a, own), rows, lambda z, y: (z, (y + 2) % RING))
    r3 = routed(jnp.where(y == 0, own, a), rows, lambda z, y: (z, (y - 1) % RING))
    asked = lax.all_to_all(asks, "tm", split_axis=0, concat_axis=0, tiled=True)
    w_key, w_value, tpos_pair = pl.pallas_call(
        weights_kernel,
        out_shape=[
            jax.ShapeDtypeStruct((LANES, 2 * D), jnp.bfloat16),
            jax.ShapeDtypeStruct((2 * LANES, D), jnp.bfloat16),
            jax.ShapeDtypeStruct((7, LANES), jnp.float32),
        ],
        in_specs=[in_vmem] * 3 + [pl.BlockSpec(memory_space=pl.ANY)] * 2,
        out_specs=[in_vmem] * 3,
        name="weights",
    )(w_k, w_v, tpos, a, b1)
    outgoing = pl.pallas_call(
        pick_kernel,
        out_shape=jax.ShapeDtypeStruct((devices * RUN, PAIRS, LANES), jnp.bfloat16),
        in_specs=[in_smem, in_vmem] + [pl.BlockSpec(memory_space=pl.ANY)] * 1,
        out_specs=in_vmem,
        compiler_params=pltpu.CompilerParams(vmem_limit_bytes=56 * MIB),
        name="pick",
    )(asked, own, w_key)
    incoming = lax.all_to_all(outgoing, "tm", split_axis=0, concat_axis=0, tiled=True)
    r6 = routed(r2, rows, lambda z, y: (z + 1, y))
    d2 = routed(c1, rows, lambda z, y: (z + 1, y) if y == 0 else None)
    q_tiles = queries[0, 0].reshape(TILES, TT, D)
    whole = lambda *shape: pl.BlockSpec(shape, lambda i, *_: (0,) * len(shape))
    tile_block = pl.BlockSpec((BLOCK, PAIRS, LANES), lambda i, *_: (i, 0, 0))
    row_block = lambda width: pl.BlockSpec((BLOCK, TT, width), lambda i, *_: (i, 0, 0))
    by_class = lambda x: x.reshape((groups, CLASSES) + x.shape[1:])
    class_block = lambda *tile: pl.BlockSpec((groups, SHARED) + tile, lambda i, *_: (0, i) + (0,) * len(tile))
    packed = pl.pallas_call(
        keyed_kernel,
        grid_spec=pltpu.PrefetchScalarGridSpec(
            num_scalar_prefetch=2,
            grid=(CLASSES // SHARED,),
            in_specs=[class_block(TT, D), whole(devices * RUN, PAIRS, LANES)]
            + [class_block(PAIRS, LANES)] * 3
            + [whole(7, LANES), whole(LANES, 2 * D)],
            out_specs=class_block(TT, LANES),
            scratch_shapes=[
                pltpu.VMEM((SHARED, KSEL, PAIRS, LANES), jnp.bfloat16),
                pltpu.VMEM((SHARED, groups, 2, PAIRS, LANES), jnp.bfloat16),
            ],
        ),
        out_shape=jax.ShapeDtypeStruct((groups, CLASSES, TT, LANES), jnp.float32),
        compiler_params=pltpu.CompilerParams(vmem_limit_bytes=56 * MIB),
        name="keyed",
    )(
        place,
        listed,
        by_class(q_tiles),
        incoming,
        by_class(b1),
        by_class(c1),
        by_class(a),
        tpos_pair,
        w_key,
    )
    branch, grad = pl.pallas_call(
        final_kernel,
        grid_spec=pltpu.PrefetchScalarGridSpec(
            num_scalar_prefetch=1,
            grid=(TILES // BLOCK,),
            in_specs=[row_block(D)]
            + [tile_block] * 5
            + [
                row_block(LANES),
                whole(7, LANES),
                whole(LANES, 2 * D),
                whole(2 * LANES, D),
                whole(D, D),
                row_block(D),
            ],
            out_specs=[row_block(D), whole(D, D)],
            scratch_shapes=[pltpu.VMEM((BLOCK, 4, PAIRS, LANES), jnp.bfloat16)],
        ),
        out_shape=[
            jax.ShapeDtypeStruct((TILES, TT, D), jnp.bfloat16),
            jax.ShapeDtypeStruct((D, D), jnp.float32),
        ],
        compiler_params=pltpu.CompilerParams(vmem_limit_bytes=56 * MIB),
        name="final",
    )(
        place,
        q_tiles,
        r2,
        r3,
        c1,
        d2,
        r6,
        packed.reshape(TILES, TT, LANES),
        tpos_pair,
        w_key,
        w_value,
        w_o,
        cot[0, 0].reshape(TILES, TT, D),
    )

    parts = lax.all_to_all(
        grad.reshape(devices, D // devices, D), "tm", split_axis=0, concat_axis=0, tiled=True
    )
    videos = lax.axis_size("video")
    summed = jnp.sum(parts, axis=0) * (1.0 / math.sqrt(videos * devices * TILES * TT))
    step = 1
    while step < videos:
        summed = summed + lax.ppermute(summed, "video", [(i, i ^ step) for i in range(videos)])
        step *= 2
    return branch.reshape(queries.shape), summed


def solution(mesh):
    in_specs = (
        P("video", "tm", None, None),
        P("video", "tm", None, None),
        P(),
        P(),
        P(),
        P(),
        P("video", "tm", None),
        P("video", "tm", None, None),
    )
    out_specs = (P("video", "tm", None, None), P("tm", None))
    return jax.shard_map(
        per_device, mesh=mesh, in_specs=in_specs, out_specs=out_specs, check_vma=False
    )
```

time: 152 us -> 136 us (0.89)
  blocking collectives: 37.2 us -> 18.2 us
  starting transfers between devices: 32.3 us -> 39.8 us
  Pallas kernels: 35.2 us -> 29.7 us
    all_to_all x1 -> x0, blocking collectives: 18 us -> none  [per_device(): asked = lax.all_to_all(asks, 'tm', split_axis=0, concat_axis=0, tiled=True)]
    all_to_all x0 -> x1, starting transfers between devices: none -> 10.2 us  [per_device(): asked = lax.all_to_all(asks, 'tm', split_axis=0, concat_axis=0, tiled=True)]
    pallas_call x1, Pallas kernels: 22.1 us -> 14.3 us  [per_device(): pl.pallas_call(final_kernel, grid_spec=pltpu.PrefetchScalarGridSpec(num_s...]
    all_to_all x0 -> x1, waiting for transfers between devices: none -> 6.67 us  [per_device(): asked = lax.all_to_all(asks, 'tm', split_axis=0, concat_axis=0, tiled=True)]
    ppermute x10 -> x7, starting transfers between devices: 26.1 us -> 20.8 us  [routed(): return lax.ppermute(shard, 'tm', pairs)]
    ppermute x10 -> x7, waiting for transfers between devices: 32 us -> 26.7 us  [routed(): return lax.ppermute(shard, 'tm', pairs)]
    all_to_all x1, starting transfers between devices: 3.93 us -> 6.48 us  [per_device(): lax.all_to_all(outgoing, 'tm', split_axis=0, concat_axis=0, tiled=True)]
    pallas_call x1 -> x2, Pallas kernels: 9.25 us -> 11.6 us  [the longest x1 10.1 us: per_device(): pl.pallas_call(keyed_kernel, grid_spec=pltpu.PrefetchScalarGridSpec(num_s...]
  transfers between devices with their start and end apart: 14 -> 12, of which waited for: 6 -> 7; matrix products, arithmetic and copies ran while one was open for 1% -> 1% of each run, Pallas kernels for 7% -> 9%
where the time goes in v3:
time: 136 us
  waiting for transfers between devices  41.1 us (30%)
  starting transfers between devices  39.8 us (29%)
  Pallas kernels  29.7 us (22%)
  blocking collectives  18.2 us (13%)
  local copies, waits for them, and re-layouts  4.58 us (3%)
  other arithmetic  1.52 us (1%)
    ppermute x7, waiting for transfers between devices, routed(): return lax.ppermute(shard, 'tm', pairs)  26.7 us
    ppermute x7, starting transfers between devices, routed(): return lax.ppermute(shard, 'tm', pairs)  20.8 us
    all_to_all x1, blocking collectives, per_device(): lax.all_to_all(grad.reshape(devices, D // devices, D), 'tm', split_axis=0...  18.2 us
    pallas_call x1, Pallas kernels, per_device(): pl.pallas_call(final_kernel, grid_spec=pltpu.PrefetchScalarGridSpec(num_s...  14.3 us
    all_to_all x1, starting transfers between devices, per_device(): asked = lax.all_to_all(asks, 'tm', split_axis=0, concat_axis=0, tiled=True)  10.2 us
    pallas_call x1, Pallas kernels, per_device(): pl.pallas_call(keyed_kernel, grid_spec=pltpu.PrefetchScalarGridSpec(num_s...  10.1 us
    ppermute x3, waiting for transfers between devices, per_device(): lax.ppermute(summed, 'video', [(i, i ^ step) for i in range(videos)])  7.72 us
    all_to_all x1, waiting for transfers between devices, per_device(): asked = lax.all_to_all(asks, 'tm', split_axis=0, concat_axis=0, tiled=True)  6.67 us
  transfers between devices with their start and end apart: 12, of which 7 were waited for; matrix products, arithmetic and copies ran while one was open for 1% of the time, Pallas kernels for 9%

profile of v3, /device:TPU:6, one launch (start us, length us, event | category | flops | bytes accessed | tf_op | source)
XLA Modules:
  0.0 135.7 jit_solution(16695937081108452648)
XLA Ops:
  0.6 1.5 %ask.1 = s32[32,128]{1,0:T(8,128)} custom-call(s32[64]{0:T(128)} %bitcast.34), custom_call_target="tpu_custom_call" | custom-call | tf_op jit(solution)/shard_map/ask/pallas_call | solution.py:212
  2.1 1.1 copy.11
  3.3 0.0 copy-start.2
  3.3 3.5 %collective-permute-start.6 = (bf16[64,32,128]{2,1,0:T(8,128)(2,1)S(1)}, bf16[64,32,128]{2,1,0:T(8,128)(2,1)S(1)}, u32[]{:S(2)}, u32[]{:S(2)}) collective-permute-start(bf16[64,32,128]{2,1,0:T(8,128)(2,1)S(1)} %bitcast.23), channel_id=1, source_target_pairs={{0,1},{1,2},{2,3},{4,5},{5,6},{6,7},{8,9},{9,10},{10,11},{12,13},{... | collective-permute-start | bytes 1572872 | tf_op jit(solution)/shard_map/ppermute | solution.py:37
  6.8 3.9 %collective-permute-start = (bf16[64,32,128]{2,1,0:T(8,128)(2,1)S(1)}, bf16[64,32,128]{2,1,0:T(8,128)(2,1)S(1)}, u32[]{:S(2)}, u32[]{:S(2)}) collective-permute-start(bf16[64,32,128]{2,1,0:T(8,128)(2,1)S(1)} %bitcast.24), channel_id=1, source_target_pairs={{0,4},{1,5},{2,6},{3,7},{4,8},{5,9},{6,10},{7,11},{8,12},{9,13},{1... | collective-permute-start | bytes 1572872 | tf_op jit(solution)/shard_map/ppermute | solution.py:37
  10.7 10.2 %all-to-all-start = ((s32[32,1,128]{2,1,0:T(1,128)}), s32[32,1,128]{2,1,0:T(1,128)S(1)}, u32[]{:S(2)}, u32[]{:S(2)}) async-start(s32[32,1,128]{2,1,0:T(1,128)} %bitcast.33), calls=%async_computation | async-start | bytes 32768 | tf_op jit(solution)/shard_map/all_to_all | solution.py:226
  20.9 0.0 collective-permute-done.6.rest_1_
  20.9 0.0 copy-start.6
  20.9 0.7 collective-permute-done.rest_0_
  21.6 0.1 copy-done.6
  21.7 0.0 copy-start
  21.7 0.8 copy-done
  22.5 1.5 %weights.1 = (bf16[128,512]{1,0:T(8,128)(2,1)}, bf16[256,256]{1,0:T(8,128)(2,1)}, f32[7,128]{1,0:T(8,128)}) custom-call(bf16[64,256]{1,0:T(8,128)(2,1)} %w_k.1, bf16[64,256]{1,0:T(8,128)(2,1)} %w_v.1, f32[7,64]{1,0:T(8,128)} %tpos.1, bf16[64,32,128]{2,1,0:T(8,128)(2,1)} %copy-done, bf16[64,32,128]{2,1,0:T(8,128)(2,1)} %copy-done.6), custom_call_target="tpu_custom_call" | custom-call | tf_op jit(solution)/shard_map/weights/pallas_call | solution.py:227
  24.0 6.7 %all-to-all-done = s32[32,1,128]{2,1,0:T(1,128)S(1)} async-done(((s32[32,1,128]{2,1,0:T(1,128)}), s32[32,1,128]{2,1,0:T(1,128)S(1)}, u32[]{:S(2)}, u32[]{:S(2)}) %all-to-all-start) | async-done | bytes 16416 | tf_op jit(solution)/shard_map/all_to_all | solution.py:226
  30.7 0.0 copy-done.2
  30.7 0.6 copy-done.10
  31.3 2.3 %pick.1 = bf16[128,32,128]{2,1,0:T(8,128)(2,1)} custom-call(s32[32,128]{1,0:T(8,128)} %bitcast.32, bf16[64,32,128]{2,1,0:T(8,128)(2,1)} %bitcast.25, bf16[128,512]{1,0:T(8,128)(2,1)} %get-tuple-element.11.rest_0_.w_key), custom_call_target="tpu_custom_call" | custom-call | tf_op jit(solution)/shard_map/pick/pallas_call | solution.py:238
  33.6 6.5 %all-to-all-start.1 = ((bf16[128,32,128]{2,1,0:T(8,128)(2,1)}), bf16[128,32,128]{2,1,0:T(8,128)(2,1)S(1)}, u32[]{:S(2)}, u32[]{:S(2)}) async-start(bf16[128,32,128]{2,1,0:T(8,128)(2,1)} %pick.1), calls=%async_computation.1 | async-start | bytes 2097152 | tf_op jit(solution)/shard_map/all_to_all | solution.py:246
  40.1 0.0 copy-done.1
  40.1 1.9 %collective-permute-start.3 = (bf16[64,32,128]{2,1,0:T(8,128)(2,1)S(1)}, bf16[64,32,128]{2,1,0:T(8,128)(2,1)S(1)}, u32[]{:S(2)}, u32[]{:S(2)}) collective-permute-start(bf16[64,32,128]{2,1,0:T(8,128)(2,1)S(1)} %copy-done.1), channel_id=1, source_target_pairs={{0,1},{1,2},{2,3},{3,0},{4,5},{5,6},{6,7},{7,4},{8,9},{9,10},{10,1... | collective-permute-start | bytes 1572872 | tf_op jit(solution)/shard_map/ppermute | solution.py:37
  42.0 0.0 copy-done.3
  42.0 0.9 broadcast_select_fusion
  42.9 2.7 %collective-permute-start.1 = (bf16[64,32,128]{2,1,0:T(8,128)(2,1)S(1)}, bf16[64,32,128]{2,1,0:T(8,128)(2,1)S(1)}, u32[]{:S(2)}, u32[]{:S(2)}) collective-permute-start(bf16[64,32,128]{2,1,0:T(8,128)(2,1)S(1)} %get-tuple-element.17), channel_id=1, source_target_pairs={{0,2},{1,3},{2,0},{3,1},{4,6},{5,7},{6,4},{7,5},{8,10},{9,11},{10,... | collective-permute-start | bytes 1572872 | tf_op jit(solution)/shard_map/ppermute | solution.py:37
  45.5 1.5 %collective-permute-start.2 = (bf16[64,32,128]{2,1,0:T(8,128)(2,1)}, bf16[64,32,128]{2,1,0:T(8,128)(2,1)S(1)}, u32[]{:S(2)}, u32[]{:S(2)}) collective-permute-start(bf16[64,32,128]{2,1,0:T(8,128)(2,1)} %get-tuple-element.16), channel_id=1, source_target_pairs={{0,3},{1,0},{2,1},{3,2},{4,7},{5,4},{6,5},{7,6},{8,11},{9,8},{10,9... | collective-permute-start | bytes 1572872 | tf_op jit(solution)/shard_map/ppermute | solution.py:37
  47.0 18.7 %collective-permute-done.3.c1 = bf16[64,32,128]{2,1,0:T(8,128)(2,1)S(1)} collective-permute-done((bf16[64,32,128]{2,1,0:T(8,128)(2,1)S(1)}, bf16[64,32,128]{2,1,0:T(8,128)(2,1)S(1)}, u32[]{:S(2)}, u32[]{:S(2)}) %collective-permute-start.3) | collective-permute-done | bytes 524320 | tf_op jit(solution)/shard_map/ppermute | solution.py:37
  65.7 3.2 %collective-permute-start.4 = (bf16[64,32,128]{2,1,0:T(8,128)(2,1)S(1)}, bf16[64,32,128]{2,1,0:T(8,128)(2,1)S(1)}, u32[]{:S(2)}, u32[]{:S(2)}) collective-permute-start(bf16[64,32,128]{2,1,0:T(8,128)(2,1)S(1)} %collective-permute-done.3.c1), channel_id=1, source_target_pairs={{0,4},{4,8},{8,12},{12,16},{16,20},{20,24},{24,28},{32,36},{36,40}... | collective-permute-start | bytes 1572872 | tf_op jit(solution)/shard_map/ppermute | solution.py:37
  69.0 7.3 %collective-permute-done.1.r2 = bf16[64,32,128]{2,1,0:T(8,128)(2,1)S(1)} collective-permute-done((bf16[64,32,128]{2,1,0:T(8,128)(2,1)S(1)}, bf16[64,32,128]{2,1,0:T(8,128)(2,1)S(1)}, u32[]{:S(2)}, u32[]{:S(2)}) %collective-permute-start.1) | collective-permute-done | bytes 524320 | tf_op jit(solution)/shard_map/ppermute | solution.py:37
  76.3 4.1 %collective-permute-start.5 = (bf16[64,32,128]{2,1,0:T(8,128)(2,1)S(1)}, bf16[64,32,128]{2,1,0:T(8,128)(2,1)}, u32[]{:S(2)}, u32[]{:S(2)}) collective-permute-start(bf16[64,32,128]{2,1,0:T(8,128)(2,1)S(1)} %collective-permute-done.1.r2), channel_id=1, source_target_pairs={{0,4},{1,5},{2,6},{3,7},{4,8},{5,9},{6,10},{7,11},{8,12},{9,13},{1... | collective-permute-start | bytes 1572872 | tf_op jit(solution)/shard_map/ppermute | solution.py:37
  80.4 0.0 all-to-all-done.1.incoming
  80.4 0.0 copy-done.5
  80.4 1.0 copy-done.4
  81.4 10.1 %keyed.1 = f32[8,8,64,128]{3,2,1,0:T(8,128)} custom-call(s32[1]{0:T(128)} %bitcast.place, s32[64]{0:T(128)} %bitcast.35, bf16[8,8,64,256]{3,2,1,0:T(8,128)(2,1)} %bitcast.19, bf16[128,32,128]{2,1,0:T(8,128)(2,1)} %copy-done.4, bf16[8,8,32,128]{3,2,1,0:T(8,128)(2,1)} %bitcast.28, bf16[8,8,32,128]{3,2,1,0:T(8,128)(2,1)} %bitcast.27, ...), custom_call_target="tpu_custom_call" | custom-call | tf_op jit(solution)/shard_map/keyed/pallas_call | solution.py:255
  91.5 0.0 collective-permute-done.2.r3
  91.5 0.0 collective-permute-done.4.d2
  91.5 0.0 copy-start.9
  91.5 0.0 collective-permute-done.5.r6
  91.5 0.0 copy-done.7
  91.5 0.7 copy-done.8
  92.3 0.2 copy-done.9
  92.4 14.3 %final.1 = (bf16[64,64,256]{2,1,0:T(8,128)(2,1)}, f32[256,256]{1,0:T(8,128)}) custom-call(s32[1]{0:T(128)} %bitcast.place, bf16[64,64,256]{2,1,0:T(8,128)(2,1)} %bitcast.20, bf16[64,32,128]{2,1,0:T(8,128)(2,1)} %copy-done.7, bf16[64,32,128]{2,1,0:T(8,128)(2,1)} %copy-done.8, bf16[64,32,128]{2,1,0:T(8,128)(2,1)} %copy-done.5, bf16[64,32,128]{2,1,0:T(8,128)(2,1)} %copy-done.9, ...), custom_call_target="tpu_custom_call" | custom-call | tf_op jit(solution)/shard_map/final/pallas_call | solution.py:283
  106.7 18.2 %all_to_all.21 = f32[32,8,256]{2,1,0:T(8,128)S(1)} all-to-all(f32[32,8,256]{2,1,0:T(8,128)} %bitcast.31), channel_id=1, replica_groups=mesh['video'=8,'tm'=32] {'tm'}, dimensions={0} | all-to-all | bytes 524288 | tf_op jit(solution)/shard_map/all_to_all | solution.py:323
  125.0 0.1 collective-permute-start.7
  125.1 1.2 collective-permute-done.7
  126.3 0.8 collective-permute-start.8
  127.1 2.8 %collective-permute-done.8 = f32[8,256]{1,0:T(8,128)S(1)} collective-permute-done((f32[8,256]{1,0:T(8,128)S(1)}, f32[8,256]{1,0:T(8,128)S(1)}, u32[]{:S(2)}, u32[]{:S(2)}) %collective-permute-start.8) | collective-permute-done | bytes 8224 | tf_op jit(solution)/shard_map/ppermute | solution.py:330
  129.9 1.4 %collective-permute-start.9 = (f32[8,256]{1,0:T(8,128)S(1)}, f32[8,256]{1,0:T(8,128)S(1)}, u32[]{:S(2)}, u32[]{:S(2)}) collective-permute-start(f32[8,256]{1,0:T(8,128)S(1)} %add.15), channel_id=1, source_target_pairs={{0,128},{32,160},{64,192},{96,224},{128,0},{160,32},{192,64},{224,... | collective-permute-start | bytes 24584 | tf_op jit(solution)/shard_map/ppermute | solution.py:330
  131.3 3.7 %collective-permute-done.9 = f32[8,256]{1,0:T(8,128)S(1)} collective-permute-done((f32[8,256]{1,0:T(8,128)S(1)}, f32[8,256]{1,0:T(8,128)S(1)}, u32[]{:S(2)}, u32[]{:S(2)}) %collective-permute-start.9) | collective-permute-done | bytes 8224 | tf_op jit(solution)/shard_map/ppermute | solution.py:330
  135.1 0.6 add.16
  (11 shorter events, 0.1 us)
Async XLA Ops:
  3.3 27.4 %copy-start.2 = (bf16[8,8,32,128]{3,2,1,0:T(8,128)(2,1)}, bf16[8,8,32,128]{3,2,1,0:T(8,128)(2,1)S(1)}, u32[]{:S(2)}) copy-start(bf16[8,8,32,128]{3,2,1,0:T(8,128)(2,1)S(1)} %copy.11) | copy-start | bytes 1572868
  3.3 17.6 %collective-permute-start.6 = (bf16[64,32,128]{2,1,0:T(8,128)(2,1)S(1)}, bf16[64,32,128]{2,1,0:T(8,128)(2,1)S(1)}, u32[]{:S(2)}, u32[]{:S(2)}) collective-permute-start(bf16[64,32,128]{2,1,0:T(8,128)(2,1)S(1)} %bitcast.23), channel_id=1, source_target_pairs={{0,1},{1,2},{2,3},{4,5},{5,6},{6,7},{8,9},{9,10},{10,11},{12,13},{... | collective-permute-start | bytes 1572872 | tf_op jit(solution)/shard_map/ppermute | solution.py:37
  6.8 14.8 %collective-permute-start = (bf16[64,32,128]{2,1,0:T(8,128)(2,1)S(1)}, bf16[64,32,128]{2,1,0:T(8,128)(2,1)S(1)}, u32[]{:S(2)}, u32[]{:S(2)}) collective-permute-start(bf16[64,32,128]{2,1,0:T(8,128)(2,1)S(1)} %bitcast.24), channel_id=1, source_target_pairs={{0,4},{1,5},{2,6},{3,7},{4,8},{5,9},{6,10},{7,11},{8,12},{9,13},{1... | collective-permute-start | bytes 1572872 | tf_op jit(solution)/shard_map/ppermute | solution.py:37
  10.7 20.0 %all-to-all-start = ((s32[32,1,128]{2,1,0:T(1,128)}), s32[32,1,128]{2,1,0:T(1,128)S(1)}, u32[]{:S(2)}, u32[]{:S(2)}) async-start(s32[32,1,128]{2,1,0:T(1,128)} %bitcast.33), calls=%async_computation | async-start | bytes 32768 | tf_op jit(solution)/shard_map/all_to_all | solution.py:226
  20.9 0.8 copy-start.6
  21.7 0.8 copy-start
  24.0 16.1 %copy-start.1 = (bf16[64,32,128]{2,1,0:T(8,128)(2,1)S(1)}, bf16[64,32,128]{2,1,0:T(8,128)(2,1)}, u32[]{:S(2)}) copy-start(bf16[64,32,128]{2,1,0:T(8,128)(2,1)} %copy-done) | copy-start | bytes 1572868
  30.7 0.6 copy-start.10
  33.6 8.4 %copy-start.3 = (bf16[8,8,32,128]{3,2,1,0:T(8,128)(2,1)S(1)}, bf16[8,8,32,128]{3,2,1,0:T(8,128)(2,1)}, u32[]{:S(2)}) copy-start(bf16[8,8,32,128]{3,2,1,0:T(8,128)(2,1)} %copy-done.2) | copy-start | bytes 1572868
  33.6 46.8 %all-to-all-start.1 = ((bf16[128,32,128]{2,1,0:T(8,128)(2,1)}), bf16[128,32,128]{2,1,0:T(8,128)(2,1)S(1)}, u32[]{:S(2)}, u32[]{:S(2)}) async-start(bf16[128,32,128]{2,1,0:T(8,128)(2,1)} %pick.1), calls=%async_computation.1 | async-start | bytes 2097152 | tf_op jit(solution)/shard_map/all_to_all | solution.py:246
  40.1 25.6 %collective-permute-start.3 = (bf16[64,32,128]{2,1,0:T(8,128)(2,1)S(1)}, bf16[64,32,128]{2,1,0:T(8,128)(2,1)S(1)}, u32[]{:S(2)}, u32[]{:S(2)}) collective-permute-start(bf16[64,32,128]{2,1,0:T(8,128)(2,1)S(1)} %copy-done.1), channel_id=1, source_target_pairs={{0,1},{1,2},{2,3},{3,0},{4,5},{5,6},{6,7},{7,4},{8,9},{9,10},{10,1... | collective-permute-start | bytes 1572872 | tf_op jit(solution)/shard_map/ppermute | solution.py:37
  42.9 33.4 %collective-permute-start.1 = (bf16[64,32,128]{2,1,0:T(8,128)(2,1)S(1)}, bf16[64,32,128]{2,1,0:T(8,128)(2,1)S(1)}, u32[]{:S(2)}, u32[]{:S(2)}) collective-permute-start(bf16[64,32,128]{2,1,0:T(8,128)(2,1)S(1)} %get-tuple-element.17), channel_id=1, source_target_pairs={{0,2},{1,3},{2,0},{3,1},{4,6},{5,7},{6,4},{7,5},{8,10},{9,11},{10,... | collective-permute-start | bytes 1572872 | tf_op jit(solution)/shard_map/ppermute | solution.py:37
  45.5 45.9 %collective-permute-start.2 = (bf16[64,32,128]{2,1,0:T(8,128)(2,1)}, bf16[64,32,128]{2,1,0:T(8,128)(2,1)S(1)}, u32[]{:S(2)}, u32[]{:S(2)}) collective-permute-start(bf16[64,32,128]{2,1,0:T(8,128)(2,1)} %get-tuple-element.16), channel_id=1, source_target_pairs={{0,3},{1,0},{2,1},{3,2},{4,7},{5,4},{6,5},{7,6},{8,11},{9,8},{10,9... | collective-permute-start | bytes 1572872 | tf_op jit(solution)/shard_map/ppermute | solution.py:37
  65.7 14.7 %copy-start.5 = (bf16[64,32,128]{2,1,0:T(8,128)(2,1)}, bf16[64,32,128]{2,1,0:T(8,128)(2,1)S(1)}, u32[]{:S(2)}) copy-start(bf16[64,32,128]{2,1,0:T(8,128)(2,1)S(1)} %collective-permute-done.3.c1) | copy-start | bytes 1572868
  65.7 25.8 %collective-permute-start.4 = (bf16[64,32,128]{2,1,0:T(8,128)(2,1)S(1)}, bf16[64,32,128]{2,1,0:T(8,128)(2,1)S(1)}, u32[]{:S(2)}, u32[]{:S(2)}) collective-permute-start(bf16[64,32,128]{2,1,0:T(8,128)(2,1)S(1)} %collective-permute-done.3.c1), channel_id=1, source_target_pairs={{0,4},{4,8},{8,12},{12,16},{16,20},{20,24},{24,28},{32,36},{36,40}... | collective-permute-start | bytes 1572872 | tf_op jit(solution)/shard_map/ppermute | solution.py:37
  76.3 15.2 %copy-start.7 = (bf16[64,32,128]{2,1,0:T(8,128)(2,1)}, bf16[64,32,128]{2,1,0:T(8,128)(2,1)S(1)}, u32[]{:S(2)}) copy-start(bf16[64,32,128]{2,1,0:T(8,128)(2,1)S(1)} %collective-permute-done.1.r2) | copy-start | bytes 1572868
  76.3 15.2 %collective-permute-start.5 = (bf16[64,32,128]{2,1,0:T(8,128)(2,1)S(1)}, bf16[64,32,128]{2,1,0:T(8,128)(2,1)}, u32[]{:S(2)}, u32[]{:S(2)}) collective-permute-start(bf16[64,32,128]{2,1,0:T(8,128)(2,1)S(1)} %collective-permute-done.1.r2), channel_id=1, source_target_pairs={{0,4},{1,5},{2,6},{3,7},{4,8},{5,9},{6,10},{7,11},{8,12},{9,13},{1... | collective-permute-start | bytes 1572872 | tf_op jit(solution)/shard_map/ppermute | solution.py:37
  80.4 1.0 copy-start.4
  91.5 0.8 copy-start.8
  91.5 1.0 copy-start.9
  125.0 1.3 collective-permute-start.7
  126.3 3.7 %collective-permute-start.8 = (f32[8,256]{1,0:T(8,128)S(1)}, f32[8,256]{1,0:T(8,128)S(1)}, u32[]{:S(2)}, u32[]{:S(2)}) collective-permute-start(f32[8,256]{1,0:T(8,128)S(1)} %fusion), channel_id=1, source_target_pairs={{0,64},{32,96},{64,0},{96,32},{128,192},{160,224},{192,128},{224,1... | collective-permute-start | bytes 24584 | tf_op jit(solution)/shard_map/ppermute | solution.py:330
  129.9 5.2 %collective-permute-start.9 = (f32[8,256]{1,0:T(8,128)S(1)}, f32[8,256]{1,0:T(8,128)S(1)}, u32[]{:S(2)}, u32[]{:S(2)}) collective-permute-start(f32[8,256]{1,0:T(8,128)S(1)} %add.15), channel_id=1, source_target_pairs={{0,128},{32,160},{64,192},{96,224},{128,0},{160,32},{192,64},{224,... | collective-permute-start | bytes 24584 | tf_op jit(solution)/shard_map/ppermute | solution.py:330

commit v4 on v3

--- a/solution.py
+++ b/solution.py
@@ -221,8 +221,10 @@
     b1 = routed(own, rows, lambda z, y: (z, y + 1) if y < 3 else None)
     y = place[0] % RING
     c1 = routed(a, rows, lambda z, y: (z, (y + 1) % RING))
-    r2 = routed(jnp.where(y > 1, a, own), rows, lambda z, y: (z, (y + 2) % RING))
-    r3 = routed(jnp.where(y == 0, own, a), rows, lambda z, y: (z, (y - 1) % RING))
+    x2 = jnp.where(y > 1, a, own)
+    r2 = routed(x2, rows, lambda z, y: (z, (y + 2) % RING))
+    x3 = jnp.where(y == 0, own, a)
+    r3 = routed(x3, rows, lambda z, y: (z, (y - 1) % RING))
     asked = lax.all_to_all(asks, "tm", split_axis=0, concat_axis=0, tiled=True)
     w_key, w_value, tpos_pair = pl.pallas_call(
         weights_kernel,
@@ -231,18 +233,18 @@
             jax.ShapeDtypeStruct((2 * LANES, D), jnp.bfloat16),
             jax.ShapeDtypeStruct((7, LANES), jnp.float32),
         ],
-        in_specs=[in_vmem] * 3 + [pl.BlockSpec(memory_space=pl.ANY)] * 2,
+        in_specs=[in_vmem] * 3 + [pl.BlockSpec(memory_space=pl.ANY)] * 0,
         out_specs=[in_vmem] * 3,
         name="weights",
-    )(w_k, w_v, tpos, a, b1)
+    )(w_k, w_v, tpos)
     outgoing = pl.pallas_call(
         pick_kernel,
         out_shape=jax.ShapeDtypeStruct((devices * RUN, PAIRS, LANES), jnp.bfloat16),
-        in_specs=[in_smem, in_vmem] + [pl.BlockSpec(memory_space=pl.ANY)] * 1,
+        in_specs=[in_smem, in_vmem] + [pl.BlockSpec(memory_space=pl.ANY)] * 2,
         out_specs=in_vmem,
-        compiler_params=pltpu.CompilerParams(vmem_limit_bytes=56 * MIB),
+        compiler_params=pltpu.CompilerParams(vmem_limit_bytes=60 * MIB),
         name="pick",
-    )(asked, own, w_key)
+    )(asked, own, x2, b1)
     incoming = lax.all_to_all(outgoing, "tm", split_axis=0, concat_axis=0, tiled=True)
     r6 = routed(r2, rows, lambda z, y: (z + 1, y))
     d2 = routed(c1, rows, lambda z, y: (z + 1, y) if y == 0 else None)
@@ -267,7 +269,7 @@
             ],
         ),
         out_shape=jax.ShapeDtypeStruct((groups, CLASSES, TT, LANES), jnp.float32),
-        compiler_params=pltpu.CompilerParams(vmem_limit_bytes=56 * MIB),
+        compiler_params=pltpu.CompilerParams(vmem_limit_bytes=60 * MIB),
         name="keyed",
     )(
         place,
@@ -302,7 +304,7 @@
             jax.ShapeDtypeStruct((TILES, TT, D), jnp.bfloat16),
             jax.ShapeDtypeStruct((D, D), jnp.float32),
         ],
-        compiler_params=pltpu.CompilerParams(vmem_limit_bytes=56 * MIB),
+        compiler_params=pltpu.CompilerParams(vmem_limit_bytes=60 * MIB),
         name="final",
     )(
         place,
@@ -325,10 +327,12 @@
     )
     videos = lax.axis_size("video")
     summed = jnp.sum(parts, axis=0) * (1.0 / math.sqrt(videos * devices * TILES * TT))
-    step = 1
-    while step < videos:
-        summed = summed + lax.ppermute(summed, "video", [(i, i ^ step) for i in range(videos)])
-        step *= 2
+    summed = summed + lax.ppermute(summed, "video", [(i, i ^ 1) for i in range(videos)])
+    others = [
+        lax.ppermute(summed, "video", [(i, (i + chip) % videos) for i in range(videos)])
+        for chip in range(2, videos, 2)
+    ]
+    summed = (summed + others[1]) + (others[0] + others[2])
     return branch.reshape(queries.shape), summed
 
 

time: 136 us -> 133 us (0.978)
  starting transfers between devices: 39.8 us -> 37.5 us
    all_to_all x1, starting transfers between devices: 6.48 us -> 3.93 us  [per_device(): lax.all_to_all(outgoing, 'tm', split_axis=0, concat_axis=0, tiled=True)]
    all_to_all x1, waiting for transfers between devices: 6.67 us -> 8.5 us  [per_device(): asked = lax.all_to_all(asks, 'tm', split_axis=0, concat_axis=0, tiled=True)]
    ppermute x3 -> x4, waiting for transfers between devices: 7.72 us -> 6.2 us  [the longest x3 5.04 us: per_device(): lax.ppermute(summed, 'video', [(i, (i + chip) % videos) for i in range(vi...]
    ppermute x3 -> x4, starting transfers between devices: 2.33 us -> 3.44 us  [the longest x3 3.35 us: per_device(): lax.ppermute(summed, 'video', [(i, (i + chip) % videos) for i in range(vi...]
    unnamed x23 -> x21, local copies, waits for them, and re-layouts: 4.58 us -> 3.87 us
  transfers between devices with their start and end apart: 12 -> 13, of which waited for: 7 -> 6; matrix products, arithmetic and copies ran while one was open for 1% -> 1% of each run, Pallas kernels for 9% -> 9%
where the time goes in v4:
time: 133 us
  waiting for transfers between devices  41.2 us (31%)
  starting transfers between devices  37.5 us (28%)
  Pallas kernels  29.7 us (22%)
  blocking collectives  17.8 us (13%)
  local copies, waits for them, and re-layouts  3.87 us (3%)
  other arithmetic  1.77 us (1%)
    ppermute x7, waiting for transfers between devices, routed(): return lax.ppermute(shard, 'tm', pairs)  26.5 us
    ppermute x7, starting transfers between devices, routed(): return lax.ppermute(shard, 'tm', pairs)  19.8 us
    all_to_all x1, blocking collectives, per_device(): lax.all_to_all(grad.reshape(devices, D // devices, D), 'tm', split_axis=0...  17.8 us
    pallas_call x1, Pallas kernels, per_device(): pl.pallas_call(final_kernel, grid_spec=pltpu.PrefetchScalarGridSpec(num_s...  14.3 us
    all_to_all x1, starting transfers between devices, per_device(): asked = lax.all_to_all(asks, 'tm', split_axis=0, concat_axis=0, tiled=True)  10.2 us
    pallas_call x1, Pallas kernels, per_device(): pl.pallas_call(keyed_kernel, grid_spec=pltpu.PrefetchScalarGridSpec(num_s...  10.1 us
    all_to_all x1, waiting for transfers between devices, per_device(): asked = lax.all_to_all(asks, 'tm', split_axis=0, concat_axis=0, tiled=True)  8.5 us
    ppermute x3, waiting for transfers between devices, per_device(): lax.ppermute(summed, 'video', [(i, (i + chip) % videos) for i in range(vi...  5.04 us
  transfers between devices with their start and end apart: 13, of which 6 were waited for; matrix products, arithmetic and copies ran while one was open for 1% of the time, Pallas kernels for 9%

profile of v4, /device:TPU:6, one launch (start us, length us, event | category | flops | bytes accessed | tf_op | source)
XLA Modules:
  0.0 132.7 jit_solution(1281183338485983830)
XLA Ops:
  0.6 1.5 %ask.1 = s32[32,128]{1,0:T(8,128)} custom-call(s32[64]{0:T(128)} %bitcast.34), custom_call_target="tpu_custom_call" | custom-call | tf_op jit(solution)/shard_map/ask/pallas_call | solution.py:212
  2.1 1.1 copy.11
  3.3 0.0 copy-start
  3.3 3.9 %collective-permute-start = (bf16[64,32,128]{2,1,0:T(8,128)(2,1)S(1)}, bf16[64,32,128]{2,1,0:T(8,128)(2,1)S(1)}, u32[]{:S(2)}, u32[]{:S(2)}) collective-permute-start(bf16[64,32,128]{2,1,0:T(8,128)(2,1)S(1)} %bitcast.22), channel_id=1, source_target_pairs={{0,4},{1,5},{2,6},{3,7},{4,8},{5,9},{6,10},{7,11},{8,12},{9,13},{1... | collective-permute-start | bytes 1572872 | tf_op jit(solution)/shard_map/ppermute | solution.py:37
  7.1 3.5 %collective-permute-start.6 = (bf16[64,32,128]{2,1,0:T(8,128)(2,1)S(1)}, bf16[64,32,128]{2,1,0:T(8,128)(2,1)S(1)}, u32[]{:S(2)}, u32[]{:S(2)}) collective-permute-start(bf16[64,32,128]{2,1,0:T(8,128)(2,1)S(1)} %bitcast.23), channel_id=1, source_target_pairs={{0,1},{1,2},{2,3},{4,5},{5,6},{6,7},{8,9},{9,10},{10,11},{12,13},{... | collective-permute-start | bytes 1572872 | tf_op jit(solution)/shard_map/ppermute | solution.py:37
  10.7 10.2 %all-to-all-start = ((s32[32,1,128]{2,1,0:T(1,128)}), s32[32,1,128]{2,1,0:T(1,128)S(1)}, u32[]{:S(2)}, u32[]{:S(2)}) async-start(s32[32,1,128]{2,1,0:T(1,128)} %bitcast.33), calls=%async_computation | async-start | bytes 32768 | tf_op jit(solution)/shard_map/all_to_all | solution.py:228
  20.9 0.0 collective-permute-done
  20.9 0.0 copy-start.4
  20.9 1.1 broadcast_select_fusion
  22.1 8.5 %all-to-all-done = s32[32,1,128]{2,1,0:T(1,128)S(1)} async-done(((s32[32,1,128]{2,1,0:T(1,128)}), s32[32,1,128]{2,1,0:T(1,128)S(1)}, u32[]{:S(2)}, u32[]{:S(2)}) %all-to-all-start) | async-done | bytes 16416 | tf_op jit(solution)/shard_map/all_to_all | solution.py:228
  30.6 0.0 collective-permute-done.6.rest_1_
  30.6 0.0 copy-done
  30.6 0.6 copy-done.9
  31.2 0.2 copy-done.2
  31.4 2.4 %pick.1 = bf16[128,32,128]{2,1,0:T(8,128)(2,1)} custom-call(s32[32,128]{1,0:T(8,128)} %bitcast.32, bf16[64,32,128]{2,1,0:T(8,128)(2,1)} %bitcast.25, bf16[64,32,128]{2,1,0:T(8,128)(2,1)} %get-tuple-element.17.rest_0_, bf16[64,32,128]{2,1,0:T(8,128)(2,1)} %copy-done.2), custom_call_target="tpu_custom_call" | custom-call | tf_op jit(solution)/shard_map/pick/pallas_call | solution.py:240
  33.8 3.9 %all-to-all-start.1 = ((bf16[128,32,128]{2,1,0:T(8,128)(2,1)}), bf16[128,32,128]{2,1,0:T(8,128)(2,1)S(1)}, u32[]{:S(2)}, u32[]{:S(2)}) async-start(bf16[128,32,128]{2,1,0:T(8,128)(2,1)} %pick.1), calls=%async_computation.1 | async-start | bytes 2097152 | tf_op jit(solution)/shard_map/all_to_all | solution.py:248
  37.7 0.0 copy-done.4
  37.7 1.8 %collective-permute-start.3 = (bf16[64,32,128]{2,1,0:T(8,128)(2,1)S(1)}, bf16[64,32,128]{2,1,0:T(8,128)(2,1)S(1)}, u32[]{:S(2)}, u32[]{:S(2)}) collective-permute-start(bf16[64,32,128]{2,1,0:T(8,128)(2,1)S(1)} %collective-permute-done), channel_id=1, source_target_pairs={{0,1},{1,2},{2,3},{3,0},{4,5},{5,6},{6,7},{7,4},{8,9},{9,10},{10,1... | collective-permute-start | bytes 1572872 | tf_op jit(solution)/shard_map/ppermute | solution.py:37
  39.5 0.0 copy-done.5
  39.5 2.7 %collective-permute-start.1 = (bf16[64,32,128]{2,1,0:T(8,128)(2,1)S(1)}, bf16[64,32,128]{2,1,0:T(8,128)(2,1)S(1)}, u32[]{:S(2)}, u32[]{:S(2)}) collective-permute-start(bf16[64,32,128]{2,1,0:T(8,128)(2,1)S(1)} %copy-done.5), channel_id=1, source_target_pairs={{0,2},{1,3},{2,0},{3,1},{4,6},{5,7},{6,4},{7,5},{8,10},{9,11},{10,... | collective-permute-start | bytes 1572872 | tf_op jit(solution)/shard_map/ppermute | solution.py:37
  42.2 1.5 %collective-permute-start.2 = (bf16[64,32,128]{2,1,0:T(8,128)(2,1)}, bf16[64,32,128]{2,1,0:T(8,128)(2,1)}, u32[]{:S(2)}, u32[]{:S(2)}) collective-permute-start(bf16[64,32,128]{2,1,0:T(8,128)(2,1)} %get-tuple-element.16), channel_id=1, source_target_pairs={{0,3},{1,0},{2,1},{3,2},{4,7},{5,4},{6,5},{7,6},{8,11},{9,8},{10,9... | collective-permute-start | bytes 1572872 | tf_op jit(solution)/shard_map/ppermute | solution.py:37
  43.6 19.4 %collective-permute-done.3.c1 = bf16[64,32,128]{2,1,0:T(8,128)(2,1)S(1)} collective-permute-done((bf16[64,32,128]{2,1,0:T(8,128)(2,1)S(1)}, bf16[64,32,128]{2,1,0:T(8,128)(2,1)S(1)}, u32[]{:S(2)}, u32[]{:S(2)}) %collective-permute-start.3) | collective-permute-done | bytes 524320 | tf_op jit(solution)/shard_map/ppermute | solution.py:37
  63.1 3.2 %collective-permute-start.4 = (bf16[64,32,128]{2,1,0:T(8,128)(2,1)S(1)}, bf16[64,32,128]{2,1,0:T(8,128)(2,1)S(1)}, u32[]{:S(2)}, u32[]{:S(2)}) collective-permute-start(bf16[64,32,128]{2,1,0:T(8,128)(2,1)S(1)} %collective-permute-done.3.c1), channel_id=1, source_target_pairs={{0,4},{4,8},{8,12},{12,16},{16,20},{20,24},{24,28},{32,36},{36,40}... | collective-permute-start | bytes 1572872 | tf_op jit(solution)/shard_map/ppermute | solution.py:37
  66.2 7.1 %collective-permute-done.1.r2 = bf16[64,32,128]{2,1,0:T(8,128)(2,1)S(1)} collective-permute-done((bf16[64,32,128]{2,1,0:T(8,128)(2,1)S(1)}, bf16[64,32,128]{2,1,0:T(8,128)(2,1)S(1)}, u32[]{:S(2)}, u32[]{:S(2)}) %collective-permute-start.1) | collective-permute-done | bytes 524320 | tf_op jit(solution)/shard_map/ppermute | solution.py:37
  73.3 3.4 %collective-permute-start.5 = (bf16[64,32,128]{2,1,0:T(8,128)(2,1)S(1)}, bf16[64,32,128]{2,1,0:T(8,128)(2,1)S(1)}, u32[]{:S(2)}, u32[]{:S(2)}) collective-permute-start(bf16[64,32,128]{2,1,0:T(8,128)(2,1)S(1)} %collective-permute-done.1.r2), channel_id=1, source_target_pairs={{0,4},{1,5},{2,6},{3,7},{4,8},{5,9},{6,10},{7,11},{8,12},{9,13},{1... | collective-permute-start | bytes 1572872 | tf_op jit(solution)/shard_map/ppermute | solution.py:37
  76.7 1.5 %weights.1 = (bf16[128,512]{1,0:T(8,128)(2,1)}, bf16[256,256]{1,0:T(8,128)(2,1)}, f32[7,128]{1,0:T(8,128)}) custom-call(bf16[64,256]{1,0:T(8,128)(2,1)} %w_k.1, bf16[64,256]{1,0:T(8,128)(2,1)} %w_v.1, f32[7,64]{1,0:T(8,128)} %tpos.1), custom_call_target="tpu_custom_call" | custom-call | tf_op jit(solution)/shard_map/weights/pallas_call | solution.py:229
  78.2 0.0 all-to-all-done.1.incoming
  78.2 0.0 copy-done.3
  78.2 1.0 copy-done.1
  79.2 10.1 %keyed.1 = f32[8,8,64,128]{3,2,1,0:T(8,128)} custom-call(s32[1]{0:T(128)} %bitcast.place, s32[64]{0:T(128)} %bitcast.35, bf16[8,8,64,256]{3,2,1,0:T(8,128)(2,1)} %bitcast.19, bf16[128,32,128]{2,1,0:T(8,128)(2,1)} %copy-done.1, bf16[8,8,32,128]{3,2,1,0:T(8,128)(2,1)} %bitcast.26, bf16[8,8,32,128]{3,2,1,0:T(8,128)(2,1)} %bitcast.27, ...), custom_call_target="tpu_custom_call" | custom-call | tf_op jit(solution)/shard_map/keyed/pallas_call | solution.py:257
  89.3 0.0 collective-permute-done.2.r3
  89.3 0.0 collective-permute-done.4.d2
  89.3 0.0 collective-permute-done.5.r6
  89.3 0.0 copy-start.8
  89.3 0.0 copy-done.6
  89.3 0.8 copy-done.7
  90.1 0.2 copy-done.8
  90.3 14.3 %final.1 = (bf16[64,64,256]{2,1,0:T(8,128)(2,1)}, f32[256,256]{1,0:T(8,128)}) custom-call(s32[1]{0:T(128)} %bitcast.place, bf16[64,64,256]{2,1,0:T(8,128)(2,1)} %bitcast.20, bf16[64,32,128]{2,1,0:T(8,128)(2,1)} %copy-done.6, bf16[64,32,128]{2,1,0:T(8,128)(2,1)} %collective-permute-done.2.r3, bf16[64,32,128]{2,1,0:T(8,128)(2,1)} %copy-done.3, ...), custom_call_target="tpu_custom_call" | custom-call | tf_op jit(solution)/shard_map/final/pallas_call | solution.py:285
  104.5 17.8 %all_to_all.21 = f32[32,8,256]{2,1,0:T(8,128)S(1)} all-to-all(f32[32,8,256]{2,1,0:T(8,128)} %bitcast.31), channel_id=1, replica_groups=mesh['video'=8,'tm'=32] {'tm'}, dimensions={0} | all-to-all | bytes 524288 | tf_op jit(solution)/shard_map/all_to_all | solution.py:325
  122.4 0.1 collective-permute-start.7
  122.5 1.2 collective-permute-done.7
  123.7 0.8 collective-permute-start.10
  124.5 2.4 %collective-permute-start.9 = (f32[8,256]{1,0:T(8,128)S(1)}, f32[8,256]{1,0:T(8,128)S(1)}, u32[]{:S(2)}, u32[]{:S(2)}) collective-permute-start(f32[8,256]{1,0:T(8,128)S(1)} %fusion), channel_id=1, source_target_pairs={{0,64},{32,96},{64,128},{96,160},{128,192},{160,224},{192,0},{224,... | collective-permute-start | bytes 24584 | tf_op jit(solution)/shard_map/ppermute | solution.py:332
  126.9 0.1 collective-permute-start.8
  127.0 1.5 %collective-permute-done.10 = f32[8,256]{1,0:T(8,128)S(1)} collective-permute-done((f32[8,256]{1,0:T(8,128)S(1)}, f32[8,256]{1,0:T(8,128)S(1)}, u32[]{:S(2)}, u32[]{:S(2)}) %collective-permute-start.10) | collective-permute-done | bytes 8224 | tf_op jit(solution)/shard_map/ppermute | solution.py:332
  128.5 0.0 collective-permute-done.9
  128.5 3.5 %collective-permute-done.8 = f32[8,256]{1,0:T(8,128)S(1)} collective-permute-done((f32[8,256]{1,0:T(8,128)S(1)}, f32[8,256]{1,0:T(8,128)S(1)}, u32[]{:S(2)}, u32[]{:S(2)}) %collective-permute-start.8) | collective-permute-done | bytes 8224 | tf_op jit(solution)/shard_map/ppermute | solution.py:332
  132.1 0.6 add_add_fusion
  (10 shorter events, 0.1 us)
Async XLA Ops:
  3.3 27.3 %copy-start = (bf16[8,8,32,128]{3,2,1,0:T(8,128)(2,1)}, bf16[8,8,32,128]{3,2,1,0:T(8,128)(2,1)S(1)}, u32[]{:S(2)}) copy-start(bf16[8,8,32,128]{3,2,1,0:T(8,128)(2,1)S(1)} %copy.11) | copy-start | bytes 1572868
  3.3 17.7 %collective-permute-start = (bf16[64,32,128]{2,1,0:T(8,128)(2,1)S(1)}, bf16[64,32,128]{2,1,0:T(8,128)(2,1)S(1)}, u32[]{:S(2)}, u32[]{:S(2)}) collective-permute-start(bf16[64,32,128]{2,1,0:T(8,128)(2,1)S(1)} %bitcast.22), channel_id=1, source_target_pairs={{0,4},{1,5},{2,6},{3,7},{4,8},{5,9},{6,10},{7,11},{8,12},{9,13},{1... | collective-permute-start | bytes 1572872 | tf_op jit(solution)/shard_map/ppermute | solution.py:37
  7.1 23.4 %collective-permute-start.6 = (bf16[64,32,128]{2,1,0:T(8,128)(2,1)S(1)}, bf16[64,32,128]{2,1,0:T(8,128)(2,1)S(1)}, u32[]{:S(2)}, u32[]{:S(2)}) collective-permute-start(bf16[64,32,128]{2,1,0:T(8,128)(2,1)S(1)} %bitcast.23), channel_id=1, source_target_pairs={{0,1},{1,2},{2,3},{4,5},{5,6},{6,7},{8,9},{9,10},{10,11},{12,13},{... | collective-permute-start | bytes 1572872 | tf_op jit(solution)/shard_map/ppermute | solution.py:37
  10.7 19.9 %all-to-all-start = ((s32[32,1,128]{2,1,0:T(1,128)}), s32[32,1,128]{2,1,0:T(1,128)S(1)}, u32[]{:S(2)}, u32[]{:S(2)}) async-start(s32[32,1,128]{2,1,0:T(1,128)} %bitcast.33), calls=%async_computation | async-start | bytes 32768 | tf_op jit(solution)/shard_map/all_to_all | solution.py:228
  20.9 16.8 %copy-start.4 = (bf16[64,32,128]{2,1,0:T(8,128)(2,1)}, bf16[64,32,128]{2,1,0:T(8,128)(2,1)S(1)}, u32[]{:S(2)}) copy-start(bf16[64,32,128]{2,1,0:T(8,128)(2,1)S(1)} %collective-permute-done) | copy-start | bytes 1572868
  30.6 0.6 copy-start.9
  30.6 0.8 copy-start.2
  31.4 8.1 %copy-start.5 = (bf16[64,32,128]{2,1,0:T(8,128)(2,1)S(1)}, bf16[64,32,128]{2,1,0:T(8,128)(2,1)}, u32[]{:S(2)}) copy-start(bf16[64,32,128]{2,1,0:T(8,128)(2,1)} %get-tuple-element.17.rest_0_) | copy-start | bytes 1572868
  33.8 44.5 %all-to-all-start.1 = ((bf16[128,32,128]{2,1,0:T(8,128)(2,1)}), bf16[128,32,128]{2,1,0:T(8,128)(2,1)S(1)}, u32[]{:S(2)}, u32[]{:S(2)}) async-start(bf16[128,32,128]{2,1,0:T(8,128)(2,1)} %pick.1), calls=%async_computation.1 | async-start | bytes 2097152 | tf_op jit(solution)/shard_map/all_to_all | solution.py:248
  37.7 25.3 %collective-permute-start.3 = (bf16[64,32,128]{2,1,0:T(8,128)(2,1)S(1)}, bf16[64,32,128]{2,1,0:T(8,128)(2,1)S(1)}, u32[]{:S(2)}, u32[]{:S(2)}) collective-permute-start(bf16[64,32,128]{2,1,0:T(8,128)(2,1)S(1)} %collective-permute-done), channel_id=1, source_target_pairs={{0,1},{1,2},{2,3},{3,0},{4,5},{5,6},{6,7},{7,4},{8,9},{9,10},{10,1... | collective-permute-start | bytes 1572872 | tf_op jit(solution)/shard_map/ppermute | solution.py:37
  39.5 33.8 %collective-permute-start.1 = (bf16[64,32,128]{2,1,0:T(8,128)(2,1)S(1)}, bf16[64,32,128]{2,1,0:T(8,128)(2,1)S(1)}, u32[]{:S(2)}, u32[]{:S(2)}) collective-permute-start(bf16[64,32,128]{2,1,0:T(8,128)(2,1)S(1)} %copy-done.5), channel_id=1, source_target_pairs={{0,2},{1,3},{2,0},{3,1},{4,6},{5,7},{6,4},{7,5},{8,10},{9,11},{10,... | collective-permute-start | bytes 1572872 | tf_op jit(solution)/shard_map/ppermute | solution.py:37
  42.2 47.1 %collective-permute-start.2 = (bf16[64,32,128]{2,1,0:T(8,128)(2,1)}, bf16[64,32,128]{2,1,0:T(8,128)(2,1)}, u32[]{:S(2)}, u32[]{:S(2)}) collective-permute-start(bf16[64,32,128]{2,1,0:T(8,128)(2,1)} %get-tuple-element.16), channel_id=1, source_target_pairs={{0,3},{1,0},{2,1},{3,2},{4,7},{5,4},{6,5},{7,6},{8,11},{9,8},{10,9... | collective-permute-start | bytes 1572872 | tf_op jit(solution)/shard_map/ppermute | solution.py:37
  63.1 15.2 %copy-start.3 = (bf16[64,32,128]{2,1,0:T(8,128)(2,1)}, bf16[64,32,128]{2,1,0:T(8,128)(2,1)S(1)}, u32[]{:S(2)}) copy-start(bf16[64,32,128]{2,1,0:T(8,128)(2,1)S(1)} %collective-permute-done.3.c1) | copy-start | bytes 1572868
  63.1 26.2 %collective-permute-start.4 = (bf16[64,32,128]{2,1,0:T(8,128)(2,1)S(1)}, bf16[64,32,128]{2,1,0:T(8,128)(2,1)S(1)}, u32[]{:S(2)}, u32[]{:S(2)}) collective-permute-start(bf16[64,32,128]{2,1,0:T(8,128)(2,1)S(1)} %collective-permute-done.3.c1), channel_id=1, source_target_pairs={{0,4},{4,8},{8,12},{12,16},{16,20},{20,24},{24,28},{32,36},{36,40}... | collective-permute-start | bytes 1572872 | tf_op jit(solution)/shard_map/ppermute | solution.py:37
  73.3 16.0 %copy-start.6 = (bf16[64,32,128]{2,1,0:T(8,128)(2,1)}, bf16[64,32,128]{2,1,0:T(8,128)(2,1)S(1)}, u32[]{:S(2)}) copy-start(bf16[64,32,128]{2,1,0:T(8,128)(2,1)S(1)} %collective-permute-done.1.r2) | copy-start | bytes 1572868
  73.3 16.0 %collective-permute-start.5 = (bf16[64,32,128]{2,1,0:T(8,128)(2,1)S(1)}, bf16[64,32,128]{2,1,0:T(8,128)(2,1)S(1)}, u32[]{:S(2)}, u32[]{:S(2)}) collective-permute-start(bf16[64,32,128]{2,1,0:T(8,128)(2,1)S(1)} %collective-permute-done.1.r2), channel_id=1, source_target_pairs={{0,4},{1,5},{2,6},{3,7},{4,8},{5,9},{6,10},{7,11},{8,12},{9,13},{1... | collective-permute-start | bytes 1572872 | tf_op jit(solution)/shard_map/ppermute | solution.py:37
  78.2 1.0 copy-start.1
  89.3 0.8 copy-start.7
  89.3 1.0 copy-start.8
  122.4 1.3 collective-permute-start.7
  123.7 4.9 %collective-permute-start.10 = (f32[8,256]{1,0:T(8,128)S(1)}, f32[8,256]{1,0:T(8,128)S(1)}, u32[]{:S(2)}, u32[]{:S(2)}) collective-permute-start(f32[8,256]{1,0:T(8,128)S(1)} %fusion), channel_id=1, source_target_pairs={{0,192},{32,224},{64,0},{96,32},{128,64},{160,96},{192,128},{224,1... | collective-permute-start | bytes 24584 | tf_op jit(solution)/shard_map/ppermute | solution.py:332
  124.5 4.0 %collective-permute-start.9 = (f32[8,256]{1,0:T(8,128)S(1)}, f32[8,256]{1,0:T(8,128)S(1)}, u32[]{:S(2)}, u32[]{:S(2)}) collective-permute-start(f32[8,256]{1,0:T(8,128)S(1)} %fusion), channel_id=1, source_target_pairs={{0,64},{32,96},{64,128},{96,160},{128,192},{160,224},{192,0},{224,... | collective-permute-start | bytes 24584 | tf_op jit(solution)/shard_map/ppermute | solution.py:332
  126.9 5.2 %collective-permute-start.8 = (f32[8,256]{1,0:T(8,128)S(1)}, f32[8,256]{1,0:T(8,128)S(1)}, u32[]{:S(2)}, u32[]{:S(2)}) collective-permute-start(f32[8,256]{1,0:T(8,128)S(1)} %fusion), channel_id=1, source_target_pairs={{0,128},{32,160},{64,192},{96,224},{128,0},{160,32},{192,64},{224,... | collective-permute-start | bytes 24584 | tf_op jit(solution)/shard_map/ppermute | solution.py:332

commit v5 on v4

--- a/solution.py
+++ b/solution.py
@@ -155,7 +155,7 @@
 
 
 def final_kernel(
-    place, q, r2, r3, c1, d2, r6, packed, tpos, w_key, w_value, w_o, cot, branch, grad, mixed
+    place, q, r2, r3, c1, d2, r6, packed, tpos, w_key, w_value, w_o, cot, branch, grad, mixed, total
 ):
     frame = place[0]
     y = frame % RING
@@ -192,11 +192,15 @@
 
     @pl.when(step == 0)
     def _():
-        grad[...] = term
+        total[...] = term
 
     @pl.when(step > 0)
     def _():
-        grad[...] += term
+        total[...] += term
+
+    @pl.when(step == pl.num_programs(0) - 1)
+    def _():
+        grad[...] = total[...].astype(jnp.bfloat16)
 
 
 def per_device(queries, memory, tpos, w_k, w_v, w_o, keyframes, cot):
@@ -233,10 +237,10 @@
             jax.ShapeDtypeStruct((2 * LANES, D), jnp.bfloat16),
             jax.ShapeDtypeStruct((7, LANES), jnp.float32),
         ],
-        in_specs=[in_vmem] * 3 + [pl.BlockSpec(memory_space=pl.ANY)] * 0,
+        in_specs=[in_vmem] * 3 + [pl.BlockSpec(memory_space=pl.ANY)] * 1,
         out_specs=[in_vmem] * 3,
         name="weights",
-    )(w_k, w_v, tpos)
+    )(w_k, w_v, tpos, x2)
     outgoing = pl.pallas_call(
         pick_kernel,
         out_shape=jax.ShapeDtypeStruct((devices * RUN, PAIRS, LANES), jnp.bfloat16),
@@ -244,7 +248,7 @@
         out_specs=in_vmem,
         compiler_params=pltpu.CompilerParams(vmem_limit_bytes=60 * MIB),
         name="pick",
-    )(asked, own, x2, b1)
+    )(asked, own, w_key, b1)
     incoming = lax.all_to_all(outgoing, "tm", split_axis=0, concat_axis=0, tiled=True)
     r6 = routed(r2, rows, lambda z, y: (z + 1, y))
     d2 = routed(c1, rows, lambda z, y: (z + 1, y) if y == 0 else None)
@@ -269,7 +273,7 @@
             ],
         ),
         out_shape=jax.ShapeDtypeStruct((groups, CLASSES, TT, LANES), jnp.float32),
-        compiler_params=pltpu.CompilerParams(vmem_limit_bytes=60 * MIB),
+        compiler_params=pltpu.CompilerParams(vmem_limit_bytes=30 * MIB),
         name="keyed",
     )(
         place,
@@ -298,13 +302,16 @@
                 row_block(D),
             ],
             out_specs=[row_block(D), whole(D, D)],
-            scratch_shapes=[pltpu.VMEM((BLOCK, 4, PAIRS, LANES), jnp.bfloat16)],
+            scratch_shapes=[
+                pltpu.VMEM((BLOCK, 4, PAIRS, LANES), jnp.bfloat16),
+                pltpu.VMEM((D, D), jnp.float32),
+            ],
         ),
         out_shape=[
             jax.ShapeDtypeStruct((TILES, TT, D), jnp.bfloat16),
-            jax.ShapeDtypeStruct((D, D), jnp.float32),
+            jax.ShapeDtypeStruct((D, D), jnp.bfloat16),
         ],
-        compiler_params=pltpu.CompilerParams(vmem_limit_bytes=60 * MIB),
+        compiler_params=pltpu.CompilerParams(vmem_limit_bytes=30 * MIB),
         name="final",
     )(
         place,
@@ -326,7 +333,7 @@
         grad.reshape(devices, D // devices, D), "tm", split_axis=0, concat_axis=0, tiled=True
     )
     videos = lax.axis_size("video")
-    summed = jnp.sum(parts, axis=0) * (1.0 / math.sqrt(videos * devices * TILES * TT))
+    summed = jnp.sum(parts.astype(jnp.float32), axis=0) * (1.0 / math.sqrt(videos * devices * TILES * TT))
     summed = summed + lax.ppermute(summed, "video", [(i, i ^ 1) for i in range(videos)])
     others = [
         lax.ppermute(summed, "video", [(i, (i + chip) % videos) for i in range(videos)])

time: 133 us -> 132 us (level)
  Pallas kernels: 29.7 us -> 27.3 us
  waiting for transfers between devices: 41.2 us -> 39.3 us
  starting transfers between devices: 37.5 us -> 39.4 us
    ppermute x7, starting transfers between devices: 19.8 us -> 21.7 us  [routed(): return lax.ppermute(shard, 'tm', pairs)]
    pallas_call x1, Pallas kernels: 10.1 us -> 8.37 us  [per_device(): pl.pallas_call(keyed_kernel, grid_spec=pltpu.PrefetchScalarGridSpec(num_s...]
    all_to_all x1, waiting for transfers between devices: 8.5 us -> 6.97 us  [per_device(): asked = lax.all_to_all(asks, 'tm', split_axis=0, concat_axis=0, tiled=True)]
    unnamed x21 -> x27, local copies, waits for them, and re-layouts: 3.87 us -> 4.02 us
  transfers between devices with their start and end apart: 13 -> 13, of which waited for: 6 -> 6; matrix products, arithmetic and copies ran while one was open for 1% -> 1% of each run, Pallas kernels for 9% -> 8%
where the time goes in v5:
time: 132 us; the launch traced here: 131 us
  starting transfers between devices  39.4 us (30%)
  waiting for transfers between devices  39.3 us (30%)
  Pallas kernels  27.3 us (21%)
  blocking collectives  18.6 us (14%)
  local copies, waits for them, and re-layouts  4.02 us (3%)
  other arithmetic  1.8 us (1%)
    ppermute x7, waiting for transfers between devices, routed(): return lax.ppermute(shard, 'tm', pairs)  26.2 us
    ppermute x7, starting transfers between devices, routed(): return lax.ppermute(shard, 'tm', pairs)  21.7 us
    all_to_all x1, blocking collectives, per_device(): lax.all_to_all(grad.reshape(devices, D // devices, D), 'tm', split_axis=0...  18.6 us
    pallas_call x1, Pallas kernels, per_device(): pl.pallas_call(final_kernel, grid_spec=pltpu.PrefetchScalarGridSpec(num_s...  13.5 us
    all_to_all x1, starting transfers between devices, per_device(): asked = lax.all_to_all(asks, 'tm', split_axis=0, concat_axis=0, tiled=True)  10.2 us
    pallas_call x1, Pallas kernels, per_device(): pl.pallas_call(keyed_kernel, grid_spec=pltpu.PrefetchScalarGridSpec(num_s...  8.37 us
    all_to_all x1, waiting for transfers between devices, per_device(): asked = lax.all_to_all(asks, 'tm', split_axis=0, concat_axis=0, tiled=True)  6.97 us
    ppermute x3, waiting for transfers between devices, per_device(): lax.ppermute(summed, 'video', [(i, (i + chip) % videos) for i in range(vi...  4.95 us
  transfers between devices with their start and end apart: 13, of which 6 were waited for; matrix products, arithmetic and copies ran while one was open for 1% of the time, Pallas kernels for 8%

profile of v5, /device:TPU:6, one launch (start us, length us, event | category | flops | bytes accessed | tf_op | source)
XLA Modules:
  0.0 131.2 jit_solution(5858629747620827461)
XLA Ops:
  0.6 1.5 %ask.1 = s32[32,128]{1,0:T(8,128)} custom-call(s32[64]{0:T(128)} %bitcast.26), custom_call_target="tpu_custom_call" | custom-call | tf_op jit(solution)/shard_map/ask/pallas_call | solution.py:216
  2.1 1.1 copy.11
  3.3 0.0 copy-start.11
  3.3 3.9 %collective-permute-start = (bf16[64,32,128]{2,1,0:T(8,128)(2,1)S(1)}, bf16[64,32,128]{2,1,0:T(8,128)(2,1)S(1)}, u32[]{:S(2)}, u32[]{:S(2)}) collective-permute-start(bf16[64,32,128]{2,1,0:T(8,128)(2,1)S(1)} %bitcast.28), channel_id=1, source_target_pairs={{0,4},{1,5},{2,6},{3,7},{4,8},{5,9},{6,10},{7,11},{8,12},{9,13},{1... | collective-permute-start | bytes 1572872 | tf_op jit(solution)/shard_map/ppermute | solution.py:37
  7.1 3.5 %collective-permute-start.6 = (bf16[64,32,128]{2,1,0:T(8,128)(2,1)S(1)}, bf16[64,32,128]{2,1,0:T(8,128)(2,1)S(1)}, u32[]{:S(2)}, u32[]{:S(2)}) collective-permute-start(bf16[64,32,128]{2,1,0:T(8,128)(2,1)S(1)} %bitcast.29), channel_id=1, source_target_pairs={{0,1},{1,2},{2,3},{4,5},{5,6},{6,7},{8,9},{9,10},{10,11},{12,13},{... | collective-permute-start | bytes 1572872 | tf_op jit(solution)/shard_map/ppermute | solution.py:37
  10.7 10.2 %all-to-all-start = ((s32[32,1,128]{2,1,0:T(1,128)}), s32[32,1,128]{2,1,0:T(1,128)S(1)}, u32[]{:S(2)}, u32[]{:S(2)}) async-start(s32[32,1,128]{2,1,0:T(1,128)} %bitcast.34), calls=%async_computation | async-start | bytes 32768 | tf_op jit(solution)/shard_map/all_to_all | solution.py:232
  20.9 0.0 collective-permute-done
  20.9 0.0 copy-start.3
  20.9 1.2 broadcast_select_fusion
  22.1 1.5 %weights.1 = (bf16[128,512]{1,0:T(8,128)(2,1)}, bf16[256,256]{1,0:T(8,128)(2,1)}, f32[7,128]{1,0:T(8,128)}) custom-call(bf16[64,256]{1,0:T(8,128)(2,1)} %w_k.1, bf16[64,256]{1,0:T(8,128)(2,1)} %w_v.1, f32[7,64]{1,0:T(8,128)} %tpos.1, bf16[64,32,128]{2,1,0:T(8,128)(2,1)} %get-tuple-element.17.rest_0_), custom_call_target="tpu_custom_call" | custom-call | tf_op jit(solution)/shard_map/weights/pallas_call | solution.py:233
  23.6 7.0 %all-to-all-done = s32[32,1,128]{2,1,0:T(1,128)S(1)} async-done(((s32[32,1,128]{2,1,0:T(1,128)}), s32[32,1,128]{2,1,0:T(1,128)S(1)}, u32[]{:S(2)}, u32[]{:S(2)}) %all-to-all-start) | async-done | bytes 16416 | tf_op jit(solution)/shard_map/all_to_all | solution.py:232
  30.6 0.0 collective-permute-done.6.rest_1_
  30.6 0.0 copy-done.3
  30.6 0.0 copy-done.11
  30.6 0.6 copy-done.12
  31.2 0.2 copy-done.1
  31.4 2.5 %pick.1 = bf16[128,32,128]{2,1,0:T(8,128)(2,1)} custom-call(s32[32,128]{1,0:T(8,128)} %bitcast.33, bf16[64,32,128]{2,1,0:T(8,128)(2,1)} %bitcast.31, bf16[128,512]{1,0:T(8,128)(2,1)} %get-tuple-element.11.rest_0_.w_key, bf16[64,32,128]{2,1,0:T(8,128)(2,1)} %copy-done.1), custom_call_target="tpu_custom_call" | custom-call | tf_op jit(solution)/shard_map/pick/pallas_call | solution.py:244
  33.9 3.9 %all-to-all-start.1 = ((bf16[128,32,128]{2,1,0:T(8,128)(2,1)}), bf16[128,32,128]{2,1,0:T(8,128)(2,1)S(1)}, u32[]{:S(2)}, u32[]{:S(2)}) async-start(bf16[128,32,128]{2,1,0:T(8,128)(2,1)} %pick.1), calls=%async_computation.1 | async-start | bytes 2097152 | tf_op jit(solution)/shard_map/all_to_all | solution.py:252
  37.8 1.8 %collective-permute-start.3 = (bf16[64,32,128]{2,1,0:T(8,128)(2,1)}, bf16[64,32,128]{2,1,0:T(8,128)(2,1)}, u32[]{:S(2)}, u32[]{:S(2)}) collective-permute-start(bf16[64,32,128]{2,1,0:T(8,128)(2,1)} %copy-done.3), channel_id=1, source_target_pairs={{0,1},{1,2},{2,3},{3,0},{4,5},{5,6},{6,7},{7,4},{8,9},{9,10},{10,1... | collective-permute-start | bytes 1572872 | tf_op jit(solution)/shard_map/ppermute | solution.py:37
  39.6 2.7 %collective-permute-start.1 = (bf16[64,32,128]{2,1,0:T(8,128)(2,1)}, bf16[64,32,128]{2,1,0:T(8,128)(2,1)}, u32[]{:S(2)}, u32[]{:S(2)}) collective-permute-start(bf16[64,32,128]{2,1,0:T(8,128)(2,1)} %get-tuple-element.17.rest_0_), channel_id=1, source_target_pairs={{0,2},{1,3},{2,0},{3,1},{4,6},{5,7},{6,4},{7,5},{8,10},{9,11},{10,... | collective-permute-start | bytes 1572872 | tf_op jit(solution)/shard_map/ppermute | solution.py:37
  42.2 1.5 %collective-permute-start.2 = (bf16[64,32,128]{2,1,0:T(8,128)(2,1)}, bf16[64,32,128]{2,1,0:T(8,128)(2,1)}, u32[]{:S(2)}, u32[]{:S(2)}) collective-permute-start(bf16[64,32,128]{2,1,0:T(8,128)(2,1)} %get-tuple-element.16), channel_id=1, source_target_pairs={{0,3},{1,0},{2,1},{3,2},{4,7},{5,4},{6,5},{7,6},{8,11},{9,8},{10,9... | collective-permute-start | bytes 1572872 | tf_op jit(solution)/shard_map/ppermute | solution.py:37
  43.7 19.8 %collective-permute-done.3.c1 = bf16[64,32,128]{2,1,0:T(8,128)(2,1)} collective-permute-done((bf16[64,32,128]{2,1,0:T(8,128)(2,1)}, bf16[64,32,128]{2,1,0:T(8,128)(2,1)}, u32[]{:S(2)}, u32[]{:S(2)}) %collective-permute-start.3) | collective-permute-done | bytes 524320 | tf_op jit(solution)/shard_map/ppermute | solution.py:37
  63.5 4.2 %collective-permute-start.4 = (bf16[64,32,128]{2,1,0:T(8,128)(2,1)}, bf16[64,32,128]{2,1,0:T(8,128)(2,1)}, u32[]{:S(2)}, u32[]{:S(2)}) collective-permute-start(bf16[64,32,128]{2,1,0:T(8,128)(2,1)} %collective-permute-done.3.c1), channel_id=1, source_target_pairs={{0,4},{4,8},{8,12},{12,16},{16,20},{20,24},{24,28},{32,36},{36,40}... | collective-permute-start | bytes 1572872 | tf_op jit(solution)/shard_map/ppermute | solution.py:37
  67.8 6.4 %collective-permute-done.1.r2 = bf16[64,32,128]{2,1,0:T(8,128)(2,1)} collective-permute-done((bf16[64,32,128]{2,1,0:T(8,128)(2,1)}, bf16[64,32,128]{2,1,0:T(8,128)(2,1)}, u32[]{:S(2)}, u32[]{:S(2)}) %collective-permute-start.1) | collective-permute-done | bytes 524320 | tf_op jit(solution)/shard_map/ppermute | solution.py:37
  74.1 4.2 %collective-permute-start.5 = (bf16[64,32,128]{2,1,0:T(8,128)(2,1)}, bf16[64,32,128]{2,1,0:T(8,128)(2,1)}, u32[]{:S(2)}, u32[]{:S(2)}) collective-permute-start(bf16[64,32,128]{2,1,0:T(8,128)(2,1)} %collective-permute-done.1.r2), channel_id=1, source_target_pairs={{0,4},{1,5},{2,6},{3,7},{4,8},{5,9},{6,10},{7,11},{8,12},{9,13},{1... | collective-permute-start | bytes 1572872 | tf_op jit(solution)/shard_map/ppermute | solution.py:37
  78.3 0.0 all-to-all-done.1.incoming
  78.3 0.0 copy-done
  78.3 0.0 copy-done.6
  78.3 0.0 copy-done.9
  78.3 0.0 copy-done.10
  78.3 0.0 copy-start.2
  78.3 1.0 copy-done.2
  79.3 1.0 copy-done.4
  80.4 8.4 %keyed.1 = f32[8,8,64,128]{3,2,1,0:T(8,128)S(1)} custom-call(s32[1]{0:T(128)} %bitcast.place, s32[64]{0:T(128)S(1)} %bitcast.27, bf16[8,8,64,256]{3,2,1,0:T(8,128)(2,1)S(1)} %bitcast.19, bf16[128,32,128]{2,1,0:T(8,128)(2,1)S(1)} %all-to-all-done.1.incoming, bf16[8,8,32,128]{3,2,1,0:T(8,128)(2,1)S(1)} %bitcast.22, bf16[8,8,32,128]{3,2,1,0:T(8,128)(2,1)} %bitcast.8.c1, ...), custom_call_target="tpu_custom_call" | custom-call | tf_op jit(solution)/shard_map/keyed/pallas_call | solution.py:261
  88.8 0.0 collective-permute-done.2.r3
  88.8 0.0 collective-permute-done.4.d2
  88.8 0.0 collective-permute-done.5.r6
  88.8 13.5 %final.1 = (bf16[64,64,256]{2,1,0:T(8,128)(2,1)}, bf16[256,256]{1,0:T(8,128)(2,1)S(1)}) custom-call(s32[1]{0:T(128)} %bitcast.place, bf16[64,64,256]{2,1,0:T(8,128)(2,1)S(1)} %bitcast.20, bf16[64,32,128]{2,1,0:T(8,128)(2,1)} %collective-permute-done.1.r2, bf16[64,32,128]{2,1,0:T(8,128)(2,1)} %collective-permute-done.2.r3, ...), custom_call_target="tpu_custom_call" | custom-call | tf_op jit(solution)/shard_map/final/pallas_call | solution.py:289
  102.3 18.6 %all_to_all.21 = bf16[32,8,256]{2,1,0:T(8,128)(2,1)S(1)} all-to-all(bf16[32,8,256]{2,1,0:T(8,128)(2,1)S(1)} %bitcast.25), channel_id=1, replica_groups=mesh['video'=8,'tm'=32] {'tm'}, dimensions={0} | all-to-all | bytes 262144 | tf_op jit(solution)/shard_map/all_to_all | solution.py:332
  120.9 0.1 collective-permute-start.7
  121.0 1.2 collective-permute-done.7
  122.2 0.8 collective-permute-start.10
  123.0 2.4 %collective-permute-start.9 = (f32[8,256]{1,0:T(8,128)S(1)}, f32[8,256]{1,0:T(8,128)S(1)}, u32[]{:S(2)}, u32[]{:S(2)}) collective-permute-start(f32[8,256]{1,0:T(8,128)S(1)} %fusion), channel_id=1, source_target_pairs={{0,64},{32,96},{64,128},{96,160},{128,192},{160,224},{192,0},{224,... | collective-permute-start | bytes 24584 | tf_op jit(solution)/shard_map/ppermute | solution.py:339
  125.4 0.2 collective-permute-start.8
  125.6 1.4 %collective-permute-done.10 = f32[8,256]{1,0:T(8,128)S(1)} collective-permute-done((f32[8,256]{1,0:T(8,128)S(1)}, f32[8,256]{1,0:T(8,128)S(1)}, u32[]{:S(2)}, u32[]{:S(2)}) %collective-permute-start.10) | collective-permute-done | bytes 8224 | tf_op jit(solution)/shard_map/ppermute | solution.py:339
  127.1 0.0 collective-permute-done.9
  127.1 3.5 %collective-permute-done.8 = f32[8,256]{1,0:T(8,128)S(1)} collective-permute-done((f32[8,256]{1,0:T(8,128)S(1)}, f32[8,256]{1,0:T(8,128)S(1)}, u32[]{:S(2)}, u32[]{:S(2)}) %collective-permute-start.8) | collective-permute-done | bytes 8224 | tf_op jit(solution)/shard_map/ppermute | solution.py:339
  130.6 0.6 add_add_fusion
  (16 shorter events, 0.1 us)
Async XLA Ops:
  3.3 27.3 %copy-start.11 = (bf16[8,8,32,128]{3,2,1,0:T(8,128)(2,1)}, bf16[8,8,32,128]{3,2,1,0:T(8,128)(2,1)S(1)}, u32[]{:S(2)}) copy-start(bf16[8,8,32,128]{3,2,1,0:T(8,128)(2,1)S(1)} %copy.11) | copy-start | bytes 1572868
  3.3 17.7 %collective-permute-start = (bf16[64,32,128]{2,1,0:T(8,128)(2,1)S(1)}, bf16[64,32,128]{2,1,0:T(8,128)(2,1)S(1)}, u32[]{:S(2)}, u32[]{:S(2)}) collective-permute-start(bf16[64,32,128]{2,1,0:T(8,128)(2,1)S(1)} %bitcast.28), channel_id=1, source_target_pairs={{0,4},{1,5},{2,6},{3,7},{4,8},{5,9},{6,10},{7,11},{8,12},{9,13},{1... | collective-permute-start | bytes 1572872 | tf_op jit(solution)/shard_map/ppermute | solution.py:37
  7.1 23.4 %collective-permute-start.6 = (bf16[64,32,128]{2,1,0:T(8,128)(2,1)S(1)}, bf16[64,32,128]{2,1,0:T(8,128)(2,1)S(1)}, u32[]{:S(2)}, u32[]{:S(2)}) collective-permute-start(bf16[64,32,128]{2,1,0:T(8,128)(2,1)S(1)} %bitcast.29), channel_id=1, source_target_pairs={{0,1},{1,2},{2,3},{4,5},{5,6},{6,7},{8,9},{9,10},{10,11},{12,13},{... | collective-permute-start | bytes 1572872 | tf_op jit(solution)/shard_map/ppermute | solution.py:37
  10.7 19.9 %all-to-all-start = ((s32[32,1,128]{2,1,0:T(1,128)}), s32[32,1,128]{2,1,0:T(1,128)S(1)}, u32[]{:S(2)}, u32[]{:S(2)}) async-start(s32[32,1,128]{2,1,0:T(1,128)} %bitcast.34), calls=%async_computation | async-start | bytes 32768 | tf_op jit(solution)/shard_map/all_to_all | solution.py:232
  20.9 9.6 %copy-start.3 = (bf16[64,32,128]{2,1,0:T(8,128)(2,1)}, bf16[64,32,128]{2,1,0:T(8,128)(2,1)S(1)}, u32[]{:S(2)}) copy-start(bf16[64,32,128]{2,1,0:T(8,128)(2,1)S(1)} %collective-permute-done) | copy-start | bytes 1572868
  30.6 0.6 copy-start.12
  30.6 0.8 copy-start.1
  31.4 46.9 %copy-start = (bf16[1,1,4096,256]{3,2,1,0:T(8,128)(2,1)S(1)}, bf16[1,1,4096,256]{3,2,1,0:T(8,128)(2,1)}, u32[]{:S(2)}) copy-start(bf16[1,1,4096,256]{3,2,1,0:T(8,128)(2,1)} %param.8) | copy-start | bytes 6291460
  31.4 46.9 %copy-start.6 = (bf16[128,512]{1,0:T(8,128)(2,1)S(1)}, bf16[128,512]{1,0:T(8,128)(2,1)}, u32[]{:S(2)}) copy-start(bf16[128,512]{1,0:T(8,128)(2,1)} %get-tuple-element.11.rest_0_.w_key) | copy-start | bytes 393220
  31.4 46.9 %copy-start.9 = (f32[7,128]{1,0:T(8,128)S(1)}, f32[7,128]{1,0:T(8,128)}, u32[]{:S(2)}) copy-start(f32[7,128]{1,0:T(8,128)} %get-tuple-element.12.tpos) | copy-start | bytes 10756
  31.4 46.9 %copy-start.10 = (s32[1,1,64]{2,1,0:T(1,128)S(1)}, s32[1,1,64]{2,1,0:T(1,128)}, u32[]{:S(2)}) copy-start(s32[1,1,64]{2,1,0:T(1,128)} %param.14) | copy-start | bytes 772
  33.9 44.4 %all-to-all-start.1 = ((bf16[128,32,128]{2,1,0:T(8,128)(2,1)}), bf16[128,32,128]{2,1,0:T(8,128)(2,1)S(1)}, u32[]{:S(2)}, u32[]{:S(2)}) async-start(bf16[128,32,128]{2,1,0:T(8,128)(2,1)} %pick.1), calls=%async_computation.1 | async-start | bytes 2097152 | tf_op jit(solution)/shard_map/all_to_all | solution.py:252
  37.8 25.7 %collective-permute-start.3 = (bf16[64,32,128]{2,1,0:T(8,128)(2,1)}, bf16[64,32,128]{2,1,0:T(8,128)(2,1)}, u32[]{:S(2)}, u32[]{:S(2)}) collective-permute-start(bf16[64,32,128]{2,1,0:T(8,128)(2,1)} %copy-done.3), channel_id=1, source_target_pairs={{0,1},{1,2},{2,3},{3,0},{4,5},{5,6},{6,7},{7,4},{8,9},{9,10},{10,1... | collective-permute-start | bytes 1572872 | tf_op jit(solution)/shard_map/ppermute | solution.py:37
  39.6 34.6 %collective-permute-start.1 = (bf16[64,32,128]{2,1,0:T(8,128)(2,1)}, bf16[64,32,128]{2,1,0:T(8,128)(2,1)}, u32[]{:S(2)}, u32[]{:S(2)}) collective-permute-start(bf16[64,32,128]{2,1,0:T(8,128)(2,1)} %get-tuple-element.17.rest_0_), channel_id=1, source_target_pairs={{0,2},{1,3},{2,0},{3,1},{4,6},{5,7},{6,4},{7,5},{8,10},{9,11},{10,... | collective-permute-start | bytes 1572872 | tf_op jit(solution)/shard_map/ppermute | solution.py:37
  42.2 46.5 %collective-permute-start.2 = (bf16[64,32,128]{2,1,0:T(8,128)(2,1)}, bf16[64,32,128]{2,1,0:T(8,128)(2,1)}, u32[]{:S(2)}, u32[]{:S(2)}) collective-permute-start(bf16[64,32,128]{2,1,0:T(8,128)(2,1)} %get-tuple-element.16), channel_id=1, source_target_pairs={{0,3},{1,0},{2,1},{3,2},{4,7},{5,4},{6,5},{7,6},{8,11},{9,8},{10,9... | collective-permute-start | bytes 1572872 | tf_op jit(solution)/shard_map/ppermute | solution.py:37
  63.5 25.3 %collective-permute-start.4 = (bf16[64,32,128]{2,1,0:T(8,128)(2,1)}, bf16[64,32,128]{2,1,0:T(8,128)(2,1)}, u32[]{:S(2)}, u32[]{:S(2)}) collective-permute-start(bf16[64,32,128]{2,1,0:T(8,128)(2,1)} %collective-permute-done.3.c1), channel_id=1, source_target_pairs={{0,4},{4,8},{8,12},{12,16},{16,20},{20,24},{24,28},{32,36},{36,40}... | collective-permute-start | bytes 1572872 | tf_op jit(solution)/shard_map/ppermute | solution.py:37
  74.1 14.7 %collective-permute-start.5 = (bf16[64,32,128]{2,1,0:T(8,128)(2,1)}, bf16[64,32,128]{2,1,0:T(8,128)(2,1)}, u32[]{:S(2)}, u32[]{:S(2)}) collective-permute-start(bf16[64,32,128]{2,1,0:T(8,128)(2,1)} %collective-permute-done.1.r2), channel_id=1, source_target_pairs={{0,4},{1,5},{2,6},{3,7},{4,8},{5,9},{6,10},{7,11},{8,12},{9,13},{1... | collective-permute-start | bytes 1572872 | tf_op jit(solution)/shard_map/ppermute | solution.py:37
  78.3 1.0 copy-start.2
  79.3 1.0 copy-start.4
  80.4 8.4 %copy-start.5 = (bf16[1,1,4096,256]{3,2,1,0:T(8,128)(2,1)S(1)}, bf16[1,1,4096,256]{3,2,1,0:T(8,128)(2,1)}, u32[]{:S(2)}) copy-start(bf16[1,1,4096,256]{3,2,1,0:T(8,128)(2,1)} %param.15) | copy-start | bytes 6291460
  80.4 8.4 %copy-start.7 = (bf16[256,256]{1,0:T(8,128)(2,1)S(1)}, bf16[256,256]{1,0:T(8,128)(2,1)}, u32[]{:S(2)}) copy-start(bf16[256,256]{1,0:T(8,128)(2,1)} %w_o.1) | copy-start | bytes 393220
  80.4 8.4 %copy-start.8 = (bf16[256,256]{1,0:T(8,128)(2,1)S(1)}, bf16[256,256]{1,0:T(8,128)(2,1)}, u32[]{:S(2)}) copy-start(bf16[256,256]{1,0:T(8,128)(2,1)} %get-tuple-element.13.w_value) | copy-start | bytes 393220
  120.9 1.3 collective-permute-start.7
  122.2 4.9 %collective-permute-start.10 = (f32[8,256]{1,0:T(8,128)S(1)}, f32[8,256]{1,0:T(8,128)S(1)}, u32[]{:S(2)}, u32[]{:S(2)}) collective-permute-start(f32[8,256]{1,0:T(8,128)S(1)} %fusion), channel_id=1, source_target_pairs={{0,192},{32,224},{64,0},{96,32},{128,64},{160,96},{192,128},{224,1... | collective-permute-start | bytes 24584 | tf_op jit(solution)/shard_map/ppermute | solution.py:339
  123.0 4.0 %collective-permute-start.9 = (f32[8,256]{1,0:T(8,128)S(1)}, f32[8,256]{1,0:T(8,128)S(1)}, u32[]{:S(2)}, u32[]{:S(2)}) collective-permute-start(f32[8,256]{1,0:T(8,128)S(1)} %fusion), channel_id=1, source_target_pairs={{0,64},{32,96},{64,128},{96,160},{128,192},{160,224},{192,0},{224,... | collective-permute-start | bytes 24584 | tf_op jit(solution)/shard_map/ppermute | solution.py:339
  125.4 5.2 %collective-permute-start.8 = (f32[8,256]{1,0:T(8,128)S(1)}, f32[8,256]{1,0:T(8,128)S(1)}, u32[]{:S(2)}, u32[]{:S(2)}) collective-permute-start(f32[8,256]{1,0:T(8,128)S(1)} %fusion), channel_id=1, source_target_pairs={{0,128},{32,160},{64,192},{96,224},{128,0},{160,32},{192,64},{224,... | collective-permute-start | bytes 24584 | tf_op jit(solution)/shard_map/ppermute | solution.py:339

commit v6 on v5

--- a/solution.py
+++ b/solution.py
@@ -218,6 +218,7 @@
         out_shape=jax.ShapeDtypeStruct((devices, LANES), jnp.int32),
         in_specs=[in_smem],
         out_specs=in_vmem,
+        compiler_params=pltpu.CompilerParams(vmem_limit_bytes=8 * MIB),
         name="ask",
     )(listed)
     own, asks = lax.optimization_barrier((own, asks))
@@ -239,6 +240,7 @@
         ],
         in_specs=[in_vmem] * 3 + [pl.BlockSpec(memory_space=pl.ANY)] * 1,
         out_specs=[in_vmem] * 3,
+        compiler_params=pltpu.CompilerParams(vmem_limit_bytes=8 * MIB),
         name="weights",
     )(w_k, w_v, tpos, x2)
     outgoing = pl.pallas_call(
@@ -246,7 +248,7 @@
         out_shape=jax.ShapeDtypeStruct((devices * RUN, PAIRS, LANES), jnp.bfloat16),
         in_specs=[in_smem, in_vmem] + [pl.BlockSpec(memory_space=pl.ANY)] * 2,
         out_specs=in_vmem,
-        compiler_params=pltpu.CompilerParams(vmem_limit_bytes=60 * MIB),
+        compiler_params=pltpu.CompilerParams(vmem_limit_bytes=8 * MIB),
         name="pick",
     )(asked, own, w_key, b1)
     incoming = lax.all_to_all(outgoing, "tm", split_axis=0, concat_axis=0, tiled=True)

time: 132 us -> 130 us (0.985)
  Pallas kernels: 27.3 us -> 24.3 us
  local copies, waits for them, and re-layouts: 4.02 us -> 5.69 us
    unnamed x27 -> x29, local copies, waits for them, and re-layouts: 4.02 us -> 5.69 us
    pallas_call x1, Pallas kernels: 1.5 us -> 0.07 us  [per_device(): pl.pallas_call(weights_kernel, out_shape=[jax.ShapeDtypeStruct((LANES, 2...]
    pallas_call x1, Pallas kernels: 2.49 us -> 1.11 us  [per_device(): pl.pallas_call(pick_kernel, out_shape=jax.ShapeDtypeStruct((devices * RUN...]
  transfers between devices with their start and end apart: 13 -> 13, of which waited for: 6 -> 6; matrix products, arithmetic and copies ran while one was open for 1% -> 1% of each run, Pallas kernels for 8% -> 7%
where the time goes in v6:
time: 130 us
  waiting for transfers between devices  40.6 us (31%)
  starting transfers between devices  38.3 us (29%)
  Pallas kernels  24.3 us (19%)
  blocking collectives  18.1 us (14%)
  local copies, waits for them, and re-layouts  5.69 us (4%)
  other arithmetic  1.65 us (1%)
    ppermute x7, waiting for transfers between devices, routed(): return lax.ppermute(shard, 'tm', pairs)  26.7 us
    ppermute x7, starting transfers between devices, routed(): return lax.ppermute(shard, 'tm', pairs)  20.6 us
    all_to_all x1, blocking collectives, per_device(): lax.all_to_all(grad.reshape(devices, D // devices, D), 'tm', split_axis=0...  18.1 us
    pallas_call x1, Pallas kernels, per_device(): pl.pallas_call(final_kernel, grid_spec=pltpu.PrefetchScalarGridSpec(num_s...  13.5 us
    all_to_all x1, starting transfers between devices, per_device(): asked = lax.all_to_all(asks, 'tm', split_axis=0, concat_axis=0, tiled=True)  10.2 us
    pallas_call x1, Pallas kernels, per_device(): pl.pallas_call(keyed_kernel, grid_spec=pltpu.PrefetchScalarGridSpec(num_s...  8.35 us
    all_to_all x1, waiting for transfers between devices, per_device(): asked = lax.all_to_all(asks, 'tm', split_axis=0, concat_axis=0, tiled=True)  7.73 us
    unnamed x29, local copies, waits for them, and re-layouts  5.69 us
  transfers between devices with their start and end apart: 13, of which 6 were waited for; matrix products, arithmetic and copies ran while one was open for 1% of the time, Pallas kernels for 7%

profile of v6, /device:TPU:6, one launch (start us, length us, event | category | flops | bytes accessed | tf_op | source)
XLA Modules:
  0.0 129.5 jit_solution(2873945346348686308)
XLA Ops:
  0.6 0.0 copy-start.10
  0.6 0.0 copy-start.9
  0.7 0.0 copy-start.11
  0.7 0.0 copy-start.12
  0.7 0.7 copy-done.12
  1.3 1.4 %ask.1 = s32[32,128]{1,0:T(8,128)} custom-call(s32[64]{0:T(128)S(1)} %bitcast.31), custom_call_target="tpu_custom_call" | custom-call | tf_op jit(solution)/shard_map/ask/pallas_call | solution.py:216
  2.7 1.1 copy.11
  3.8 3.9 %collective-permute-start = (bf16[64,32,128]{2,1,0:T(8,128)(2,1)S(1)}, bf16[64,32,128]{2,1,0:T(8,128)(2,1)S(1)}, u32[]{:S(2)}, u32[]{:S(2)}) collective-permute-start(bf16[64,32,128]{2,1,0:T(8,128)(2,1)S(1)} %bitcast.22), channel_id=1, source_target_pairs={{0,4},{1,5},{2,6},{3,7},{4,8},{5,9},{6,10},{7,11},{8,12},{9,13},{1... | collective-permute-start | bytes 1572872 | tf_op jit(solution)/shard_map/ppermute | solution.py:37
  7.7 3.5 %collective-permute-start.6 = (bf16[64,32,128]{2,1,0:T(8,128)(2,1)S(1)}, bf16[64,32,128]{2,1,0:T(8,128)(2,1)S(1)}, u32[]{:S(2)}, u32[]{:S(2)}) collective-permute-start(bf16[64,32,128]{2,1,0:T(8,128)(2,1)S(1)} %bitcast.23), channel_id=1, source_target_pairs={{0,1},{1,2},{2,3},{4,5},{5,6},{6,7},{8,9},{9,10},{10,11},{12,13},{... | collective-permute-start | bytes 1572872 | tf_op jit(solution)/shard_map/ppermute | solution.py:37
  11.2 10.2 %all-to-all-start = ((s32[32,1,128]{2,1,0:T(1,128)}), s32[32,1,128]{2,1,0:T(1,128)S(1)}, u32[]{:S(2)}, u32[]{:S(2)}) async-start(s32[32,1,128]{2,1,0:T(1,128)} %bitcast.5), calls=%async_computation | async-start | bytes 32768 | tf_op jit(solution)/shard_map/all_to_all | solution.py:233
  21.5 0.0 collective-permute-done
  21.5 0.0 copy-start.4
  21.5 1.0 broadcast_select_fusion
  22.5 0.1 weights.1
  22.6 0.8 copy-done.6
  23.4 7.7 %all-to-all-done = s32[32,1,128]{2,1,0:T(1,128)S(1)} async-done(((s32[32,1,128]{2,1,0:T(1,128)}), s32[32,1,128]{2,1,0:T(1,128)S(1)}, u32[]{:S(2)}, u32[]{:S(2)}) %all-to-all-start) | async-done | bytes 16416 | tf_op jit(solution)/shard_map/all_to_all | solution.py:233
  31.1 0.0 collective-permute-done.6.rest_1_
  31.1 0.0 copy-start
  31.2 0.0 copy-start.13
  31.2 1.1 pick.1
  32.3 0.0 copy-start.1
  32.3 1.0 copy-done.1
  33.3 3.9 %all-to-all-start.1 = ((bf16[128,32,128]{2,1,0:T(8,128)(2,1)}), bf16[128,32,128]{2,1,0:T(8,128)(2,1)S(1)}, u32[]{:S(2)}, u32[]{:S(2)}) async-start(bf16[128,32,128]{2,1,0:T(8,128)(2,1)} %copy-done.1), calls=%async_computation.1 | async-start | bytes 2097152 | tf_op jit(solution)/shard_map/all_to_all | solution.py:254
  37.2 1.8 %collective-permute-start.3 = (bf16[64,32,128]{2,1,0:T(8,128)(2,1)}, bf16[64,32,128]{2,1,0:T(8,128)(2,1)}, u32[]{:S(2)}, u32[]{:S(2)}) collective-permute-start(bf16[64,32,128]{2,1,0:T(8,128)(2,1)} %copy-done.4), channel_id=1, source_target_pairs={{0,1},{1,2},{2,3},{3,0},{4,5},{5,6},{6,7},{7,4},{8,9},{9,10},{10,1... | collective-permute-start | bytes 1572872 | tf_op jit(solution)/shard_map/ppermute | solution.py:37
  39.0 2.7 %collective-permute-start.1 = (bf16[64,32,128]{2,1,0:T(8,128)(2,1)}, bf16[64,32,128]{2,1,0:T(8,128)(2,1)}, u32[]{:S(2)}, u32[]{:S(2)}) collective-permute-start(bf16[64,32,128]{2,1,0:T(8,128)(2,1)} %copy-done.6), channel_id=1, source_target_pairs={{0,2},{1,3},{2,0},{3,1},{4,6},{5,7},{6,4},{7,5},{8,10},{9,11},{10,... | collective-permute-start | bytes 1572872 | tf_op jit(solution)/shard_map/ppermute | solution.py:37
  41.6 1.5 %collective-permute-start.2 = (bf16[64,32,128]{2,1,0:T(8,128)(2,1)}, bf16[64,32,128]{2,1,0:T(8,128)(2,1)}, u32[]{:S(2)}, u32[]{:S(2)}) collective-permute-start(bf16[64,32,128]{2,1,0:T(8,128)(2,1)} %get-tuple-element.16), channel_id=1, source_target_pairs={{0,3},{1,0},{2,1},{3,2},{4,7},{5,4},{6,5},{7,6},{8,11},{9,8},{10,9... | collective-permute-start | bytes 1572872 | tf_op jit(solution)/shard_map/ppermute | solution.py:37
  43.1 20.5 %collective-permute-done.3.c1 = bf16[64,32,128]{2,1,0:T(8,128)(2,1)} collective-permute-done((bf16[64,32,128]{2,1,0:T(8,128)(2,1)}, bf16[64,32,128]{2,1,0:T(8,128)(2,1)}, u32[]{:S(2)}, u32[]{:S(2)}) %collective-permute-start.3) | collective-permute-done | bytes 524320 | tf_op jit(solution)/shard_map/ppermute | solution.py:37
  63.6 3.1 %collective-permute-start.4 = (bf16[64,32,128]{2,1,0:T(8,128)(2,1)}, bf16[64,32,128]{2,1,0:T(8,128)(2,1)}, u32[]{:S(2)}, u32[]{:S(2)}) collective-permute-start(bf16[64,32,128]{2,1,0:T(8,128)(2,1)} %collective-permute-done.3.c1), channel_id=1, source_target_pairs={{0,4},{4,8},{8,12},{12,16},{16,20},{20,24},{24,28},{32,36},{36,40}... | collective-permute-start | bytes 1572872 | tf_op jit(solution)/shard_map/ppermute | solution.py:37
  66.7 6.2 %collective-permute-done.1.r2 = bf16[64,32,128]{2,1,0:T(8,128)(2,1)} collective-permute-done((bf16[64,32,128]{2,1,0:T(8,128)(2,1)}, bf16[64,32,128]{2,1,0:T(8,128)(2,1)}, u32[]{:S(2)}, u32[]{:S(2)}) %collective-permute-start.1) | collective-permute-done | bytes 524320 | tf_op jit(solution)/shard_map/ppermute | solution.py:37
  72.9 4.2 %collective-permute-start.5 = (bf16[64,32,128]{2,1,0:T(8,128)(2,1)}, bf16[64,32,128]{2,1,0:T(8,128)(2,1)}, u32[]{:S(2)}, u32[]{:S(2)}) collective-permute-start(bf16[64,32,128]{2,1,0:T(8,128)(2,1)} %collective-permute-done.1.r2), channel_id=1, source_target_pairs={{0,4},{1,5},{2,6},{3,7},{4,8},{5,9},{6,10},{7,11},{8,12},{9,13},{1... | collective-permute-start | bytes 1572872 | tf_op jit(solution)/shard_map/ppermute | solution.py:37
  77.1 0.0 all-to-all-done.1.incoming
  77.1 1.0 copy-done.3
  78.2 1.0 copy-done.5
  79.2 8.4 %keyed.1 = f32[8,8,64,128]{3,2,1,0:T(8,128)S(1)} custom-call(s32[1]{0:T(128)} %bitcast.place, s32[64]{0:T(128)S(1)} %bitcast.32, bf16[8,8,64,256]{3,2,1,0:T(8,128)(2,1)S(1)} %bitcast.19, bf16[128,32,128]{2,1,0:T(8,128)(2,1)S(1)} %all-to-all-done.1.incoming, bf16[8,8,32,128]{3,2,1,0:T(8,128)(2,1)S(1)} %bitcast.26, bf16[8,8,32,128]{3,2,1,0:T(8,128)(2,1)} %bitcast.8.c1, ...), custom_call_target="tpu_custom_call" | custom-call | tf_op jit(solution)/shard_map/keyed/pallas_call | solution.py:263
  87.6 0.0 collective-permute-done.2.r3
  87.6 0.0 collective-permute-done.4.d2
  87.6 0.0 collective-permute-done.5.r6
  87.6 13.5 %final.1 = (bf16[64,64,256]{2,1,0:T(8,128)(2,1)}, bf16[256,256]{1,0:T(8,128)(2,1)S(1)}) custom-call(s32[1]{0:T(128)} %bitcast.place, bf16[64,64,256]{2,1,0:T(8,128)(2,1)S(1)} %bitcast.20, bf16[64,32,128]{2,1,0:T(8,128)(2,1)} %collective-permute-done.1.r2, bf16[64,32,128]{2,1,0:T(8,128)(2,1)} %collective-permute-done.2.r3, ...), custom_call_target="tpu_custom_call" | custom-call | tf_op jit(solution)/shard_map/final/pallas_call | solution.py:291
  101.1 18.1 %all_to_all.21 = bf16[32,8,256]{2,1,0:T(8,128)(2,1)S(1)} all-to-all(bf16[32,8,256]{2,1,0:T(8,128)(2,1)S(1)} %bitcast.29), channel_id=1, replica_groups=mesh['video'=8,'tm'=32] {'tm'}, dimensions={0} | all-to-all | bytes 262144 | tf_op jit(solution)/shard_map/all_to_all | solution.py:334
  119.2 0.1 collective-permute-start.7
  119.3 1.2 collective-permute-done.7
  120.5 0.8 collective-permute-start.10
  121.3 2.4 %collective-permute-start.9 = (f32[8,256]{1,0:T(8,128)S(1)}, f32[8,256]{1,0:T(8,128)S(1)}, u32[]{:S(2)}, u32[]{:S(2)}) collective-permute-start(f32[8,256]{1,0:T(8,128)S(1)} %fusion), channel_id=1, source_target_pairs={{0,64},{32,96},{64,128},{96,160},{128,192},{160,224},{192,0},{224,... | collective-permute-start | bytes 24584 | tf_op jit(solution)/shard_map/ppermute | solution.py:341
  123.7 0.2 collective-permute-start.8
  123.9 1.4 %collective-permute-done.10 = f32[8,256]{1,0:T(8,128)S(1)} collective-permute-done((f32[8,256]{1,0:T(8,128)S(1)}, f32[8,256]{1,0:T(8,128)S(1)}, u32[]{:S(2)}, u32[]{:S(2)}) %collective-permute-start.10) | collective-permute-done | bytes 8224 | tf_op jit(solution)/shard_map/ppermute | solution.py:341
  125.4 0.0 collective-permute-done.9
  125.4 3.5 %collective-permute-done.8 = f32[8,256]{1,0:T(8,128)S(1)} collective-permute-done((f32[8,256]{1,0:T(8,128)S(1)}, f32[8,256]{1,0:T(8,128)S(1)}, u32[]{:S(2)}, u32[]{:S(2)}) %collective-permute-start.8) | collective-permute-done | bytes 8224 | tf_op jit(solution)/shard_map/ppermute | solution.py:341
  128.9 0.6 add_add_fusion
  (18 shorter events, 0.1 us)
Async XLA Ops:
  0.6 21.9 %copy-start.10 = (bf16[64,256]{1,0:T(8,128)(2,1)S(1)}, bf16[64,256]{1,0:T(8,128)(2,1)}, u32[]{:S(2)}) copy-start(bf16[64,256]{1,0:T(8,128)(2,1)} %w_v.1) | copy-start | bytes 98308
  0.6 21.9 %copy-start.9 = (bf16[64,256]{1,0:T(8,128)(2,1)S(1)}, bf16[64,256]{1,0:T(8,128)(2,1)}, u32[]{:S(2)}) copy-start(bf16[64,256]{1,0:T(8,128)(2,1)} %w_k.1) | copy-start | bytes 98308
  0.7 21.9 %copy-start.11 = (f32[7,64]{1,0:T(8,128)S(1)}, f32[7,64]{1,0:T(8,128)}, u32[]{:S(2)}) copy-start(f32[7,64]{1,0:T(8,128)} %tpos.1) | copy-start | bytes 5380
  0.7 0.7 copy-start.12
  3.8 17.7 %collective-permute-start = (bf16[64,32,128]{2,1,0:T(8,128)(2,1)S(1)}, bf16[64,32,128]{2,1,0:T(8,128)(2,1)S(1)}, u32[]{:S(2)}, u32[]{:S(2)}) collective-permute-start(bf16[64,32,128]{2,1,0:T(8,128)(2,1)S(1)} %bitcast.22), channel_id=1, source_target_pairs={{0,4},{1,5},{2,6},{3,7},{4,8},{5,9},{6,10},{7,11},{8,12},{9,13},{1... | collective-permute-start | bytes 1572872 | tf_op jit(solution)/shard_map/ppermute | solution.py:37
  7.7 23.4 %collective-permute-start.6 = (bf16[64,32,128]{2,1,0:T(8,128)(2,1)S(1)}, bf16[64,32,128]{2,1,0:T(8,128)(2,1)S(1)}, u32[]{:S(2)}, u32[]{:S(2)}) collective-permute-start(bf16[64,32,128]{2,1,0:T(8,128)(2,1)S(1)} %bitcast.23), channel_id=1, source_target_pairs={{0,1},{1,2},{2,3},{4,5},{5,6},{6,7},{8,9},{9,10},{10,11},{12,13},{... | collective-permute-start | bytes 1572872 | tf_op jit(solution)/shard_map/ppermute | solution.py:37
  11.2 19.9 %all-to-all-start = ((s32[32,1,128]{2,1,0:T(1,128)}), s32[32,1,128]{2,1,0:T(1,128)S(1)}, u32[]{:S(2)}, u32[]{:S(2)}) async-start(s32[32,1,128]{2,1,0:T(1,128)} %bitcast.5), calls=%async_computation | async-start | bytes 32768 | tf_op jit(solution)/shard_map/all_to_all | solution.py:233
  21.5 9.6 %copy-start.4 = (bf16[64,32,128]{2,1,0:T(8,128)(2,1)}, bf16[64,32,128]{2,1,0:T(8,128)(2,1)S(1)}, u32[]{:S(2)}) copy-start(bf16[64,32,128]{2,1,0:T(8,128)(2,1)S(1)} %collective-permute-done) | copy-start | bytes 1572868
  22.6 0.8 copy-start.6
  31.1 2.1 %copy-start.2 = (bf16[64,32,128]{2,1,0:T(8,128)(2,1)}, bf16[64,32,128]{2,1,0:T(8,128)(2,1)S(1)}, u32[]{:S(2)}) copy-start(bf16[64,32,128]{2,1,0:T(8,128)(2,1)S(1)} %collective-permute-done.6.rest_1_) | copy-start | bytes 1572868
  31.1 46.0 %copy-start = (bf16[1,1,4096,256]{3,2,1,0:T(8,128)(2,1)S(1)}, bf16[1,1,4096,256]{3,2,1,0:T(8,128)(2,1)}, u32[]{:S(2)}) copy-start(bf16[1,1,4096,256]{3,2,1,0:T(8,128)(2,1)} %param.8) | copy-start | bytes 6291460
  31.2 46.0 %copy-start.13 = (s32[1,1,64]{2,1,0:T(1,128)S(1)}, s32[1,1,64]{2,1,0:T(1,128)}, u32[]{:S(2)}) copy-start(s32[1,1,64]{2,1,0:T(1,128)} %param.14) | copy-start | bytes 772
  32.3 1.0 copy-start.1
  33.3 43.9 %all-to-all-start.1 = ((bf16[128,32,128]{2,1,0:T(8,128)(2,1)}), bf16[128,32,128]{2,1,0:T(8,128)(2,1)S(1)}, u32[]{:S(2)}, u32[]{:S(2)}) async-start(bf16[128,32,128]{2,1,0:T(8,128)(2,1)} %copy-done.1), calls=%async_computation.1 | async-start | bytes 2097152 | tf_op jit(solution)/shard_map/all_to_all | solution.py:254
  37.2 26.4 %collective-permute-start.3 = (bf16[64,32,128]{2,1,0:T(8,128)(2,1)}, bf16[64,32,128]{2,1,0:T(8,128)(2,1)}, u32[]{:S(2)}, u32[]{:S(2)}) collective-permute-start(bf16[64,32,128]{2,1,0:T(8,128)(2,1)} %copy-done.4), channel_id=1, source_target_pairs={{0,1},{1,2},{2,3},{3,0},{4,5},{5,6},{6,7},{7,4},{8,9},{9,10},{10,1... | collective-permute-start | bytes 1572872 | tf_op jit(solution)/shard_map/ppermute | solution.py:37
  39.0 34.0 %collective-permute-start.1 = (bf16[64,32,128]{2,1,0:T(8,128)(2,1)}, bf16[64,32,128]{2,1,0:T(8,128)(2,1)}, u32[]{:S(2)}, u32[]{:S(2)}) collective-permute-start(bf16[64,32,128]{2,1,0:T(8,128)(2,1)} %copy-done.6), channel_id=1, source_target_pairs={{0,2},{1,3},{2,0},{3,1},{4,6},{5,7},{6,4},{7,5},{8,10},{9,11},{10,... | collective-permute-start | bytes 1572872 | tf_op jit(solution)/shard_map/ppermute | solution.py:37
  41.6 45.9 %collective-permute-start.2 = (bf16[64,32,128]{2,1,0:T(8,128)(2,1)}, bf16[64,32,128]{2,1,0:T(8,128)(2,1)}, u32[]{:S(2)}, u32[]{:S(2)}) collective-permute-start(bf16[64,32,128]{2,1,0:T(8,128)(2,1)} %get-tuple-element.16), channel_id=1, source_target_pairs={{0,3},{1,0},{2,1},{3,2},{4,7},{5,4},{6,5},{7,6},{8,11},{9,8},{10,9... | collective-permute-start | bytes 1572872 | tf_op jit(solution)/shard_map/ppermute | solution.py:37
  63.6 24.0 %collective-permute-start.4 = (bf16[64,32,128]{2,1,0:T(8,128)(2,1)}, bf16[64,32,128]{2,1,0:T(8,128)(2,1)}, u32[]{:S(2)}, u32[]{:S(2)}) collective-permute-start(bf16[64,32,128]{2,1,0:T(8,128)(2,1)} %collective-permute-done.3.c1), channel_id=1, source_target_pairs={{0,4},{4,8},{8,12},{12,16},{16,20},{20,24},{24,28},{32,36},{36,40}... | collective-permute-start | bytes 1572872 | tf_op jit(solution)/shard_map/ppermute | solution.py:37
  72.9 14.7 %collective-permute-start.5 = (bf16[64,32,128]{2,1,0:T(8,128)(2,1)}, bf16[64,32,128]{2,1,0:T(8,128)(2,1)}, u32[]{:S(2)}, u32[]{:S(2)}) collective-permute-start(bf16[64,32,128]{2,1,0:T(8,128)(2,1)} %collective-permute-done.1.r2), channel_id=1, source_target_pairs={{0,4},{1,5},{2,6},{3,7},{4,8},{5,9},{6,10},{7,11},{8,12},{9,13},{1... | collective-permute-start | bytes 1572872 | tf_op jit(solution)/shard_map/ppermute | solution.py:37
  77.1 1.0 copy-start.3
  78.2 1.0 copy-start.5
  79.2 8.4 %copy-start.7 = (bf16[1,1,4096,256]{3,2,1,0:T(8,128)(2,1)S(1)}, bf16[1,1,4096,256]{3,2,1,0:T(8,128)(2,1)}, u32[]{:S(2)}) copy-start(bf16[1,1,4096,256]{3,2,1,0:T(8,128)(2,1)} %param.15) | copy-start | bytes 6291460
  79.2 8.4 %copy-start.8 = (bf16[256,256]{1,0:T(8,128)(2,1)S(1)}, bf16[256,256]{1,0:T(8,128)(2,1)}, u32[]{:S(2)}) copy-start(bf16[256,256]{1,0:T(8,128)(2,1)} %w_o.1) | copy-start | bytes 393220
  119.2 1.3 collective-permute-start.7
  120.5 4.9 %collective-permute-start.10 = (f32[8,256]{1,0:T(8,128)S(1)}, f32[8,256]{1,0:T(8,128)S(1)}, u32[]{:S(2)}, u32[]{:S(2)}) collective-permute-start(f32[8,256]{1,0:T(8,128)S(1)} %fusion), channel_id=1, source_target_pairs={{0,192},{32,224},{64,0},{96,32},{128,64},{160,96},{192,128},{224,1... | collective-permute-start | bytes 24584 | tf_op jit(solution)/shard_map/ppermute | solution.py:341
  121.3 4.0 %collective-permute-start.9 = (f32[8,256]{1,0:T(8,128)S(1)}, f32[8,256]{1,0:T(8,128)S(1)}, u32[]{:S(2)}, u32[]{:S(2)}) collective-permute-start(f32[8,256]{1,0:T(8,128)S(1)} %fusion), channel_id=1, source_target_pairs={{0,64},{32,96},{64,128},{96,160},{128,192},{160,224},{192,0},{224,... | collective-permute-start | bytes 24584 | tf_op jit(solution)/shard_map/ppermute | solution.py:341
  123.7 5.2 %collective-permute-start.8 = (f32[8,256]{1,0:T(8,128)S(1)}, f32[8,256]{1,0:T(8,128)S(1)}, u32[]{:S(2)}, u32[]{:S(2)}) collective-permute-start(f32[8,256]{1,0:T(8,128)S(1)} %fusion), channel_id=1, source_target_pairs={{0,128},{32,160},{64,192},{96,224},{128,0},{160,32},{192,64},{224,... | collective-permute-start | bytes 24584 | tf_op jit(solution)/shard_map/ppermute | solution.py:341

commit v7 on v6

--- a/solution.py
+++ b/solution.py
@@ -218,7 +218,6 @@
         out_shape=jax.ShapeDtypeStruct((devices, LANES), jnp.int32),
         in_specs=[in_smem],
         out_specs=in_vmem,
-        compiler_params=pltpu.CompilerParams(vmem_limit_bytes=8 * MIB),
         name="ask",
     )(listed)
     own, asks = lax.optimization_barrier((own, asks))

time: 130 us -> 130 us (level)
    unnamed x29 -> x27, local copies, waits for them, and re-layouts: 5.69 us -> 5.03 us
where the time goes in v7:
time: 130 us; the launch traced here: 129 us
  waiting for transfers between devices  40.5 us (31%)
  starting transfers between devices  38.3 us (29%)
  Pallas kernels  24.6 us (19%)
  blocking collectives  18.1 us (14%)
  local copies, waits for them, and re-layouts  5.03 us (4%)
  other arithmetic  1.66 us (1%)
    ppermute x7, waiting for transfers between devices, routed(): return lax.ppermute(shard, 'tm', pairs)  26.7 us
    ppermute x7, starting transfers between devices, routed(): return lax.ppermute(shard, 'tm', pairs)  20.6 us
    all_to_all x1, blocking collectives, per_device(): lax.all_to_all(grad.reshape(devices, D // devices, D), 'tm', split_axis=0...  18.1 us
    pallas_call x1, Pallas kernels, per_device(): pl.pallas_call(final_kernel, grid_spec=pltpu.PrefetchScalarGridSpec(num_s...  13.5 us
    all_to_all x1, starting transfers between devices, per_device(): asked = lax.all_to_all(asks, 'tm', split_axis=0, concat_axis=0, tiled=True)  10.2 us
    pallas_call x1, Pallas kernels, per_device(): pl.pallas_call(keyed_kernel, grid_spec=pltpu.PrefetchScalarGridSpec(num_s...  8.34 us
    all_to_all x1, waiting for transfers between devices, per_device(): asked = lax.all_to_all(asks, 'tm', split_axis=0, concat_axis=0, tiled=True)  7.72 us
    unnamed x27, local copies, waits for them, and re-layouts  5.03 us
  transfers between devices with their start and end apart: 13, of which 6 were waited for; matrix products, arithmetic and copies ran while one was open for 1% of the time, Pallas kernels for 7%

profile of v7, /device:TPU:6, one launch (start us, length us, event | category | flops | bytes accessed | tf_op | source)
XLA Modules:
  0.0 129.1 jit_solution(3422746600292147540)
XLA Ops:
  0.6 0.0 copy-start.10
  0.6 0.0 copy-start.9
  0.7 0.0 copy-start.11
  0.7 1.6 %ask.1 = s32[32,128]{1,0:T(8,128)} custom-call(s32[64]{0:T(128)} %bitcast.31), custom_call_target="tpu_custom_call" | custom-call | tf_op jit(solution)/shard_map/ask/pallas_call | solution.py:216
  2.3 1.1 copy.11
  3.4 3.9 %collective-permute-start = (bf16[64,32,128]{2,1,0:T(8,128)(2,1)S(1)}, bf16[64,32,128]{2,1,0:T(8,128)(2,1)S(1)}, u32[]{:S(2)}, u32[]{:S(2)}) collective-permute-start(bf16[64,32,128]{2,1,0:T(8,128)(2,1)S(1)} %bitcast.22), channel_id=1, source_target_pairs={{0,4},{1,5},{2,6},{3,7},{4,8},{5,9},{6,10},{7,11},{8,12},{9,13},{1... | collective-permute-start | bytes 1572872 | tf_op jit(solution)/shard_map/ppermute | solution.py:37
  7.3 3.5 %collective-permute-start.6 = (bf16[64,32,128]{2,1,0:T(8,128)(2,1)S(1)}, bf16[64,32,128]{2,1,0:T(8,128)(2,1)S(1)}, u32[]{:S(2)}, u32[]{:S(2)}) collective-permute-start(bf16[64,32,128]{2,1,0:T(8,128)(2,1)S(1)} %bitcast.23), channel_id=1, source_target_pairs={{0,1},{1,2},{2,3},{4,5},{5,6},{6,7},{8,9},{9,10},{10,11},{12,13},{... | collective-permute-start | bytes 1572872 | tf_op jit(solution)/shard_map/ppermute | solution.py:37
  10.8 10.2 %all-to-all-start = ((s32[32,1,128]{2,1,0:T(1,128)}), s32[32,1,128]{2,1,0:T(1,128)S(1)}, u32[]{:S(2)}, u32[]{:S(2)}) async-start(s32[32,1,128]{2,1,0:T(1,128)} %bitcast.34), calls=%async_computation | async-start | bytes 32768 | tf_op jit(solution)/shard_map/all_to_all | solution.py:232
  21.1 0.0 collective-permute-done
  21.1 1.0 broadcast_select_fusion
  22.1 0.0 copy-done.9
  22.1 0.1 weights.1
  22.2 0.8 copy-done.6
  23.0 7.7 %all-to-all-done = s32[32,1,128]{2,1,0:T(1,128)S(1)} async-done(((s32[32,1,128]{2,1,0:T(1,128)}), s32[32,1,128]{2,1,0:T(1,128)S(1)}, u32[]{:S(2)}, u32[]{:S(2)}) %all-to-all-start) | async-done | bytes 16416 | tf_op jit(solution)/shard_map/all_to_all | solution.py:232
  30.7 0.0 collective-permute-done.6.rest_1_
  30.7 0.0 copy-start
  30.7 0.0 copy-start.12
  30.8 1.1 pick.1
  31.9 0.0 copy-start.1
  31.9 1.0 copy-done.1
  32.8 0.0 copy-done.2
  32.8 3.9 %all-to-all-start.1 = ((bf16[128,32,128]{2,1,0:T(8,128)(2,1)}), bf16[128,32,128]{2,1,0:T(8,128)(2,1)S(1)}, u32[]{:S(2)}, u32[]{:S(2)}) async-start(bf16[128,32,128]{2,1,0:T(8,128)(2,1)} %copy-done.1), calls=%async_computation.1 | async-start | bytes 2097152 | tf_op jit(solution)/shard_map/all_to_all | solution.py:253
  36.8 1.8 %collective-permute-start.3 = (bf16[64,32,128]{2,1,0:T(8,128)(2,1)}, bf16[64,32,128]{2,1,0:T(8,128)(2,1)}, u32[]{:S(2)}, u32[]{:S(2)}) collective-permute-start(bf16[64,32,128]{2,1,0:T(8,128)(2,1)} %copy-done.4), channel_id=1, source_target_pairs={{0,1},{1,2},{2,3},{3,0},{4,5},{5,6},{6,7},{7,4},{8,9},{9,10},{10,1... | collective-permute-start | bytes 1572872 | tf_op jit(solution)/shard_map/ppermute | solution.py:37
  38.5 2.7 %collective-permute-start.1 = (bf16[64,32,128]{2,1,0:T(8,128)(2,1)}, bf16[64,32,128]{2,1,0:T(8,128)(2,1)}, u32[]{:S(2)}, u32[]{:S(2)}) collective-permute-start(bf16[64,32,128]{2,1,0:T(8,128)(2,1)} %copy-done.6), channel_id=1, source_target_pairs={{0,2},{1,3},{2,0},{3,1},{4,6},{5,7},{6,4},{7,5},{8,10},{9,11},{10,... | collective-permute-start | bytes 1572872 | tf_op jit(solution)/shard_map/ppermute | solution.py:37
  41.2 1.5 %collective-permute-start.2 = (bf16[64,32,128]{2,1,0:T(8,128)(2,1)}, bf16[64,32,128]{2,1,0:T(8,128)(2,1)}, u32[]{:S(2)}, u32[]{:S(2)}) collective-permute-start(bf16[64,32,128]{2,1,0:T(8,128)(2,1)} %get-tuple-element.16), channel_id=1, source_target_pairs={{0,3},{1,0},{2,1},{3,2},{4,7},{5,4},{6,5},{7,6},{8,11},{9,8},{10,9... | collective-permute-start | bytes 1572872 | tf_op jit(solution)/shard_map/ppermute | solution.py:37
  42.7 20.5 %collective-permute-done.3.c1 = bf16[64,32,128]{2,1,0:T(8,128)(2,1)} collective-permute-done((bf16[64,32,128]{2,1,0:T(8,128)(2,1)}, bf16[64,32,128]{2,1,0:T(8,128)(2,1)}, u32[]{:S(2)}, u32[]{:S(2)}) %collective-permute-start.3) | collective-permute-done | bytes 524320 | tf_op jit(solution)/shard_map/ppermute | solution.py:37
  63.2 3.1 %collective-permute-start.4 = (bf16[64,32,128]{2,1,0:T(8,128)(2,1)}, bf16[64,32,128]{2,1,0:T(8,128)(2,1)}, u32[]{:S(2)}, u32[]{:S(2)}) collective-permute-start(bf16[64,32,128]{2,1,0:T(8,128)(2,1)} %collective-permute-done.3.c1), channel_id=1, source_target_pairs={{0,4},{4,8},{8,12},{12,16},{16,20},{20,24},{24,28},{32,36},{36,40}... | collective-permute-start | bytes 1572872 | tf_op jit(solution)/shard_map/ppermute | solution.py:37
  66.3 6.2 %collective-permute-done.1.r2 = bf16[64,32,128]{2,1,0:T(8,128)(2,1)} collective-permute-done((bf16[64,32,128]{2,1,0:T(8,128)(2,1)}, bf16[64,32,128]{2,1,0:T(8,128)(2,1)}, u32[]{:S(2)}, u32[]{:S(2)}) %collective-permute-start.1) | collective-permute-done | bytes 524320 | tf_op jit(solution)/shard_map/ppermute | solution.py:37
  72.5 4.2 %collective-permute-start.5 = (bf16[64,32,128]{2,1,0:T(8,128)(2,1)}, bf16[64,32,128]{2,1,0:T(8,128)(2,1)}, u32[]{:S(2)}, u32[]{:S(2)}) collective-permute-start(bf16[64,32,128]{2,1,0:T(8,128)(2,1)} %collective-permute-done.1.r2), channel_id=1, source_target_pairs={{0,4},{1,5},{2,6},{3,7},{4,8},{5,9},{6,10},{7,11},{8,12},{9,13},{1... | collective-permute-start | bytes 1572872 | tf_op jit(solution)/shard_map/ppermute | solution.py:37
  76.7 0.0 all-to-all-done.1.incoming
  76.7 0.0 copy-done.12
  76.7 1.0 copy-done.3
  77.8 1.0 copy-done.5
  78.8 8.3 %keyed.1 = f32[8,8,64,128]{3,2,1,0:T(8,128)S(1)} custom-call(s32[1]{0:T(128)} %bitcast.place, s32[64]{0:T(128)S(1)} %bitcast.32, bf16[8,8,64,256]{3,2,1,0:T(8,128)(2,1)S(1)} %bitcast.19, bf16[128,32,128]{2,1,0:T(8,128)(2,1)S(1)} %all-to-all-done.1.incoming, bf16[8,8,32,128]{3,2,1,0:T(8,128)(2,1)S(1)} %bitcast.26, bf16[8,8,32,128]{3,2,1,0:T(8,128)(2,1)} %bitcast.8.c1, ...), custom_call_target="tpu_custom_call" | custom-call | tf_op jit(solution)/shard_map/keyed/pallas_call | solution.py:262
  87.2 0.0 collective-permute-done.2.r3
  87.2 0.0 collective-permute-done.4.d2
  87.2 0.0 collective-permute-done.5.r6
  87.2 13.5 %final.1 = (bf16[64,64,256]{2,1,0:T(8,128)(2,1)}, bf16[256,256]{1,0:T(8,128)(2,1)S(1)}) custom-call(s32[1]{0:T(128)} %bitcast.place, bf16[64,64,256]{2,1,0:T(8,128)(2,1)S(1)} %bitcast.20, bf16[64,32,128]{2,1,0:T(8,128)(2,1)} %collective-permute-done.1.r2, bf16[64,32,128]{2,1,0:T(8,128)(2,1)} %collective-permute-done.2.r3, ...), custom_call_target="tpu_custom_call" | custom-call | tf_op jit(solution)/shard_map/final/pallas_call | solution.py:290
  100.7 18.1 %all_to_all.21 = bf16[32,8,256]{2,1,0:T(8,128)(2,1)S(1)} all-to-all(bf16[32,8,256]{2,1,0:T(8,128)(2,1)S(1)} %bitcast.29), channel_id=1, replica_groups=mesh['video'=8,'tm'=32] {'tm'}, dimensions={0} | all-to-all | bytes 262144 | tf_op jit(solution)/shard_map/all_to_all | solution.py:333
  118.8 0.1 collective-permute-start.7
  118.9 1.2 collective-permute-done.7
  120.1 0.8 collective-permute-start.10
  120.9 2.4 %collective-permute-start.9 = (f32[8,256]{1,0:T(8,128)S(1)}, f32[8,256]{1,0:T(8,128)S(1)}, u32[]{:S(2)}, u32[]{:S(2)}) collective-permute-start(f32[8,256]{1,0:T(8,128)S(1)} %fusion), channel_id=1, source_target_pairs={{0,64},{32,96},{64,128},{96,160},{128,192},{160,224},{192,0},{224,... | collective-permute-start | bytes 24584 | tf_op jit(solution)/shard_map/ppermute | solution.py:340
  123.3 0.2 collective-permute-start.8
  123.5 1.4 %collective-permute-done.10 = f32[8,256]{1,0:T(8,128)S(1)} collective-permute-done((f32[8,256]{1,0:T(8,128)S(1)}, f32[8,256]{1,0:T(8,128)S(1)}, u32[]{:S(2)}, u32[]{:S(2)}) %collective-permute-start.10) | collective-permute-done | bytes 8224 | tf_op jit(solution)/shard_map/ppermute | solution.py:340
  125.0 0.0 collective-permute-done.9
  125.0 3.5 %collective-permute-done.8 = f32[8,256]{1,0:T(8,128)S(1)} collective-permute-done((f32[8,256]{1,0:T(8,128)S(1)}, f32[8,256]{1,0:T(8,128)S(1)}, u32[]{:S(2)}, u32[]{:S(2)}) %collective-permute-start.8) | collective-permute-done | bytes 8224 | tf_op jit(solution)/shard_map/ppermute | solution.py:340
  128.5 0.6 add_add_fusion
  (16 shorter events, 0.1 us)
Async XLA Ops:
  0.6 21.5 %copy-start.10 = (bf16[64,256]{1,0:T(8,128)(2,1)S(1)}, bf16[64,256]{1,0:T(8,128)(2,1)}, u32[]{:S(2)}) copy-start(bf16[64,256]{1,0:T(8,128)(2,1)} %w_v.1) | copy-start | bytes 98308
  0.6 21.5 %copy-start.9 = (bf16[64,256]{1,0:T(8,128)(2,1)S(1)}, bf16[64,256]{1,0:T(8,128)(2,1)}, u32[]{:S(2)}) copy-start(bf16[64,256]{1,0:T(8,128)(2,1)} %w_k.1) | copy-start | bytes 98308
  0.7 21.5 %copy-start.11 = (f32[7,64]{1,0:T(8,128)S(1)}, f32[7,64]{1,0:T(8,128)}, u32[]{:S(2)}) copy-start(f32[7,64]{1,0:T(8,128)} %tpos.1) | copy-start | bytes 5380
  3.4 17.7 %collective-permute-start = (bf16[64,32,128]{2,1,0:T(8,128)(2,1)S(1)}, bf16[64,32,128]{2,1,0:T(8,128)(2,1)S(1)}, u32[]{:S(2)}, u32[]{:S(2)}) collective-permute-start(bf16[64,32,128]{2,1,0:T(8,128)(2,1)S(1)} %bitcast.22), channel_id=1, source_target_pairs={{0,4},{1,5},{2,6},{3,7},{4,8},{5,9},{6,10},{7,11},{8,12},{9,13},{1... | collective-permute-start | bytes 1572872 | tf_op jit(solution)/shard_map/ppermute | solution.py:37
  7.3 23.4 %collective-permute-start.6 = (bf16[64,32,128]{2,1,0:T(8,128)(2,1)S(1)}, bf16[64,32,128]{2,1,0:T(8,128)(2,1)S(1)}, u32[]{:S(2)}, u32[]{:S(2)}) collective-permute-start(bf16[64,32,128]{2,1,0:T(8,128)(2,1)S(1)} %bitcast.23), channel_id=1, source_target_pairs={{0,1},{1,2},{2,3},{4,5},{5,6},{6,7},{8,9},{9,10},{10,11},{12,13},{... | collective-permute-start | bytes 1572872 | tf_op jit(solution)/shard_map/ppermute | solution.py:37
  10.8 19.9 %all-to-all-start = ((s32[32,1,128]{2,1,0:T(1,128)}), s32[32,1,128]{2,1,0:T(1,128)S(1)}, u32[]{:S(2)}, u32[]{:S(2)}) async-start(s32[32,1,128]{2,1,0:T(1,128)} %bitcast.34), calls=%async_computation | async-start | bytes 32768 | tf_op jit(solution)/shard_map/all_to_all | solution.py:232
  21.1 9.6 %copy-start.4 = (bf16[64,32,128]{2,1,0:T(8,128)(2,1)}, bf16[64,32,128]{2,1,0:T(8,128)(2,1)S(1)}, u32[]{:S(2)}) copy-start(bf16[64,32,128]{2,1,0:T(8,128)(2,1)S(1)} %collective-permute-done) | copy-start | bytes 1572868
  22.2 0.8 copy-start.6
  30.7 2.1 %copy-start.2 = (bf16[64,32,128]{2,1,0:T(8,128)(2,1)}, bf16[64,32,128]{2,1,0:T(8,128)(2,1)S(1)}, u32[]{:S(2)}) copy-start(bf16[64,32,128]{2,1,0:T(8,128)(2,1)S(1)} %collective-permute-done.6.rest_1_) | copy-start | bytes 1572868
  30.7 46.0 %copy-start = (bf16[1,1,4096,256]{3,2,1,0:T(8,128)(2,1)S(1)}, bf16[1,1,4096,256]{3,2,1,0:T(8,128)(2,1)}, u32[]{:S(2)}) copy-start(bf16[1,1,4096,256]{3,2,1,0:T(8,128)(2,1)} %param.8) | copy-start | bytes 6291460
  30.7 46.0 %copy-start.12 = (s32[1,1,64]{2,1,0:T(1,128)S(1)}, s32[1,1,64]{2,1,0:T(1,128)}, u32[]{:S(2)}) copy-start(s32[1,1,64]{2,1,0:T(1,128)} %param.14) | copy-start | bytes 772
  31.9 1.0 copy-start.1
  32.8 43.9 %all-to-all-start.1 = ((bf16[128,32,128]{2,1,0:T(8,128)(2,1)}), bf16[128,32,128]{2,1,0:T(8,128)(2,1)S(1)}, u32[]{:S(2)}, u32[]{:S(2)}) async-start(bf16[128,32,128]{2,1,0:T(8,128)(2,1)} %copy-done.1), calls=%async_computation.1 | async-start | bytes 2097152 | tf_op jit(solution)/shard_map/all_to_all | solution.py:253
  36.8 26.4 %collective-permute-start.3 = (bf16[64,32,128]{2,1,0:T(8,128)(2,1)}, bf16[64,32,128]{2,1,0:T(8,128)(2,1)}, u32[]{:S(2)}, u32[]{:S(2)}) collective-permute-start(bf16[64,32,128]{2,1,0:T(8,128)(2,1)} %copy-done.4), channel_id=1, source_target_pairs={{0,1},{1,2},{2,3},{3,0},{4,5},{5,6},{6,7},{7,4},{8,9},{9,10},{10,1... | collective-permute-start | bytes 1572872 | tf_op jit(solution)/shard_map/ppermute | solution.py:37
  38.5 34.0 %collective-permute-start.1 = (bf16[64,32,128]{2,1,0:T(8,128)(2,1)}, bf16[64,32,128]{2,1,0:T(8,128)(2,1)}, u32[]{:S(2)}, u32[]{:S(2)}) collective-permute-start(bf16[64,32,128]{2,1,0:T(8,128)(2,1)} %copy-done.6), channel_id=1, source_target_pairs={{0,2},{1,3},{2,0},{3,1},{4,6},{5,7},{6,4},{7,5},{8,10},{9,11},{10,... | collective-permute-start | bytes 1572872 | tf_op jit(solution)/shard_map/ppermute | solution.py:37
  41.2 45.9 %collective-permute-start.2 = (bf16[64,32,128]{2,1,0:T(8,128)(2,1)}, bf16[64,32,128]{2,1,0:T(8,128)(2,1)}, u32[]{:S(2)}, u32[]{:S(2)}) collective-permute-start(bf16[64,32,128]{2,1,0:T(8,128)(2,1)} %get-tuple-element.16), channel_id=1, source_target_pairs={{0,3},{1,0},{2,1},{3,2},{4,7},{5,4},{6,5},{7,6},{8,11},{9,8},{10,9... | collective-permute-start | bytes 1572872 | tf_op jit(solution)/shard_map/ppermute | solution.py:37
  63.2 24.0 %collective-permute-start.4 = (bf16[64,32,128]{2,1,0:T(8,128)(2,1)}, bf16[64,32,128]{2,1,0:T(8,128)(2,1)}, u32[]{:S(2)}, u32[]{:S(2)}) collective-permute-start(bf16[64,32,128]{2,1,0:T(8,128)(2,1)} %collective-permute-done.3.c1), channel_id=1, source_target_pairs={{0,4},{4,8},{8,12},{12,16},{16,20},{20,24},{24,28},{32,36},{36,40}... | collective-permute-start | bytes 1572872 | tf_op jit(solution)/shard_map/ppermute | solution.py:37
  72.5 14.7 %collective-permute-start.5 = (bf16[64,32,128]{2,1,0:T(8,128)(2,1)}, bf16[64,32,128]{2,1,0:T(8,128)(2,1)}, u32[]{:S(2)}, u32[]{:S(2)}) collective-permute-start(bf16[64,32,128]{2,1,0:T(8,128)(2,1)} %collective-permute-done.1.r2), channel_id=1, source_target_pairs={{0,4},{1,5},{2,6},{3,7},{4,8},{5,9},{6,10},{7,11},{8,12},{9,13},{1... | collective-permute-start | bytes 1572872 | tf_op jit(solution)/shard_map/ppermute | solution.py:37
  76.7 1.0 copy-start.3
  77.8 1.0 copy-start.5
  78.8 8.4 %copy-start.7 = (bf16[1,1,4096,256]{3,2,1,0:T(8,128)(2,1)S(1)}, bf16[1,1,4096,256]{3,2,1,0:T(8,128)(2,1)}, u32[]{:S(2)}) copy-start(bf16[1,1,4096,256]{3,2,1,0:T(8,128)(2,1)} %param.15) | copy-start | bytes 6291460
  78.8 8.4 %copy-start.8 = (bf16[256,256]{1,0:T(8,128)(2,1)S(1)}, bf16[256,256]{1,0:T(8,128)(2,1)}, u32[]{:S(2)}) copy-start(bf16[256,256]{1,0:T(8,128)(2,1)} %w_o.1) | copy-start | bytes 393220
  118.8 1.3 collective-permute-start.7
  120.1 4.9 %collective-permute-start.10 = (f32[8,256]{1,0:T(8,128)S(1)}, f32[8,256]{1,0:T(8,128)S(1)}, u32[]{:S(2)}, u32[]{:S(2)}) collective-permute-start(f32[8,256]{1,0:T(8,128)S(1)} %fusion), channel_id=1, source_target_pairs={{0,192},{32,224},{64,0},{96,32},{128,64},{160,96},{192,128},{224,1... | collective-permute-start | bytes 24584 | tf_op jit(solution)/shard_map/ppermute | solution.py:340
  120.9 4.0 %collective-permute-start.9 = (f32[8,256]{1,0:T(8,128)S(1)}, f32[8,256]{1,0:T(8,128)S(1)}, u32[]{:S(2)}, u32[]{:S(2)}) collective-permute-start(f32[8,256]{1,0:T(8,128)S(1)} %fusion), channel_id=1, source_target_pairs={{0,64},{32,96},{64,128},{96,160},{128,192},{160,224},{192,0},{224,... | collective-permute-start | bytes 24584 | tf_op jit(solution)/shard_map/ppermute | solution.py:340
  123.3 5.2 %collective-permute-start.8 = (f32[8,256]{1,0:T(8,128)S(1)}, f32[8,256]{1,0:T(8,128)S(1)}, u32[]{:S(2)}, u32[]{:S(2)}) collective-permute-start(f32[8,256]{1,0:T(8,128)S(1)} %fusion), channel_id=1, source_target_pairs={{0,128},{32,160},{64,192},{96,224},{128,0},{160,32},{192,64},{224,... | collective-permute-start | bytes 24584 | tf_op jit(solution)/shard_map/ppermute | solution.py:340
